TPU v7x, 256 devices: a whole 4x4x8 slice. The times are simulated.
256 devices in a mesh: dom: 32 (over y_lo, z, core), rep: 8 (over y_hi, x).
Axes of the slice: x: 4, y: 4 (y_hi: 2, y_lo: 2; y = y_hi * 2 + y_lo), z: 8, core: 2. Of those that a mesh axis runs over, the one named last changes fastest.
Arguments:
- features: bfloat16 [32768, 128], P('dom'), may hold values from -6 to 6
- tile_values: bfloat16 [32, 8, 32, 128, 128], P('dom', 'rep'), may hold values from 0 to 0.026977539
- tile_rows: int32 [32, 8, 32], P('dom', 'rep'), may hold values from 0 to 7, as said below
- tile_cols: int32 [32, 8, 32], P('dom', 'rep'), may hold values from 0 to 255, as said below
- tile_count: int32 [32, 8], P('dom', 'rep'), may hold values from 4 to 32, as said below
- weight: bfloat16 [128, 128], replicated, may hold values from -0.5 to 0.5
- bias: float32 [128], replicated, may hold values from -3 to 3
- cotangent: bfloat16 [32768, 128], P('dom'), may hold values from -6 to 6
Outputs:
- activations: bfloat16 [32768, 128], P('dom')
- feature_grad: float32 [32768, 128], P('dom')
- weight_grad: float32 [128, 128], replicated
- bias_grad: float32 [128], replicated
Inputs may be any that keep to these rules, and one draw needn't show every extreme that they name: `tile_rows`: row tile of a slot within its node block; every slot, live or not, holds an index in range. `tile_cols`: column tile of a slot; the slots of all devices of one node block name distinct (row tile, column tile) positions. The first tile_count slots of a device are live, the rest are ignored; some device has all 32 slots live.
All inputs are finite; a program needn't handle non-finite values.
Results may differ from a plain program's by a relative error of at most 0.007.
Values may be sent and summed in bfloat16 or wider, within the bound.
No kernel may reach another device: no remote copies, remote signals or barrier semaphores. Data moves between devices by JAX's collectives and lax.ppermute only.
A program may use at most 64 MiB of HBM per device.

v0:
```python
import jax
import jax.numpy as jnp
from jax import lax
from jax.sharding import PartitionSpec as P


def gelu_tanh(v):
    return jax.nn.gelu(v, approximate=True)


def place_rows(placing, products):
    placed = jnp.einsum("rs,sif->rif", placing, products, precision=lax.Precision.HIGHEST)
    return placed.reshape(-1, products.shape[2])


def shards(features, tile_values, tile_rows, tile_cols, tile_count, weight, bias, cotangent):
    values = tile_values[0, 0]
    rows = tile_rows[0, 0]
    cols = tile_cols[0, 0]
    slots = values.shape[0]
    tile = values.shape[-1]
    block_rows = features.shape[0]
    width = features.shape[1]
    row_tiles = block_rows // tile
    alive = (jnp.arange(slots, dtype=jnp.int32) < tile_count[0, 0]).astype(jnp.float32)
    placing = (rows[None, :] == jnp.arange(row_tiles, dtype=jnp.int32)[:, None]).astype(
        jnp.float32
    ) * alive[None, :]
    everyone = lax.all_gather(features, "dom", axis=0, tiled=True)
    sources = everyone.reshape(-1, tile, width)[cols]
    products = jnp.einsum("sik,skf->sif", values, sources, preferred_element_type=jnp.float32)
    partial_sum = place_rows(placing, products)
    aggregated = lax.psum(partial_sum, "rep").astype(jnp.bfloat16)
    preact = jnp.dot(aggregated, weight, preferred_element_type=jnp.float32) + bias
    activations = gelu_tanh(preact).astype(jnp.bfloat16)
    _, pullback = jax.vjp(gelu_tanh, preact)
    delta = pullback(cotangent.astype(jnp.float32))[0].astype(jnp.bfloat16)
    local_weight = jnp.dot(aggregated.T, delta, preferred_element_type=jnp.float32)
    local_bias = jnp.sum(delta.astype(jnp.float32), axis=0)
    weight_grad, bias_grad = lax.psum((local_weight, local_bias), "dom")
    back = jnp.dot(delta, weight.T, preferred_element_type=jnp.float32).astype(jnp.bfloat16)
    back_blocks = back.reshape(row_tiles, tile, width)[rows]
    slot_terms = jnp.einsum("sik,sif->skf", values, back_blocks, preferred_element_type=jnp.float32)
    slot_terms = slot_terms * alive[:, None, None]
    span = block_rows * lax.axis_size("dom")
    tile_ids = jnp.arange(span // tile, dtype=jnp.int32)
    picking = (tile_ids[:, None] == cols[None, :]).astype(jnp.float32)
    summed = jnp.einsum("cs,skf->ckf", picking, slot_terms, precision=lax.Precision.HIGHEST)
    summed = summed.reshape(span, width)
    shares = lax.psum_scatter(summed, "dom", scatter_dimension=0, tiled=True)
    feature_grad = lax.psum(shares, "rep")
    return (activations, feature_grad, weight_grad, bias_grad)


def solution(mesh):
    return jax.shard_map(
        shards,
        mesh=mesh,
        in_specs=(
            P("dom", None),
            P("dom", "rep", None, None, None),
            P("dom", "rep", None),
            P("dom", "rep", None),
            P("dom", "rep"),
            P(),
            P(),
            P("dom", None),
        ),
        out_specs=(P("dom", None), P("dom", None), P(), P()),
        check_vma=False,
    )
```

profile of v0, /device:TPU:2, one launch (start us, length us, event | category | flops | bytes accessed | tf_op | source)
XLA Modules:
  0.0 607.5 jit_solution(11029567159736102308)
XLA Ops:
  7.2 0.0 copy-start
  7.2 0.0 all-gather.2.cloned.1.call-start
  7.2 0.7 all-gather.2.cloned.1.call-update
  7.9 0.0 reduce-scatter.2.cloned.1.call-start
  8.6 0.7 fusion.31
  9.3 0.7 fusion.32
  10.0 75.2 %all-gather.2.cloned.1.call-done = bf16[32768,128]{1,0:T(8,128)(2,1)} async-done(((bf16[1024,128]{1,0:T(8,128)(2,1)}), bf16[32768,128]{1,0:T(8,128)(2,1)}) %all-gather.2.cloned.1.call-update) | async-done | bytes 8388624 | tf_op jit(solution)/shard_map/all_gather | solution.py:29
  85.1 5.1 gather_fusion
  90.3 0.0 copy-done
  90.3 2.1 fusion.7
  92.4 0.0 copy-start.5
  92.4 2.0 copy.14
  94.4 0.0 copy-done.5
  94.4 0.0 copy-start.3
  94.4 0.0 copy-start.6
  94.4 0.0 copy-start.7
  94.4 2.7 fusion.2
  97.2 0.1 copy.12
  97.3 42.1 %all-reduce.7 = bf16[1024,128]{1,0:T(8,128)(2,1)S(1)} all-reduce(f32[1024,128]{1,0:T(8,128)S(1)} %bitcast.43), channel_id=1, replica_groups=mesh['dom'=32,'rep'=8] {'rep'}, use_global_device_ids=true, to_apply=%region_0.0 | all-reduce | flops 131072 | bytes 786432 | tf_op jit(solution)/shard_map/psum | solution.py:33
  139.4 0.0 copy-done.3
  139.4 0.0 copy-done.6
  139.4 0.0 copy-done.7
  139.4 1.3 convert_reduce_fusion
  140.7 0.0 copy-start.1
  140.7 0.2 convolution_convert_fusion
  140.9 0.5 copy-done.1
  141.4 0.7 gather_fusion.1
  142.2 1.9 fusion.5
  144.0 0.0 copy-start.4
  144.0 2.4 copy.15
  146.4 0.0 copy-done.4
  146.4 6.8 %fusion = f32[256,128,128]{2,0,1:T(8,128)S(1)} fusion(f32[32,128,128]{1,0,2:T(8,128)S(1)} %copy.15, f32[32]{0:T(128)S(1)} %compare_convert_fusion, s32[32]{0:T(128)S(1)} %bitcast.45), kind=kOutput, calls=%fused_computation.2 | convolution fusion | flops 1611145216 | bytes 18874624 | tf_op jit(solution)/shard_map/cs,skf->ckf/dot_general | solution.py:48
  153.2 20.2 %copy.13 = f32[256,128,128]{2,1,0:T(8,128)} copy(f32[256,128,128]{2,0,1:T(8,128)S(1)} %fusion) | data formatting | bytes 33554432 | tf_op jit(solution)/shard_map/cs,skf->ckf/dot_general | solution.py:48
  173.4 0.0 copy-start.2
  173.4 0.0 reduce-scatter.2.cloned.1.call-update
  173.5 0.0 all-reduce.6.cloned.1.call-start
  173.5 0.9 copy-done.2
  174.4 0.9 fusion.35
  175.3 0.0 all-reduce.6.cloned.1.call-update
  175.3 0.0 all-reduce.4.cloned.1.call-start
  175.4 143.5 %reduce-scatter.2.cloned.1.call-done = f32[1024,128]{1,0:T(8,128)} async-done(((f32[32768,128]{1,0:T(8,128)}), f32[1024,128]{1,0:T(8,128)}) %reduce-scatter.2.cloned.1.call-update) | async-done | bytes 524304 | tf_op jit(solution)/shard_map/reduce_scatter | solution.py:50
  318.9 0.0 all-reduce.4.cloned.1.call-update
  318.9 54.3 %psum.31 = f32[128]{0:T(128)} all-reduce(f32[128]{0:T(128)S(1)} %get-tuple-element.4), channel_id=1, replica_groups=mesh['dom'=32,'rep'=8] {'dom'}, use_global_device_ids=true, to_apply=%region_5.0 | all-reduce | flops 128 | bytes 1024 | tf_op jit(solution)/shard_map/psum | solution.py:40
  373.2 135.3 %all-reduce.6.cloned.1.call-done = f32[128,128]{1,0:T(8,128)} async-done(((f32[128,128]{1,0:T(8,128)}), f32[128,128]{1,0:T(8,128)}) %all-reduce.6.cloned.1.call-update) | async-done | bytes 65552 | tf_op jit(solution)/shard_map/psum | solution.py:40
  508.4 89.2 %all-reduce.4.cloned.1.call-done = f32[1024,128]{1,0:T(8,128)} async-done(((f32[1024,128]{1,0:T(8,128)}), f32[1024,128]{1,0:T(8,128)}) %all-reduce.4.cloned.1.call-update) | async-done | bytes 524304 | tf_op jit(solution)/shard_map/psum | solution.py:51
  597.6 1.9 copy.21
  599.5 1.5 copy.22
  (3 shorter events, 0.0 us)
Async XLA Ops:
  7.2 83.1 %copy-start = (bf16[1,1,32,128,128]{4,3,2,1,0:T(8,128)(2,1)S(1)}, bf16[1,1,32,128,128]{4,3,2,1,0:T(8,128)(2,1)}, u32[]{:S(2)}) copy-start(bf16[1,1,32,128,128]{4,3,2,1,0:T(8,128)(2,1)} %param.9) | copy-start | bytes 3145732
  7.2 78.0 %all-gather.2.cloned.1.call-start = ((), (), s32[]{:S(2)}) async-start(), calls=%async_computation.1 | async-start | bytes 8650752 | tf_op jit(solution)/shard_map/all_gather | solution.py:29
  7.9 311.0 %reduce-scatter.2.cloned.1.call-start = ((), (), s32[]{:S(2)}) async-start(), calls=%async_computation.2 | async-start | bytes 17301504 | tf_op jit(solution)/shard_map/reduce_scatter | solution.py:50
  92.4 2.1 copy-start.5
  94.4 44.9 %copy-start.3 = (bf16[128,128]{1,0:T(8,128)(2,1)S(1)}, bf16[128,128]{1,0:T(8,128)(2,1)}, u32[]{:S(2)}) copy-start(bf16[128,128]{1,0:T(8,128)(2,1)} %param.13) | copy-start | bytes 98308
  94.4 45.0 %copy-start.6 = (bf16[1024,128]{1,0:T(8,128)(2,1)S(1)}, bf16[1024,128]{1,0:T(8,128)(2,1)}, u32[]{:S(2)}) copy-start(bf16[1024,128]{1,0:T(8,128)(2,1)} %param.15) | copy-start | bytes 786436
  94.4 45.0 %copy-start.7 = (f32[128]{0:T(128)S(1)}, f32[128]{0:T(128)}, u32[]{:S(2)}) copy-start(f32[128]{0:T(128)} %param.14) | copy-start | bytes 1540
  140.7 0.7 copy-start.1
  144.0 2.4 copy-start.4
  173.4 0.9 copy-start.2
  173.5 335.0 %all-reduce.6.cloned.1.call-start = ((), (), s32[]{:S(2)}) async-start(), calls=%async_computation.4 | async-start | bytes 131072 | tf_op jit(solution)/shard_map/psum | solution.py:40
  175.3 422.3 %all-reduce.4.cloned.1.call-start = ((), (), s32[]{:S(2)}) async-start(), calls=%async_computation.3 | async-start | bytes 1048576 | tf_op jit(solution)/shard_map/psum | solution.py:51
Sparse Core Ops, SparseCore 0:
  9.9 75.2 all-gather.1
  173.6 145.2 reduce-scatter.1
  322.1 186.2 all-reduce.5
  511.1 86.4 all-reduce.3
where the time goes:
time: 611 us; the launch traced here: 607 us
  waiting for transfers between devices  444 us (73%)
  blocking collectives  96.3 us (16%)
  local copies, waits for them, and re-layouts  35.3 us (6%)
  matrix products  15.9 us (3%)
  between operations  14.5 us (2%)
    reduce_scatter x1, waiting for transfers between devices, shards(): shares = lax.psum_scatter(summed, 'dom', scatter_dimension=0, tiled=True)  144 us
    psum x1, waiting for transfers between devices, shards(): weight_grad, bias_grad = lax.psum((local_weight, local_bias), 'dom')  135 us
    psum x1, waiting for transfers between devices, shards(): feature_grad = lax.psum(shares, 'rep')  89.2 us
    all_gather x1, waiting for transfers between devices, shards(): everyone = lax.all_gather(features, 'dom', axis=0, tiled=True)  75.2 us
    psum x1, blocking collectives, shards(): weight_grad, bias_grad = lax.psum((local_weight, local_bias), 'dom')  54.3 us
    psum x1, blocking collectives, shards(): aggregated = lax.psum(partial_sum, 'rep').astype(jnp.bfloat16)  42.1 us
    dot_general x1, local copies, waits for them, and re-layouts, shards(): jnp.einsum('cs,skf->ckf', picking, slot_terms, precision=lax.Precision.HI...  20.2 us
  transfers between devices with their start and end apart: 4, of which 4 were waited for; matrix products, arithmetic and copies ran while one was open for 0% of the time, Pallas kernels for 0%

commit v1 on v0

v1 whole, which is shorter than its diff:
```python
import functools

import jax
import jax.numpy as jnp
from jax import lax
from jax.experimental import pallas as pl
from jax.experimental.pallas import tpu as pltpu
from jax.sharding import Mesh, PartitionSpec as P

AXES = ("yl", "z", "c", "yh", "x")
SIZES = (2, 8, 2, 2, 4)
DOM = ("yl", "z", "c")
PEERS = ("yl", "z")
REP = ("yh", "x")

TILE = 128
SLOTS = 32
ROW_TILES = 8
NX = 4
NH = 2
NP = 16
WIDE = 128
THIN = WIDE // NX
MAIN = ROW_TILES * THIN
EXTRA = 32
CHUNK = MAIN + EXTRA
GRADS = WIDE // (NX * NH)
META = 3 * SLOTS
UNROLL = 16

F32 = jnp.float32
BF16 = jnp.bfloat16
CONTRACT_LAST = (((1,), (1,)), ((), ()))
CONTRACT_FIRST = (((0,), (0,)), ((), ()))
PLAIN = (((1,), (0,)), ((), ()))


def mul(a, b, how):
    return lax.dot_general(a, b, how, preferred_element_type=F32)


def params(mb):
    return pltpu.CompilerParams(vmem_limit_bytes=mb * 1024 * 1024)


def prep_kernel(ids, feat, out):
    first = ids[0] * THIN
    rows = lax.broadcasted_iota(jnp.int32, (THIN, WIDE), 0) + first
    cols = lax.broadcasted_iota(jnp.int32, (THIN, WIDE), 1)
    pick = (rows == cols).astype(BF16)
    for t in range(ROW_TILES):
        part = mul(pick, feat[t * TILE : (t + 1) * TILE, :], CONTRACT_LAST).astype(BF16)
        for p in range(NP):
            out[p, t * THIN : (t + 1) * THIN, :] = part


def slot_place(meta, at, s):
    row = meta[at + s]
    col = meta[at + SLOTS + s]
    live = s < meta[at + 2 * SLOTS]
    owner = col // ROW_TILES
    core = owner % 2
    place = (owner // 2) * ROW_TILES + col % ROW_TILES
    return row, core, place, live


def forward_kernel(ids, meta, tiles, mine, other, out, acc):
    i = pl.program_id(0)

    @pl.when(i == 0)
    def _():
        acc[...] = jnp.zeros_like(acc)

    at = ((ids[0] - i + NX) % NX) * META
    my_core = ids[1]

    def body(g, carry):
        rows, prods = [], []
        for u in range(UNROLL):
            s = g * UNROLL + u
            row, core, place, live = slot_place(meta, at, s)
            src = jnp.where(core == my_core, mine[place], other[place])
            src = jnp.where(live, src, jnp.zeros_like(src))
            prods.append(mul(src, tiles[0, s], CONTRACT_LAST))
            rows.append(row)
        for row, prod in zip(rows, prods):
            acc[row] += prod
        return carry

    lax.fori_loop(0, SLOTS // UNROLL, body, 0)

    @pl.when(i == NX - 1)
    def _():
        done = acc[...].astype(BF16)
        for r in range(NX * NH):
            out[r] = done


def backward_kernel(ids, meta, tiles, parts, weight, bias, cot, act, keep, send, acc, back):
    i = pl.program_id(0)

    @pl.when(i == 0)
    def _():
        acc[...] = jnp.zeros_like(acc)
        x_at = pl.multiple_of(ids[0] * THIN, THIN)
        r_at = pl.multiple_of(ids[2] * GRADS, GRADS)
        w_rows = weight[pl.ds(x_at, THIN), :]
        grow = lax.broadcasted_iota(jnp.int32, (GRADS, WIDE), 0) + r_at
        gcol = lax.broadcasted_iota(jnp.int32, (GRADS, WIDE), 1)
        gpick = (grow == gcol).astype(BF16)
        wsum = jnp.zeros((GRADS, WIDE), F32)
        bsum = jnp.zeros((1, WIDE), F32)
        for t in range(ROW_TILES):
            agg_t = jnp.concatenate(
                [parts[x, t].astype(F32) + parts[NX + x, t].astype(F32) for x in range(NX)], axis=0
            ).astype(BF16)
            pre = mul(agg_t, weight[...], CONTRACT_FIRST) + bias[...]
            sq = pre * pre
            th = jnp.tanh(0.7978845608028654 * pre * (1.0 + 0.044715 * sq))
            half = 0.5 * (1.0 + th)
            act[t * TILE : (t + 1) * TILE, :] = (pre * half).astype(BF16)
            slope = half + 0.5 * pre * (1.0 - th * th) * (
                0.7978845608028654 * (1.0 + (3 * 0.044715) * sq)
            )
            delta = (cot[t * TILE : (t + 1) * TILE, :].astype(F32) * slope).astype(BF16)
            back[t] = mul(w_rows, delta, CONTRACT_LAST).astype(BF16)
            own = mul(gpick, agg_t, PLAIN).astype(BF16)
            wsum = wsum + mul(own, delta, PLAIN)
            bsum = bsum + jnp.sum(delta.astype(F32), axis=0, keepdims=True)
        rest = jnp.where(
            lax.broadcasted_iota(jnp.int32, (EXTRA - GRADS, WIDE), 0) == 0,
            jnp.broadcast_to(bsum, (EXTRA - GRADS, WIDE)),
            0.0,
        )
        extra = jnp.concatenate([wsum, rest], axis=0).astype(BF16)
        for p in range(NP):
            keep[p, MAIN:, :] = extra
            send[p, MAIN:, :] = extra

    at = ((ids[0] - i + NX) % NX) * META
    my_core = ids[1]

    def body(g, carry):
        places, prods = [], []
        for u in range(UNROLL):
            s = g * UNROLL + u
            row, core, place, live = slot_place(meta, at, s)
            src = jnp.where(live, back[row], jnp.zeros((THIN, TILE), BF16))
            prods.append(mul(src, tiles[0, s], PLAIN))
            places.append(jnp.where(core == my_core, 0, NP * ROW_TILES) + place)
        for place, prod in zip(places, prods):
            acc[place] += prod
        return carry

    lax.fori_loop(0, SLOTS // UNROLL, body, 0)

    @pl.when(i == NX - 1)
    def _():
        for p in range(NP):
            for t in range(ROW_TILES):
                keep[p, t * THIN : (t + 1) * THIN, :] = acc[p * ROW_TILES + t].astype(BF16)
                send[p, t * THIN : (t + 1) * THIN, :] = acc[(NP + p) * ROW_TILES + t].astype(BF16)


def gather_sum_kernel(got, out):
    total = got[0].astype(F32)
    for p in range(1, NP):
        total = total + got[p].astype(F32)
    total = total.astype(BF16)
    for r in range(NX * NH):
        out[r] = total


def finish_kernel(got, grad, wgrad, bgrad):
    for t in range(ROW_TILES):
        rows = slice(t * THIN, (t + 1) * THIN)
        block = jnp.concatenate(
            [got[x, rows, :].astype(F32) + got[NX + x, rows, :].astype(F32) for x in range(NX)], axis=0
        )
        grad[t * TILE : (t + 1) * TILE, :] = block.T
    for r in range(NX * NH):
        wgrad[r * GRADS : (r + 1) * GRADS, :] = got[r, MAIN : MAIN + GRADS, :].astype(F32)
    bgrad[...] = got[0, MAIN + GRADS : CHUNK, :].astype(F32)[0:1, :]


def rotate(value, step):
    return lax.ppermute(value, "x", [(k, (k + step) % NX) for k in range(NX)])


def swap_core(value):
    return lax.ppermute(value, "c", [(0, 1), (1, 0)])


def exchange(value, axes):
    return lax.all_to_all(value, axes, 0, 0, tiled=True)


def whole(shape):
    return pl.BlockSpec(shape, lambda *_: (0,) * len(shape))


def shards(features, tile_values, tile_rows, tile_cols, tile_count, weight, bias, cotangent):
    x = lax.axis_index("x").astype(jnp.int32)
    core = lax.axis_index("c").astype(jnp.int32)
    r = lax.axis_index("yh").astype(jnp.int32) * NX + x
    ids = jnp.stack([x, core, r])
    tiles = lax.all_gather(tile_values[0, 0], "x", axis=0)
    own_meta = jnp.concatenate(
        [
            tile_rows[0, 0],
            tile_cols[0, 0],
            jnp.broadcast_to(tile_count[0, 0], (SLOTS,)),
        ]
    )
    meta = jnp.concatenate([own_meta] + [rotate(own_meta, k) for k in range(1, NX)])

    copies = pl.pallas_call(
        prep_kernel,
        out_shape=jax.ShapeDtypeStruct((NP, MAIN, TILE), BF16),
        grid_spec=pltpu.PrefetchScalarGridSpec(
            num_scalar_prefetch=1,
            grid=(1,),
            in_specs=[whole((ROW_TILES * TILE, WIDE))],
            out_specs=whole((NP, MAIN, TILE)),
        ),
        compiler_params=params(16),
        name="prep",
    )(ids, features)
    mine = exchange(copies, PEERS)
    other = swap_core(mine)
    mine = mine.reshape(NP * ROW_TILES, THIN, TILE)
    other = other.reshape(NP * ROW_TILES, THIN, TILE)

    tile_spec = pl.BlockSpec((1, SLOTS, TILE, TILE), lambda i, *_: (i, 0, 0, 0))
    parts = pl.pallas_call(
        forward_kernel,
        out_shape=jax.ShapeDtypeStruct((NX * NH, ROW_TILES, THIN, TILE), BF16),
        grid_spec=pltpu.PrefetchScalarGridSpec(
            num_scalar_prefetch=2,
            grid=(NX,),
            in_specs=[tile_spec, whole(mine.shape), whole(other.shape)],
            out_specs=whole((NX * NH, ROW_TILES, THIN, TILE)),
            scratch_shapes=[pltpu.VMEM((ROW_TILES, THIN, TILE), F32)],
        ),
        compiler_params=params(32),
        name="forward",
    )(ids, meta, tiles, mine, other)
    parts = exchange(parts, REP)

    activations, keep, send = pl.pallas_call(
        backward_kernel,
        out_shape=(
            jax.ShapeDtypeStruct((ROW_TILES * TILE, WIDE), BF16),
            jax.ShapeDtypeStruct((NP, CHUNK, TILE), BF16),
            jax.ShapeDtypeStruct((NP, CHUNK, TILE), BF16),
        ),
        grid_spec=pltpu.PrefetchScalarGridSpec(
            num_scalar_prefetch=2,
            grid=(NX,),
            in_specs=[
                tile_spec,
                whole(parts.shape),
                whole((WIDE, WIDE)),
                whole((1, WIDE)),
                whole((ROW_TILES * TILE, WIDE)),
            ],
            out_specs=(
                whole((ROW_TILES * TILE, WIDE)),
                whole((NP, CHUNK, TILE)),
                whole((NP, CHUNK, TILE)),
            ),
            scratch_shapes=[
                pltpu.VMEM((2 * NP * ROW_TILES, THIN, TILE), F32),
                pltpu.VMEM((ROW_TILES, THIN, TILE), BF16),
            ],
        ),
        compiler_params=params(40),
        name="backward",
    )(ids, meta, tiles, parts, weight, bias.reshape(1, WIDE), cotangent)

    paired = (keep.astype(F32) + swap_core(send).astype(F32)).astype(BF16)
    got = exchange(paired, PEERS)
    shared = pl.pallas_call(
        gather_sum_kernel,
        out_shape=jax.ShapeDtypeStruct((NX * NH, CHUNK, TILE), BF16),
        compiler_params=params(16),
        name="gather_sum",
    )(got)
    got = exchange(shared, REP)
    feature_grad, weight_grad, bias_grad = pl.pallas_call(
        finish_kernel,
        out_shape=(
            jax.ShapeDtypeStruct((ROW_TILES * TILE, WIDE), F32),
            jax.ShapeDtypeStruct((WIDE, WIDE), F32),
            jax.ShapeDtypeStruct((1, WIDE), F32),
        ),
        compiler_params=params(16),
        name="finish",
    )(got)
    return (activations, feature_grad, weight_grad, bias_grad.reshape(WIDE))


def solution(mesh):
    fine = Mesh(mesh.devices.reshape(SIZES), AXES)
    return jax.shard_map(
        shards,
        mesh=fine,
        in_specs=(
            P(DOM, None),
            P(DOM, REP, None, None, None),
            P(DOM, REP, None),
            P(DOM, REP, None),
            P(DOM, REP),
            P(),
            P(),
            P(DOM, None),
        ),
        out_specs=(P(DOM, None), P(DOM, None), P(), P()),
        check_vma=False,
    )
```

time: 611 us -> 156 us (0.26)
  waiting for transfers between devices: 444 us -> 15.6 us
  local copies, waits for them, and re-layouts: 35.3 us -> 2.42 us
  matrix products: 15.9 us -> 0 us
  Pallas kernels: 0 us -> 11.4 us
  blocking collectives: 96.3 us -> 106 us
    psum x2 -> x0, waiting for transfers between devices: 224 us -> none  [the longest x1 135 us: shards(): weight_grad, bias_grad = lax.psum((local_weight, local_bias), 'dom')]
    reduce_scatter x1 -> x0, waiting for transfers between devices: 144 us -> none  [shards(): shares = lax.psum_scatter(summed, 'dom', scatter_dimension=0, tiled=True)]
    all_to_all x0 -> x4, blocking collectives: none -> 106 us  [exchange(): return lax.all_to_all(value, axes, 0, 0, tiled=True)]
    psum x2 -> x0, blocking collectives: 96.3 us -> none  [the longest x1 54.3 us: shards(): weight_grad, bias_grad = lax.psum((local_weight, local_bias), 'dom')]
    all_gather x1, waiting for transfers between devices: 75.2 us -> 10.4 us  [shards(): tiles = lax.all_gather(tile_values[0, 0], 'x', axis=0)]
    dot_general x4 -> x0, local copies, waits for them, and re-layouts: 24.8 us -> none  [the longest x1 20.2 us: shards(): jnp.einsum('cs,skf->ckf', picking, slot_terms, precision=lax.Precision.HI...]
    dot_general x7 -> x0, matrix products: 15.9 us -> none  [the longest x1 6.8 us: shards(): jnp.einsum('cs,skf->ckf', picking, slot_terms, precision=lax.Precision.HI...]
    pallas_call x0 -> x5, Pallas kernels: none -> 11.4 us  [the longest x1 5.56 us: shards(): pl.pallas_call(backward_kernel, out_shape=(jax.ShapeDtypeStruct((ROW_TILE...]
  transfers between devices with their start and end apart: 4 -> 6, of which waited for: 4 -> 4; matrix products, arithmetic and copies ran while one was open for 0% -> 0% of each run, Pallas kernels for 0% -> 1%
where the time goes in v1:
time: 156 us; the launch traced here: 155 us
  blocking collectives  106 us (68%)
  waiting for transfers between devices  15.6 us (10%)
  between operations  14.8 us (9%)
  Pallas kernels  11.4 us (7%)
  starting transfers between devices  4.82 us (3%)
  local copies, waits for them, and re-layouts  2.42 us (2%)
    all_to_all x4, blocking collectives, exchange(): return lax.all_to_all(value, axes, 0, 0, tiled=True)  106 us
    all_gather x1, waiting for transfers between devices, shards(): tiles = lax.all_gather(tile_values[0, 0], 'x', axis=0)  10.4 us
    pallas_call x1, Pallas kernels, shards(): pl.pallas_call(backward_kernel, out_shape=(jax.ShapeDtypeStruct((ROW_TILE...  5.56 us
    ppermute x3, starting transfers between devices, rotate(): return lax.ppermute(value, 'x', [(k, (k + step) % NX) for k in range(NX)])  4.77 us
    pallas_call x1, Pallas kernels, shards(): pl.pallas_call(forward_kernel, out_shape=jax.ShapeDtypeStruct((NX * NH, R...  3.84 us
  transfers between devices with their start and end apart: 6, of which 4 were waited for; matrix products, arithmetic and copies ran while one was open for 0% of the time, Pallas kernels for 1%

profile of v1, /device:TPU:2, one launch (start us, length us, event | category | flops | bytes accessed | tf_op | source)
XLA Modules:
  0.0 155.1 jit_solution(4529323256803499944)
XLA Ops:
  7.2 0.0 copy-start.2
  7.2 0.0 all-gather.3.cloned.1.call-start
  7.2 0.7 all-gather.3.cloned.1.call-update
  7.9 0.1 pad_add_fusion.ids
  8.0 0.1 copy-done.2
  8.1 0.8 prep.1
  8.9 0.0 copy-start.6
  8.9 0.0 copy-start.7
  9.0 36.3 %all_to_all.20 = bf16[16,256,128]{2,1,0:T(8,128)(2,1)S(1)} all-to-all(bf16[16,256,128]{2,1,0:T(8,128)(2,1)S(1)} %prep.1), channel_id=1, replica_groups=mesh['yl'=2,'z'=8,'c'=2,'yh'=2,'x'=4] {'yl','z'}, dimensions={0} | all-to-all | bytes 2097152 | tf_op jit(solution)/shard_map/all_to_all | solution.py:195
  45.3 0.0 collective-permute-start.3
  45.9 0.0 copy-done.6
  45.9 0.0 copy-done.7
  46.0 0.1 pad_add_fusion.1
  46.0 0.6 collective-permute-start.2
  46.6 2.4 %collective-permute-start.1 = (s32[96]{0:T(128)S(1)}, s32[96]{0:T(128)S(1)}, u32[]{:S(2)}, u32[]{:S(2)}) collective-permute-start(s32[96]{0:T(128)S(1)} %pad_add_fusion.1), channel_id=1, source_target_pairs={{0,2},{1,3},{2,0},{3,1},{4,6},{5,7},{6,4},{7,5},{8,10},{9,11},{10,... | collective-permute-start | bytes 1160 | tf_op jit(solution)/shard_map/ppermute | solution.py:187
  49.0 1.8 %collective-permute-start = (s32[96]{0:T(128)S(1)}, s32[96]{0:T(128)S(1)}, u32[]{:S(2)}, u32[]{:S(2)}) collective-permute-start(s32[96]{0:T(128)S(1)} %pad_add_fusion.1), channel_id=1, source_target_pairs={{0,1},{1,2},{2,3},{3,0},{4,5},{5,6},{6,7},{7,4},{8,9},{9,10},{10,1... | collective-permute-start | bytes 1160 | tf_op jit(solution)/shard_map/ppermute | solution.py:187
  50.8 0.0 collective-permute-done.2
  50.8 0.8 collective-permute-done.1
  51.6 0.9 collective-permute-done
  52.5 0.1 concatenate.8.meta
  52.6 0.0 collective-permute-done.3
  52.6 10.4 %all-gather.3.cloned.1.call-done = bf16[4,1,32,128,128]{4,3,2,1,0:T(8,128)(2,1)} async-done(((bf16[1,1,32,128,128]{4,3,2,1,0:T(8,128)(2,1)}), bf16[4,1,32,128,128]{4,3,2,1,0:T(8,128)(2,1)}) %all-gather.3.cloned.1.call-update) | async-done | bytes 4194320 | tf_op jit(solution)/shard_map/all_gather | solution.py:207
  63.0 0.0 copy-start
  63.0 2.2 %copy-done = bf16[4,1,32,128,128]{4,3,2,1,0:T(8,128)(2,1)S(1)} copy-done((bf16[4,1,32,128,128]{4,3,2,1,0:T(8,128)(2,1)S(1)}, bf16[4,1,32,128,128]{4,3,2,1,0:T(8,128)(2,1)}, u32[]{:S(2)}) %copy-start) | copy-done | bytes 4194328
  65.2 0.0 copy-start.1
  65.2 0.0 copy-start.4
  65.2 0.0 copy-start.5
  65.2 3.8 %forward.1 = bf16[8,8,32,128]{3,2,1,0:T(8,128)(2,1)S(1)} custom-call(s32[3]{0:T(128)S(1)} %pad_add_fusion.ids, s32[384]{0:T(512)S(1)} %concatenate.8.meta, bf16[4,32,128,128]{3,2,1,0:T(8,128)(2,1)S(1)} %bitcast.12, bf16[128,32,128]{2,1,0:T(8,128)(2,1)S(1)} %bitcast.14, bf16[128,32,128]{2,1,0:T(8,128)(2,1)S(1)} %bitcast.15), custom_call_target="tpu_custom_call" | custom-call | tf_op jit(solution)/shard_map/forward/pallas_call | solution.py:235
  69.0 0.0 copy-start.3
  69.0 17.4 %all_to_all.21.parts = bf16[8,8,32,128]{3,2,1,0:T(8,128)(2,1)S(1)} all-to-all(bf16[8,8,32,128]{3,2,1,0:T(8,128)(2,1)S(1)} %forward.1), channel_id=1, replica_groups=mesh['yl'=2,'z'=8,'c'=2,'yh'=2,'x'=4] {'yh','x'}, dimensions={0} | all-to-all | bytes 1048576 | tf_op jit(solution)/shard_map/all_to_all | solution.py:195
  86.4 0.0 copy-done.1
  86.4 0.0 copy-done.4
  86.4 0.0 copy-done.5
  86.4 0.0 copy-done.3
  86.4 5.6 %backward.1 = (bf16[1024,128]{1,0:T(8,128)(2,1)}, bf16[16,288,128]{2,1,0:T(8,128)(2,1)S(1)}, bf16[16,288,128]{2,1,0:T(8,128)(2,1)S(1)}) custom-call(s32[3]{0:T(128)S(1)} %pad_add_fusion.ids, s32[384]{0:T(512)S(1)} %concatenate.8.meta, bf16[4,32,128,128]{3,2,1,0:T(8,128)(2,1)S(1)} %bitcast.13, bf16[8,8,32,128]{3,2,1,0:T(8,128)(2,1)S(1)} %all_to_all.21.parts, ...), custom_call_target="tpu_custom_call" | custom-call | tf_op jit(solution)/shard_map/backward/pallas_call | solution.py:250
  92.0 0.0 collective-permute-start.4
  92.0 2.8 %collective-permute-done.4 = bf16[16,288,128]{2,1,0:T(8,128)(2,1)S(1)} collective-permute-done((bf16[16,288,128]{2,1,0:T(8,128)(2,1)S(1)}, bf16[16,288,128]{2,1,0:T(8,128)(2,1)S(1)}, u32[]{:S(2)}, u32[]{:S(2)}) %collective-permute-start.4) | collective-permute-done | bytes 1179680 | tf_op jit(solution)/shard_map/ppermute | solution.py:191
  94.8 0.3 add_convert_fusion
  95.1 38.3 %all_to_all.22.got = bf16[16,288,128]{2,1,0:T(8,128)(2,1)S(1)} all-to-all(bf16[16,288,128]{2,1,0:T(8,128)(2,1)S(1)} %add_convert_fusion), channel_id=1, replica_groups=mesh['yl'=2,'z'=8,'c'=2,'yh'=2,'x'=4] {'yl','z'}, dimensions={0} | all-to-all | bytes 2359296 | tf_op jit(solution)/shard_map/all_to_all | solution.py:195
  133.4 0.2 gather_sum.1
  133.6 13.6 %all_to_all.23.got = bf16[8,288,128]{2,1,0:T(8,128)(2,1)S(1)} all-to-all(bf16[8,288,128]{2,1,0:T(8,128)(2,1)S(1)} %gather_sum.1), channel_id=1, replica_groups=mesh['yl'=2,'z'=8,'c'=2,'yh'=2,'x'=4] {'yh','x'}, dimensions={0} | all-to-all | bytes 1179648 | tf_op jit(solution)/shard_map/all_to_all | solution.py:195
  147.2 1.0 finish.1
  (1 shorter events, 0.0 us)
Async XLA Ops:
  7.2 1.0 copy-start.2
  7.2 55.8 %all-gather.3.cloned.1.call-start = ((), (), s32[]{:S(2)}) async-start(), calls=%async_computation.4 | async-start | bytes 5242880 | tf_op jit(solution)/shard_map/all_gather | solution.py:207
  8.9 37.0 %copy-start.6 = (s32[1,1,32]{2,1,0:T(1,128)S(1)}, s32[1,1,32]{2,1,0:T(1,128)}, u32[]{:S(2)}) copy-start(s32[1,1,32]{2,1,0:T(1,128)} %param.10) | copy-start | bytes 388
  8.9 37.0 %copy-start.7 = (s32[1,1,32]{2,1,0:T(1,128)S(1)}, s32[1,1,32]{2,1,0:T(1,128)}, u32[]{:S(2)}) copy-start(s32[1,1,32]{2,1,0:T(1,128)} %param.11) | copy-start | bytes 388
  45.3 7.4 %collective-permute-start.3 = (bf16[16,256,128]{2,1,0:T(8,128)(2,1)S(1)}, bf16[16,256,128]{2,1,0:T(8,128)(2,1)S(1)}, u32[]{:S(2)}, u32[]{:S(2)}) collective-permute-start(bf16[16,256,128]{2,1,0:T(8,128)(2,1)S(1)} %all_to_all.20), channel_id=1, source_target_pairs={{0,8},{8,0},{1,9},{9,1},{2,10},{10,2},{3,11},{11,3},{4,12},{12,4},... | collective-permute-start | bytes 3145736 | tf_op jit(solution)/shard_map/ppermute | solution.py:191
  46.0 4.8 %collective-permute-start.2 = (s32[96]{0:T(128)S(1)}, s32[96]{0:T(128)S(1)}, u32[]{:S(2)}, u32[]{:S(2)}) collective-permute-start(s32[96]{0:T(128)S(1)} %pad_add_fusion.1), channel_id=1, source_target_pairs={{0,3},{1,0},{2,1},{3,2},{4,7},{5,4},{6,5},{7,6},{8,11},{9,8},{10,9... | collective-permute-start | bytes 1160 | tf_op jit(solution)/shard_map/ppermute | solution.py:187
  46.6 5.0 %collective-permute-start.1 = (s32[96]{0:T(128)S(1)}, s32[96]{0:T(128)S(1)}, u32[]{:S(2)}, u32[]{:S(2)}) collective-permute-start(s32[96]{0:T(128)S(1)} %pad_add_fusion.1), channel_id=1, source_target_pairs={{0,2},{1,3},{2,0},{3,1},{4,6},{5,7},{6,4},{7,5},{8,10},{9,11},{10,... | collective-permute-start | bytes 1160 | tf_op jit(solution)/shard_map/ppermute | solution.py:187
  49.0 3.5 %collective-permute-start = (s32[96]{0:T(128)S(1)}, s32[96]{0:T(128)S(1)}, u32[]{:S(2)}, u32[]{:S(2)}) collective-permute-start(s32[96]{0:T(128)S(1)} %pad_add_fusion.1), channel_id=1, source_target_pairs={{0,1},{1,2},{2,3},{3,0},{4,5},{5,6},{6,7},{7,4},{8,9},{9,10},{10,1... | collective-permute-start | bytes 1160 | tf_op jit(solution)/shard_map/ppermute | solution.py:187
  63.0 2.2 %copy-start = (bf16[4,1,32,128,128]{4,3,2,1,0:T(8,128)(2,1)S(1)}, bf16[4,1,32,128,128]{4,3,2,1,0:T(8,128)(2,1)}, u32[]{:S(2)}) copy-start(bf16[4,1,32,128,128]{4,3,2,1,0:T(8,128)(2,1)} %all-gather.3.cloned.1.call-done) | copy-start | bytes 12582916
  65.2 21.2 %copy-start.1 = (bf16[4,1,32,128,128]{4,3,2,1,0:T(8,128)(2,1)S(1)}, bf16[4,1,32,128,128]{4,3,2,1,0:T(8,128)(2,1)}, u32[]{:S(2)}) copy-start(bf16[4,1,32,128,128]{4,3,2,1,0:T(8,128)(2,1)} %all-gather.3.cloned.1.call-done) | copy-start | bytes 12582916
  65.2 21.2 %copy-start.4 = (bf16[128,128]{1,0:T(8,128)(2,1)S(1)}, bf16[128,128]{1,0:T(8,128)(2,1)}, u32[]{:S(2)}) copy-start(bf16[128,128]{1,0:T(8,128)(2,1)} %weight.1) | copy-start | bytes 98308
  65.2 21.2 %copy-start.5 = (f32[128]{0:T(128)S(1)}, f32[128]{0:T(128)}, u32[]{:S(2)}) copy-start(f32[128]{0:T(128)} %param.14) | copy-start | bytes 1540
  69.0 17.4 %copy-start.3 = (bf16[1024,128]{1,0:T(8,128)(2,1)S(1)}, bf16[1024,128]{1,0:T(8,128)(2,1)}, u32[]{:S(2)}) copy-start(bf16[1024,128]{1,0:T(8,128)(2,1)} %cot.1) | copy-start | bytes 786436
  92.0 2.8 %collective-permute-start.4 = (bf16[16,288,128]{2,1,0:T(8,128)(2,1)S(1)}, bf16[16,288,128]{2,1,0:T(8,128)(2,1)S(1)}, u32[]{:S(2)}, u32[]{:S(2)}) collective-permute-start(bf16[16,288,128]{2,1,0:T(8,128)(2,1)S(1)} %get-tuple-element.12), channel_id=1, source_target_pairs={{0,8},{8,0},{1,9},{9,1},{2,10},{10,2},{3,11},{11,3},{4,12},{12,4},... | collective-permute-start | bytes 3538952 | tf_op jit(solution)/shard_map/ppermute | solution.py:191
Sparse Core Ops, SparseCore 0:
  9.8 53.1 all-gather.2

commit v2 on v0

v2 whole, which is shorter than its diff:
```python
import jax
import jax.numpy as jnp
from jax import lax
from jax.experimental import pallas as pl
from jax.experimental.pallas import tpu as pltpu
from jax.sharding import Mesh, PartitionSpec as P

AXES = ("yl", "z", "c", "yh", "x")
SIZES = (2, 8, 2, 2, 4)
DOM = ("yl", "z", "c")
PEERS = ("yl", "z")
REP = ("yh", "x")

TILE = 128
SLOTS = 32
HALF = SLOTS // 2
ROW_TILES = 8
NX = 4
NY = 4
NZ = 8
NP = 16
NR = 8
WIDE = 128
THIN = WIDE // NX
MAIN = ROW_TILES * THIN
BLOCK_HALF = ROW_TILES // 2
LAST = BLOCK_HALF * THIN
GRADS = THIN // 2
EXTRA = 32
SWAPS = 4
PIECE = NZ * LAST
META = 128
RELAY_COST = pl.CostEstimate(flops=20 * 10**9, bytes_accessed=60 * 10**6, transcendentals=0)
UNROLL = 16

F32 = jnp.float32
BF16 = jnp.bfloat16
CONTRACT_LAST = (((1,), (1,)), ((), ()))
CONTRACT_FIRST = (((0,), (0,)), ((), ()))
PLAIN = (((1,), (0,)), ((), ()))


def mul(a, b, how):
    return lax.dot_general(a, b, how, preferred_element_type=F32)


def prep_kernel(ids, feat, out):
    first = ids[0] * THIN
    rows = lax.broadcasted_iota(jnp.int32, (THIN, WIDE), 0) + first
    cols = lax.broadcasted_iota(jnp.int32, (THIN, WIDE), 1)
    pick = (rows == cols).astype(BF16)
    for t in range(ROW_TILES):
        part = mul(pick, feat[t * TILE : (t + 1) * TILE, :], CONTRACT_LAST).astype(BF16)
        for p in range(NP):
            out[p, t * THIN : (t + 1) * THIN, :] = part


def each_group(tile_refs, work):
    for ref, source, skip in tile_refs:
        lax.fori_loop(
            0, ref.shape[0] // UNROLL, lambda g, _, a=ref, b=source, c=skip: work(a, b, c, g), 0
        )


def relay_kernel(left, right, own_meta, meta_l, meta_r, meta_f, out_a, out_b, meta):
    out_a[...] = left[0:HALF]
    out_b[...] = right[HALF:SLOTS]
    for k, part in enumerate((own_meta, meta_l, meta_r, meta_f)):
        meta[k : k + 1, :] = part[...]


def forward_kernel(ids, meta, own, left, right, far_a, far_b, mine, *rest):
    others, out = rest[:SWAPS], rest[SWAPS]
    out[...] = jnp.zeros_like(out)
    my_core = ids[1]
    per = NP * ROW_TILES // SWAPS

    def work(tiles, source, skip, g):
        at = source * META
        rows, prods = [], []
        for u in range(UNROLL):
            s = g * UNROLL + u
            row = meta[at + skip + s]
            col = meta[at + SLOTS + skip + s]
            live = skip + s < meta[at + 2 * SLOTS]
            owner = col // ROW_TILES
            place = (owner // 2) * ROW_TILES + col % ROW_TILES
            src, inner = mine[place], place % per
            for k, other in enumerate(others):
                here = (owner % 2 != my_core) & (place // per == k)
                src = jnp.where(here, other[inner], src)
            src = jnp.where(live, src, jnp.zeros_like(src))
            prods.append(mul(src, tiles[s], CONTRACT_LAST))
            rows.append(row)
        for row, prod in zip(rows, prods):
            out[row] += prod
        return 0

    each_group([(own, 0, 0), (left, 1, 0), (right, 2, 0), (far_a, 3, 0), (far_b, 3, HALF)], work)


def backward_kernel(
    ids, meta, own, left, right, far_a, far_b, agg, agg_l, agg_r, agg_f, weight, bias, cot,
    act, keep, send, acc, back, full, slopes, wsum,
):
    x, my_core, yl, yh = ids[0], ids[1], ids[2], ids[3]
    acc[...] = jnp.zeros_like(acc)
    for t in range(ROW_TILES):
        for k, part in ((0, agg), (1, agg_l), (3, agg_r), (2, agg_f)):
            full[t, pl.ds(pl.multiple_of(((x - k + NX) % NX) * THIN, THIN), THIN), :] = part[t]
    w_rows = weight[pl.ds(pl.multiple_of(x * THIN, THIN), THIN), :]
    for t in range(ROW_TILES):
        pre = mul(full[t], weight[...], CONTRACT_FIRST) + bias[...]
        sq = pre * pre
        th = jnp.tanh(0.7978845608028654 * pre * (1.0 + 0.044715 * sq))
        half = 0.5 * (1.0 + th)
        act[t * TILE : (t + 1) * TILE, :] = (pre * half).astype(BF16)
        slope = half + 0.5 * pre * (1.0 - th * th) * (
            0.7978845608028654 * (1.0 + (3 * 0.044715) * sq)
        )
        delta = (cot[t * TILE : (t + 1) * TILE, :].astype(F32) * slope).astype(BF16)
        slopes[t] = delta
        back[t] = mul(w_rows, delta, CONTRACT_LAST).astype(BF16)
    bsum = jnp.zeros((1, WIDE), F32)
    wpart = jnp.zeros((THIN, WIDE), F32)
    for t in range(BLOCK_HALF):
        at = yh * BLOCK_HALF + t
        delta = slopes[at]
        wpart = wpart + mul(agg[at], delta, PLAIN)
        bsum = bsum + jnp.sum(delta.astype(F32), axis=0, keepdims=True)
    wsum[...] = wpart
    rest = jnp.where(
        lax.broadcasted_iota(jnp.int32, (EXTRA - GRADS, WIDE), 0) == 0,
        jnp.broadcast_to(bsum, (EXTRA - GRADS, WIDE)),
        0.0,
    )
    y = yh * 2 + yl
    for k in range(NY):
        there = ((y + k) % NY) // 2
        some = wsum[pl.ds(pl.multiple_of(there * GRADS, GRADS), GRADS), :]
        extra = jnp.concatenate([some, rest], axis=0).astype(BF16)
        keep[k, PIECE:, :] = extra
        send[k, PIECE:, :] = extra

    def work(tiles, source, skip, g):
        at = source * META
        places, prods = [], []
        for u in range(UNROLL):
            s = g * UNROLL + u
            row = meta[at + skip + s]
            col = meta[at + SLOTS + skip + s]
            live = skip + s < meta[at + 2 * SLOTS]
            owner, block = col // ROW_TILES, col % ROW_TILES
            core, z, to_yl = owner % 2, (owner // 2) % NZ, owner // (2 * NZ)
            k = ((block // BLOCK_HALF) * 2 + to_yl - y + NY) % NY
            place = jnp.where(core == my_core, 0, NY) + k
            place = (place * NZ + z) * BLOCK_HALF + block % BLOCK_HALF
            src = jnp.where(live, back[row], jnp.zeros((THIN, TILE), BF16))
            prods.append(mul(src, tiles[s], PLAIN))
            places.append(place)
        for place, prod in zip(places, prods):
            acc[place] += prod
        return 0

    each_group([(own, 0, 0), (left, 1, 0), (right, 2, 0), (far_a, 3, 0), (far_b, 3, HALF)], work)
    per = NZ * BLOCK_HALF
    for k in range(NY):
        for i in range(per):
            keep[k, i * THIN : (i + 1) * THIN, :] = acc[k * per + i].astype(BF16)
            send[k, i * THIN : (i + 1) * THIN, :] = acc[(NY + k) * per + i].astype(BF16)


def pair_kernel(keep, got, *outs):
    for k, out in enumerate(outs):
        out[...] = (keep[k].astype(F32) + got[k].astype(F32)).astype(BF16)


def y_sum_kernel(own, before, across, after, out):
    def total(rows):
        near = own[rows, :].astype(F32) + across[rows, :].astype(F32)
        return (near + (before[rows, :].astype(F32) + after[rows, :].astype(F32))).astype(BF16)

    extra = total(slice(PIECE, PIECE + EXTRA))
    for z in range(NZ):
        out[z, 0:LAST, :] = total(slice(z * LAST, (z + 1) * LAST))
        out[z, LAST:, :] = extra


def z_sum_kernel(got, out):
    total = got[0].astype(F32)
    for z in range(1, NZ):
        total = total + got[z].astype(F32)
    total = total.astype(BF16)
    for r in range(NR):
        out[r] = total


def finish_kernel(got, grad, wgrad, bgrad):
    for t in range(ROW_TILES):
        first = (t // BLOCK_HALF) * NX
        at = (t % BLOCK_HALF) * THIN
        block = jnp.concatenate(
            [got[first + x, at : at + THIN, :].astype(F32) for x in range(NX)], axis=0
        )
        grad[t * TILE : (t + 1) * TILE, :] = block.T
    for yh in range(2):
        for x in range(NX):
            to = x * THIN + yh * GRADS
            wgrad[to : to + GRADS, :] = got[yh * NX + x, LAST : LAST + GRADS, :].astype(F32)
    bgrad[...] = got[0, LAST + GRADS : LAST + EXTRA, :].astype(F32)[0:1, :]


def rotate(value, step):
    return lax.ppermute(value, "x", [(k, (k + step) % NX) for k in range(NX)])


def along_y(value, step):
    pairs = []
    for y in range(NY):
        to = (y + step) % NY
        pairs.append(((y % 2) * 2 + y // 2, (to % 2) * 2 + to // 2))
    return lax.ppermute(value, ("yl", "yh"), pairs)


def swap(value, axis):
    return lax.ppermute(value, axis, [(0, 1), (1, 0)])


def exchange(value, axes):
    return lax.all_to_all(value, axes, 0, 0, tiled=True)


def kernel_call(body, name, outs, scalars, scratch, mb, *args, cost=None):
    one = isinstance(outs, tuple)
    shapes = [outs] if one else outs
    result = pl.pallas_call(
        body,
        out_shape=[jax.ShapeDtypeStruct(s, d) for s, d in shapes],
        grid_spec=pltpu.PrefetchScalarGridSpec(
            num_scalar_prefetch=scalars,
            grid=(),
            in_specs=[pl.BlockSpec(memory_space=pltpu.VMEM)] * (len(args) - scalars),
            out_specs=[pl.BlockSpec(memory_space=pltpu.VMEM)] * len(shapes),
            scratch_shapes=scratch,
        ),
        compiler_params=pltpu.CompilerParams(vmem_limit_bytes=mb * 1024 * 1024),
        cost_estimate=cost,
        name=name,
    )(*args)
    return result[0] if one else result


def shards(features, tile_values, tile_rows, tile_cols, tile_count, weight, bias, cotangent):
    x, core, yl, yh = (lax.axis_index(a).astype(jnp.int32) for a in ("x", "c", "yl", "yh"))
    ids = jnp.stack([x, core, yl, yh])
    own = tile_values[0, 0]
    left = rotate(own, 1)
    right = rotate(own, NX - 1)
    count = jnp.broadcast_to(tile_count, (1, META - 2 * SLOTS))
    own_meta = jnp.concatenate([tile_rows[0], tile_cols[0], count], axis=1)
    half = ((HALF, TILE, TILE), BF16)
    pass_a, pass_b, meta = kernel_call(
        relay_kernel,
        "relay",
        [half, half, ((NX, META), jnp.int32)],
        0,
        [],
        16,
        left,
        right,
        own_meta,
        rotate(own_meta, 1),
        rotate(own_meta, NX - 1),
        rotate(own_meta, 2),
        cost=RELAY_COST,
    )
    meta = meta.reshape(NX * META)
    far_a, far_b = rotate(pass_a, 1), rotate(pass_b, NX - 1)
    tiles = (own, left, right, far_a, far_b)

    copies = kernel_call(prep_kernel, "prep", ((NP, MAIN, TILE), BF16), 1, [], 16, ids, features)
    mine = exchange(copies, PEERS)
    mine = mine.reshape(NP * ROW_TILES, THIN, TILE)
    per = NP * ROW_TILES // SWAPS
    others = [swap(mine[k * per : (k + 1) * per], "c") for k in range(SWAPS)]

    thin = (ROW_TILES, THIN, TILE)
    part = kernel_call(
        forward_kernel, "forward", (thin, F32), 2, [], 40, ids, meta, *tiles, mine, *others
    )
    agg = (part + swap(part, "yh")).astype(BF16)
    agg_l, agg_r, agg_f = rotate(agg, 1), rotate(agg, NX - 1), rotate(agg, 2)

    piece = PIECE + EXTRA
    square = (ROW_TILES, TILE, WIDE)
    activations, keep, send = kernel_call(
        backward_kernel,
        "backward",
        [((ROW_TILES * TILE, WIDE), BF16), ((NY, piece, TILE), BF16), ((NY, piece, TILE), BF16)],
        2,
        [
            pltpu.VMEM((2 * NY * NZ * BLOCK_HALF, THIN, TILE), F32),
            pltpu.VMEM(thin, BF16),
            pltpu.VMEM(square, BF16),
            pltpu.VMEM(square, BF16),
            pltpu.VMEM((THIN, WIDE), F32),
        ],
        40,
        ids,
        meta,
        *tiles,
        agg,
        agg_l,
        agg_r,
        agg_f,
        weight,
        bias.reshape(1, WIDE),
        cotangent,
    )
    got = swap(send, "c")
    stay, one, two, three = kernel_call(
        pair_kernel, "pair", [((piece, TILE), BF16)] * NY, 0, [], 16, keep, got
    )
    before, across, after = along_y(one, 1), along_y(two, 2), along_y(three, 3)
    last = LAST + EXTRA
    summed = kernel_call(
        y_sum_kernel, "y_sum", ((NZ, last, TILE), BF16), 0, [], 16, stay, before, across, after
    )
    got = exchange(summed, "z")
    shared = kernel_call(z_sum_kernel, "z_sum", ((NR, last, TILE), BF16), 0, [], 16, got)
    got = exchange(shared, REP)
    feature_grad, weight_grad, bias_grad = kernel_call(
        finish_kernel,
        "finish",
        [((ROW_TILES * TILE, WIDE), F32), ((WIDE, WIDE), F32), ((1, WIDE), F32)],
        0,
        [],
        16,
        got,
    )
    return (activations, feature_grad, weight_grad, bias_grad.reshape(WIDE))


def solution(mesh):
    fine = Mesh(mesh.devices.reshape(SIZES), AXES)
    return jax.shard_map(
        shards,
        mesh=fine,
        in_specs=(
            P(DOM, None),
            P(DOM, REP, None, None, None),
            P(DOM, REP, None),
            P(DOM, REP, None),
            P(DOM, REP),
            P(),
            P(),
            P(DOM, None),
        ),
        out_specs=(P(DOM, None), P(DOM, None), P(), P()),
        check_vma=False,
    )
```

time: 611 us -> 131 us (0.21)
  waiting for transfers between devices: 444 us -> 44.2 us
  blocking collectives: 96.3 us -> 30.8 us
  starting transfers between devices: 0.16 us -> 32.5 us
  local copies, waits for them, and re-layouts: 35.3 us -> 2.98 us
  Pallas kernels: 0 us -> 16.9 us
  matrix products: 15.9 us -> 0 us
  between operations: 14.5 us -> 1.39 us
    psum x2 -> x0, waiting for transfers between devices: 224 us -> none  [the longest x1 135 us: shards(): weight_grad, bias_grad = lax.psum((local_weight, local_bias), 'dom')]
    reduce_scatter x1 -> x0, waiting for transfers between devices: 144 us -> none  [shards(): shares = lax.psum_scatter(summed, 'dom', scatter_dimension=0, tiled=True)]
    psum x2 -> x0, blocking collectives: 96.3 us -> none  [the longest x1 54.3 us: shards(): weight_grad, bias_grad = lax.psum((local_weight, local_bias), 'dom')]
    all_gather x1 -> x0, waiting for transfers between devices: 75.2 us -> none  [shards(): everyone = lax.all_gather(features, 'dom', axis=0, tiled=True)]
    all_to_all x0 -> x2, blocking collectives: none -> 30.8 us  [exchange(): return lax.all_to_all(value, axes, 0, 0, tiled=True)]
    ppermute x0 -> x19, waiting for transfers between devices: none -> 28.5 us  [the longest x3 10.6 us: along_y(): return lax.ppermute(value, ('yl', 'yh'), pairs)]
    dot_general x4 -> x0, local copies, waits for them, and re-layouts: 24.8 us -> none  [the longest x1 20.2 us: shards(): jnp.einsum('cs,skf->ckf', picking, slot_terms, precision=lax.Precision.HI...]
    ppermute x0 -> x19, starting transfers between devices: none -> 22.9 us  [the longest x10 13.3 us: rotate(): return lax.ppermute(value, 'x', [(k, (k + step) % NX) for k in range(NX)])]
  transfers between devices with their start and end apart: 4 -> 20, of which waited for: 4 -> 14; matrix products, arithmetic and copies ran while one was open for 0% -> 1% of each run, Pallas kernels for 0% -> 1%
where the time goes in v2:
time: 131 us; the launch traced here: 130 us
  waiting for transfers between devices  44.2 us (34%)
  starting transfers between devices  32.5 us (25%)
  blocking collectives  30.8 us (24%)
  Pallas kernels  16.9 us (13%)
  local copies, waits for them, and re-layouts  2.98 us (2%)
  between operations  1.39 us (1%)
    all_to_all x2, blocking collectives, exchange(): return lax.all_to_all(value, axes, 0, 0, tiled=True)  30.8 us
    pallas_call x8, Pallas kernels, kernel_call(): pl.pallas_call(body, out_shape=[jax.ShapeDtypeStruct(s, d) for s, d in sh...  16.9 us
    all_to_all x1, waiting for transfers between devices, exchange(): return lax.all_to_all(value, axes, 0, 0, tiled=True)  15.7 us
    ppermute x10, starting transfers between devices, rotate(): return lax.ppermute(value, 'x', [(k, (k + step) % NX) for k in range(NX)])  13.3 us
    ppermute x3, waiting for transfers between devices, along_y(): return lax.ppermute(value, ('yl', 'yh'), pairs)  10.6 us
    all_to_all x1, starting transfers between devices, exchange(): return lax.all_to_all(value, axes, 0, 0, tiled=True)  9.58 us
    ppermute x10, waiting for transfers between devices, rotate(): return lax.ppermute(value, 'x', [(k, (k + step) % NX) for k in range(NX)])  9.45 us
    ppermute x6, waiting for transfers between devices, swap(): return lax.ppermute(value, axis, [(0, 1), (1, 0)])  8.47 us
  transfers between devices with their start and end apart: 20, of which 14 were waited for; matrix products, arithmetic and copies ran while one was open for 1% of the time, Pallas kernels for 1%

profile of v2, /device:TPU:2, one launch (start us, length us, event | category | flops | bytes accessed | tf_op | source)
XLA Modules:
  0.0 129.6 jit_solution(12661949428730200220)
XLA Ops:
  0.6 2.3 %collective-permute-start.1 = (bf16[32,128,128]{2,1,0:T(8,128)(2,1)}, bf16[32,128,128]{2,1,0:T(8,128)(2,1)S(1)}, u32[]{:S(2)}, u32[]{:S(2)}) collective-permute-start(bf16[32,128,128]{2,1,0:T(8,128)(2,1)} %bitcast.20), channel_id=1, source_target_pairs={{0,3},{1,0},{2,1},{3,2},{4,7},{5,4},{6,5},{7,6},{8,11},{9,8},{10,9... | collective-permute-start | bytes 3145736 | tf_op jit(solution)/shard_map/ppermute | solution.py:214
  3.6 0.7 bitcast_add_fusion.own_meta
  4.4 3.1 %collective-permute-start.4 = (s32[1,128]{1,0:T(1,128)S(1)}, s32[1,128]{1,0:T(1,128)S(1)}, u32[]{:S(2)}, u32[]{:S(2)}) collective-permute-start(s32[1,128]{1,0:T(1,128)S(1)} %bitcast_add_fusion.own_meta), channel_id=1, source_target_pairs={{0,2},{1,3},{2,0},{3,1},{4,6},{5,7},{6,4},{7,5},{8,10},{9,11},{10,... | collective-permute-start | bytes 1544 | tf_op jit(solution)/shard_map/ppermute | solution.py:214
  7.5 0.2 collective-permute-start.3
  7.7 1.8 %collective-permute-start.2 = (s32[1,128]{1,0:T(1,128)S(1)}, s32[1,128]{1,0:T(1,128)S(1)}, u32[]{:S(2)}, u32[]{:S(2)}) collective-permute-start(s32[1,128]{1,0:T(1,128)S(1)} %bitcast_add_fusion.own_meta), channel_id=1, source_target_pairs={{0,1},{1,2},{2,3},{3,0},{4,5},{5,6},{6,7},{7,4},{8,9},{9,10},{10,1... | collective-permute-start | bytes 1544 | tf_op jit(solution)/shard_map/ppermute | solution.py:214
  9.5 0.1 pad_add_fusion.ids
  9.6 0.9 copy-done.4
  10.6 0.8 prep.1
  11.4 1.0 copy-done.3
  12.3 9.6 %all-to-all-start = ((bf16[16,256,128]{2,1,0:T(8,128)(2,1)}), bf16[16,256,128]{2,1,0:T(8,128)(2,1)S(1)}, u32[]{:S(2)}, u32[]{:S(2)}) async-start(bf16[16,256,128]{2,1,0:T(8,128)(2,1)} %copy-done.3), calls=%async_computation | async-start | bytes 2097152 | tf_op jit(solution)/shard_map/all_to_all | solution.py:230
  21.9 4.8 %collective-permute-done.4.meta_f = s32[1,128]{1,0:T(1,128)S(1)} collective-permute-done((s32[1,128]{1,0:T(1,128)S(1)}, s32[1,128]{1,0:T(1,128)S(1)}, u32[]{:S(2)}, u32[]{:S(2)}) %collective-permute-start.4) | collective-permute-done | bytes 544 | tf_op jit(solution)/shard_map/ppermute | solution.py:214
  26.7 0.5 collective-permute-done.2.meta_l
  27.2 1.0 relay.1
  28.3 1.0 copy-done.1
  29.2 1.4 %collective-permute-start.5 = (bf16[16,128,128]{2,1,0:T(8,128)(2,1)}, bf16[16,128,128]{2,1,0:T(8,128)(2,1)}, u32[]{:S(2)}, u32[]{:S(2)}) collective-permute-start(bf16[16,128,128]{2,1,0:T(8,128)(2,1)} %get-tuple-element.18), channel_id=1, source_target_pairs={{0,1},{1,2},{2,3},{3,0},{4,5},{5,6},{6,7},{7,4},{8,9},{9,10},{10,1... | collective-permute-start | bytes 1572872 | tf_op jit(solution)/shard_map/ppermute | solution.py:214
  30.6 1.5 %collective-permute-start.6 = (bf16[16,128,128]{2,1,0:T(8,128)(2,1)}, bf16[16,128,128]{2,1,0:T(8,128)(2,1)}, u32[]{:S(2)}, u32[]{:S(2)}) collective-permute-start(bf16[16,128,128]{2,1,0:T(8,128)(2,1)} %get-tuple-element.19), channel_id=1, source_target_pairs={{0,3},{1,0},{2,1},{3,2},{4,7},{5,4},{6,5},{7,6},{8,11},{9,8},{10,9... | collective-permute-start | bytes 1572872 | tf_op jit(solution)/shard_map/ppermute | solution.py:214
  32.2 15.7 %all-to-all-done = bf16[16,256,128]{2,1,0:T(8,128)(2,1)S(1)} async-done(((bf16[16,256,128]{2,1,0:T(8,128)(2,1)}), bf16[16,256,128]{2,1,0:T(8,128)(2,1)S(1)}, u32[]{:S(2)}, u32[]{:S(2)}) %all-to-all-start) | async-done | bytes 1048608 | tf_op jit(solution)/shard_map/all_to_all | solution.py:230
  47.8 0.1 fusion
  47.9 0.1 collective-permute-start.9
  48.0 0.5 collective-permute-start.10
  48.5 0.1 collective-permute-start.8
  48.6 0.4 collective-permute-start.7
  49.0 0.5 collective-permute-done.9.rest_2_
  49.5 0.4 collective-permute-done.10.rest_3_
  49.9 0.4 collective-permute-done.8.rest_1_
  50.3 0.4 collective-permute-done.7.rest_0_
  50.7 0.0 copy-start.7
  50.7 5.8 %forward.1 = f32[8,32,128]{2,1,0:T(8,128)S(1)} custom-call(s32[4]{0:T(128)S(1)} %pad_add_fusion.ids, s32[512]{0:T(512)S(1)} %bitcast.24, bf16[32,128,128]{2,1,0:T(8,128)(2,1)S(1)} %bitcast.22, bf16[32,128,128]{2,1,0:T(8,128)(2,1)S(1)} %copy-done.2, bf16[32,128,128]{2,1,0:T(8,128)(2,1)S(1)} %collective-permute-done.1.right, ...), custom_call_target="tpu_custom_call" | custom-call | tf_op jit(solution)/shard_map/forward/pallas_call | solution.py:236
  56.5 3.0 %collective-permute-start.11 = (f32[8,32,128]{2,1,0:T(8,128)S(1)}, f32[8,32,128]{2,1,0:T(8,128)S(1)}, u32[]{:S(2)}, u32[]{:S(2)}) collective-permute-start(f32[8,32,128]{2,1,0:T(8,128)S(1)} %forward.1), channel_id=1, source_target_pairs={{0,4},{4,0},{1,5},{5,1},{2,6},{6,2},{3,7},{7,3},{8,12},{12,8},{9,1... | collective-permute-start | bytes 393224 | tf_op jit(solution)/shard_map/ppermute | solution.py:226
  59.4 4.1 %collective-permute-done.11 = f32[8,32,128]{2,1,0:T(8,128)S(1)} collective-permute-done((f32[8,32,128]{2,1,0:T(8,128)S(1)}, f32[8,32,128]{2,1,0:T(8,128)S(1)}, u32[]{:S(2)}, u32[]{:S(2)}) %collective-permute-start.11) | collective-permute-done | bytes 131104 | tf_op jit(solution)/shard_map/ppermute | solution.py:226
  63.6 0.8 collective-permute-start.14
  64.4 0.6 collective-permute-start.13
  65.0 1.4 %collective-permute-start.12 = (bf16[8,32,128]{2,1,0:T(8,128)(2,1)S(1)}, bf16[8,32,128]{2,1,0:T(8,128)(2,1)S(1)}, u32[]{:S(2)}, u32[]{:S(2)}) collective-permute-start(bf16[8,32,128]{2,1,0:T(8,128)(2,1)S(1)} %add_convert_fusion.agg), channel_id=1, source_target_pairs={{0,1},{1,2},{2,3},{3,0},{4,5},{5,6},{6,7},{7,4},{8,9},{9,10},{10,1... | collective-permute-start | bytes 196616 | tf_op jit(solution)/shard_map/ppermute | solution.py:214
  66.5 3.0 %collective-permute-done.14.agg_f = bf16[8,32,128]{2,1,0:T(8,128)(2,1)S(1)} collective-permute-done((bf16[8,32,128]{2,1,0:T(8,128)(2,1)S(1)}, bf16[8,32,128]{2,1,0:T(8,128)(2,1)S(1)}, u32[]{:S(2)}, u32[]{:S(2)}) %collective-permute-start.14) | collective-permute-done | bytes 65568 | tf_op jit(solution)/shard_map/ppermute | solution.py:214
  69.5 1.2 collective-permute-done.12.agg_l
  70.6 7.9 %backward.1 = (bf16[1024,128]{1,0:T(8,128)(2,1)}, bf16[4,1056,128]{2,1,0:T(8,128)(2,1)S(1)}, bf16[4,1056,128]{2,1,0:T(8,128)(2,1)S(1)}) custom-call(s32[4]{0:T(128)S(1)} %pad_add_fusion.ids, s32[512]{0:T(512)S(1)} %bitcast.25, bf16[32,128,128]{2,1,0:T(8,128)(2,1)S(1)} %bitcast.23, bf16[32,128,128]{2,1,0:T(8,128)(2,1)S(1)} %copy-done.2, ...), custom_call_target="tpu_custom_call" | custom-call | tf_op jit(solution)/shard_map/backward/pallas_call | solution.py:236
  78.5 2.7 %collective-permute-done.15.got = bf16[4,1056,128]{2,1,0:T(8,128)(2,1)S(1)} collective-permute-done((bf16[4,1056,128]{2,1,0:T(8,128)(2,1)S(1)}, bf16[4,1056,128]{2,1,0:T(8,128)(2,1)S(1)}, u32[]{:S(2)}, u32[]{:S(2)}) %collective-permute-start.15) | collective-permute-done | bytes 1081376 | tf_op jit(solution)/shard_map/ppermute | solution.py:226
  81.2 0.2 pair.1
  81.4 0.4 collective-permute-start.16
  81.8 2.9 %collective-permute-start.17 = (bf16[1056,128]{1,0:T(8,128)(2,1)S(1)}, bf16[1056,128]{1,0:T(8,128)(2,1)S(1)}, u32[]{:S(2)}, u32[]{:S(2)}) collective-permute-start(bf16[1056,128]{1,0:T(8,128)(2,1)S(1)} %get-tuple-element.25), channel_id=1, source_target_pairs={{0,4},{128,132},{4,0},{132,128},{1,5},{129,133},{5,1},{133,129},{2... | collective-permute-start | bytes 811016 | tf_op jit(solution)/shard_map/ppermute | solution.py:222
  84.7 2.3 %collective-permute-start.18 = (bf16[1056,128]{1,0:T(8,128)(2,1)S(1)}, bf16[1056,128]{1,0:T(8,128)(2,1)S(1)}, u32[]{:S(2)}, u32[]{:S(2)}) collective-permute-start(bf16[1056,128]{1,0:T(8,128)(2,1)S(1)} %get-tuple-element.26), channel_id=1, source_target_pairs={{0,132},{128,0},{4,128},{132,4},{1,133},{129,1},{5,129},{133,5},{2... | collective-permute-start | bytes 811016 | tf_op jit(solution)/shard_map/ppermute | solution.py:222
  87.0 5.0 %collective-permute-done.16.before = bf16[1056,128]{1,0:T(8,128)(2,1)S(1)} collective-permute-done((bf16[1056,128]{1,0:T(8,128)(2,1)S(1)}, bf16[1056,128]{1,0:T(8,128)(2,1)S(1)}, u32[]{:S(2)}, u32[]{:S(2)}) %collective-permute-start.16) | collective-permute-done | bytes 270368 | tf_op jit(solution)/shard_map/ppermute | solution.py:222
  92.1 5.0 %collective-permute-done.17.across = bf16[1056,128]{1,0:T(8,128)(2,1)S(1)} collective-permute-done((bf16[1056,128]{1,0:T(8,128)(2,1)S(1)}, bf16[1056,128]{1,0:T(8,128)(2,1)S(1)}, u32[]{:S(2)}, u32[]{:S(2)}) %collective-permute-start.17) | collective-permute-done | bytes 270368 | tf_op jit(solution)/shard_map/ppermute | solution.py:222
  97.0 0.6 collective-permute-done.18.after
  97.7 0.1 y_sum.1
  97.8 16.3 %all_to_all.15.got = bf16[8,160,128]{2,1,0:T(8,128)(2,1)S(1)} all-to-all(bf16[8,160,128]{2,1,0:T(8,128)(2,1)S(1)} %y_sum.1), channel_id=1, replica_groups=mesh['yl'=2,'z'=8,'c'=2,'yh'=2,'x'=4] {'z'}, dimensions={0} | all-to-all | bytes 655360 | tf_op jit(solution)/shard_map/all_to_all | solution.py:230
  114.1 14.6 %all_to_all.16.got = bf16[8,160,128]{2,1,0:T(8,128)(2,1)S(1)} all-to-all(bf16[8,160,128]{2,1,0:T(8,128)(2,1)S(1)} %z_sum.1), channel_id=1, replica_groups=mesh['yl'=2,'z'=8,'c'=2,'yh'=2,'x'=4] {'yh','x'}, dimensions={0} | all-to-all | bytes 655360 | tf_op jit(solution)/shard_map/all_to_all | solution.py:230
  128.7 0.9 finish.1
  (23 shorter events, 0.1 us)
Async XLA Ops:
  0.6 26.6 %collective-permute-start.1 = (bf16[32,128,128]{2,1,0:T(8,128)(2,1)}, bf16[32,128,128]{2,1,0:T(8,128)(2,1)S(1)}, u32[]{:S(2)}, u32[]{:S(2)}) collective-permute-start(bf16[32,128,128]{2,1,0:T(8,128)(2,1)} %bitcast.20), channel_id=1, source_target_pairs={{0,3},{1,0},{2,1},{3,2},{4,7},{5,4},{6,5},{7,6},{8,11},{9,8},{10,9... | collective-permute-start | bytes 3145736 | tf_op jit(solution)/shard_map/ppermute | solution.py:214
  3.0 24.2 %collective-permute-start = (bf16[32,128,128]{2,1,0:T(8,128)(2,1)}, bf16[32,128,128]{2,1,0:T(8,128)(2,1)S(1)}, u32[]{:S(2)}, u32[]{:S(2)}) collective-permute-start(bf16[32,128,128]{2,1,0:T(8,128)(2,1)} %bitcast.21), channel_id=1, source_target_pairs={{0,1},{1,2},{2,3},{3,0},{4,5},{5,6},{6,7},{7,4},{8,9},{9,10},{10,1... | collective-permute-start | bytes 3145736 | tf_op jit(solution)/shard_map/ppermute | solution.py:214
  4.4 22.3 %collective-permute-start.4 = (s32[1,128]{1,0:T(1,128)S(1)}, s32[1,128]{1,0:T(1,128)S(1)}, u32[]{:S(2)}, u32[]{:S(2)}) collective-permute-start(s32[1,128]{1,0:T(1,128)S(1)} %bitcast_add_fusion.own_meta), channel_id=1, source_target_pairs={{0,2},{1,3},{2,0},{3,1},{4,6},{5,7},{6,4},{7,5},{8,10},{9,11},{10,... | collective-permute-start | bytes 1544 | tf_op jit(solution)/shard_map/ppermute | solution.py:214
  7.5 19.2 %collective-permute-start.3 = (s32[1,128]{1,0:T(1,128)S(1)}, s32[1,128]{1,0:T(1,128)S(1)}, u32[]{:S(2)}, u32[]{:S(2)}) collective-permute-start(s32[1,128]{1,0:T(1,128)S(1)} %bitcast_add_fusion.own_meta), channel_id=1, source_target_pairs={{0,3},{1,0},{2,1},{3,2},{4,7},{5,4},{6,5},{7,6},{8,11},{9,8},{10,9... | collective-permute-start | bytes 1544 | tf_op jit(solution)/shard_map/ppermute | solution.py:214
  7.7 19.5 %collective-permute-start.2 = (s32[1,128]{1,0:T(1,128)S(1)}, s32[1,128]{1,0:T(1,128)S(1)}, u32[]{:S(2)}, u32[]{:S(2)}) collective-permute-start(s32[1,128]{1,0:T(1,128)S(1)} %bitcast_add_fusion.own_meta), channel_id=1, source_target_pairs={{0,1},{1,2},{2,3},{3,0},{4,5},{5,6},{6,7},{7,4},{8,9},{9,10},{10,1... | collective-permute-start | bytes 1544 | tf_op jit(solution)/shard_map/ppermute | solution.py:214
  9.6 1.0 copy-start.4
  11.4 1.0 copy-start.3
  12.3 35.5 %all-to-all-start = ((bf16[16,256,128]{2,1,0:T(8,128)(2,1)}), bf16[16,256,128]{2,1,0:T(8,128)(2,1)S(1)}, u32[]{:S(2)}, u32[]{:S(2)}) async-start(bf16[16,256,128]{2,1,0:T(8,128)(2,1)} %copy-done.3), calls=%async_computation | async-start | bytes 2097152 | tf_op jit(solution)/shard_map/all_to_all | solution.py:230
  28.3 1.0 copy-start.1
  29.2 21.4 %copy-start = (bf16[1,1,32,128,128]{4,3,2,1,0:T(8,128)(2,1)S(1)}, bf16[1,1,32,128,128]{4,3,2,1,0:T(8,128)(2,1)}, u32[]{:S(2)}) copy-start(bf16[1,1,32,128,128]{4,3,2,1,0:T(8,128)(2,1)} %param.9) | copy-start | bytes 3145732
  29.2 19.4 %collective-permute-start.5 = (bf16[16,128,128]{2,1,0:T(8,128)(2,1)}, bf16[16,128,128]{2,1,0:T(8,128)(2,1)}, u32[]{:S(2)}, u32[]{:S(2)}) collective-permute-start(bf16[16,128,128]{2,1,0:T(8,128)(2,1)} %get-tuple-element.18), channel_id=1, source_target_pairs={{0,1},{1,2},{2,3},{3,0},{4,5},{5,6},{6,7},{7,4},{8,9},{9,10},{10,1... | collective-permute-start | bytes 1572872 | tf_op jit(solution)/shard_map/ppermute | solution.py:214
  30.6 18.4 %collective-permute-start.6 = (bf16[16,128,128]{2,1,0:T(8,128)(2,1)}, bf16[16,128,128]{2,1,0:T(8,128)(2,1)}, u32[]{:S(2)}, u32[]{:S(2)}) collective-permute-start(bf16[16,128,128]{2,1,0:T(8,128)(2,1)} %get-tuple-element.19), channel_id=1, source_target_pairs={{0,3},{1,0},{2,1},{3,2},{4,7},{5,4},{6,5},{7,6},{8,11},{9,8},{10,9... | collective-permute-start | bytes 1572872 | tf_op jit(solution)/shard_map/ppermute | solution.py:214
  47.8 2.8 %copy-start.2 = (bf16[32,128,128]{2,1,0:T(8,128)(2,1)S(1)}, bf16[32,128,128]{2,1,0:T(8,128)(2,1)}, u32[]{:S(2)}) copy-start(bf16[32,128,128]{2,1,0:T(8,128)(2,1)} %copy-done.1) | copy-start | bytes 3145732
  47.9 1.6 %collective-permute-start.9 = (bf16[32,32,128]{2,1,0:T(8,128)(2,1)S(1)}, bf16[32,32,128]{2,1,0:T(8,128)(2,1)S(1)}, u32[]{:S(2)}, u32[]{:S(2)}) collective-permute-start(bf16[32,32,128]{2,1,0:T(8,128)(2,1)S(1)} %bitcast.30), channel_id=1, source_target_pairs={{0,8},{8,0},{1,9},{9,1},{2,10},{10,2},{3,11},{11,3},{4,12},{12,4},... | collective-permute-start | bytes 786440 | tf_op jit(solution)/shard_map/ppermute | solution.py:226
  48.0 1.9 %collective-permute-start.10 = (bf16[32,32,128]{2,1,0:T(8,128)(2,1)S(1)}, bf16[32,32,128]{2,1,0:T(8,128)(2,1)S(1)}, u32[]{:S(2)}, u32[]{:S(2)}) collective-permute-start(bf16[32,32,128]{2,1,0:T(8,128)(2,1)S(1)} %bitcast.29), channel_id=1, source_target_pairs={{0,8},{8,0},{1,9},{9,1},{2,10},{10,2},{3,11},{11,3},{4,12},{12,4},... | collective-permute-start | bytes 786440 | tf_op jit(solution)/shard_map/ppermute | solution.py:226
  48.5 1.8 %collective-permute-start.8 = (bf16[32,32,128]{2,1,0:T(8,128)(2,1)S(1)}, bf16[32,32,128]{2,1,0:T(8,128)(2,1)S(1)}, u32[]{:S(2)}, u32[]{:S(2)}) collective-permute-start(bf16[32,32,128]{2,1,0:T(8,128)(2,1)S(1)} %bitcast.28), channel_id=1, source_target_pairs={{0,8},{8,0},{1,9},{9,1},{2,10},{10,2},{3,11},{11,3},{4,12},{12,4},... | collective-permute-start | bytes 786440 | tf_op jit(solution)/shard_map/ppermute | solution.py:226
  48.6 2.0 %collective-permute-start.7 = (bf16[32,32,128]{2,1,0:T(8,128)(2,1)S(1)}, bf16[32,32,128]{2,1,0:T(8,128)(2,1)S(1)}, u32[]{:S(2)}, u32[]{:S(2)}) collective-permute-start(bf16[32,32,128]{2,1,0:T(8,128)(2,1)S(1)} %bitcast.27), channel_id=1, source_target_pairs={{0,8},{8,0},{1,9},{9,1},{2,10},{10,2},{3,11},{11,3},{4,12},{12,4},... | collective-permute-start | bytes 786440 | tf_op jit(solution)/shard_map/ppermute | solution.py:226
  50.6 20.0 %copy-start.5 = (bf16[1024,128]{1,0:T(8,128)(2,1)S(1)}, bf16[1024,128]{1,0:T(8,128)(2,1)}, u32[]{:S(2)}) copy-start(bf16[1024,128]{1,0:T(8,128)(2,1)} %cot.1) | copy-start | bytes 786436
  50.6 20.0 %copy-start.6 = (bf16[128,128]{1,0:T(8,128)(2,1)S(1)}, bf16[128,128]{1,0:T(8,128)(2,1)}, u32[]{:S(2)}) copy-start(bf16[128,128]{1,0:T(8,128)(2,1)} %weight.1) | copy-start | bytes 98308
  50.7 20.0 %copy-start.7 = (f32[128]{0:T(128)S(1)}, f32[128]{0:T(128)}, u32[]{:S(2)}) copy-start(f32[128]{0:T(128)} %param.14) | copy-start | bytes 1540
  56.5 7.1 %collective-permute-start.11 = (f32[8,32,128]{2,1,0:T(8,128)S(1)}, f32[8,32,128]{2,1,0:T(8,128)S(1)}, u32[]{:S(2)}, u32[]{:S(2)}) collective-permute-start(f32[8,32,128]{2,1,0:T(8,128)S(1)} %forward.1), channel_id=1, source_target_pairs={{0,4},{4,0},{1,5},{5,1},{2,6},{6,2},{3,7},{7,3},{8,12},{12,8},{9,1... | collective-permute-start | bytes 393224 | tf_op jit(solution)/shard_map/ppermute | solution.py:226
  63.6 5.9 %collective-permute-start.14 = (bf16[8,32,128]{2,1,0:T(8,128)(2,1)S(1)}, bf16[8,32,128]{2,1,0:T(8,128)(2,1)S(1)}, u32[]{:S(2)}, u32[]{:S(2)}) collective-permute-start(bf16[8,32,128]{2,1,0:T(8,128)(2,1)S(1)} %add_convert_fusion.agg), channel_id=1, source_target_pairs={{0,2},{1,3},{2,0},{3,1},{4,6},{5,7},{6,4},{7,5},{8,10},{9,11},{10,... | collective-permute-start | bytes 196616 | tf_op jit(solution)/shard_map/ppermute | solution.py:214
  64.4 5.0 %collective-permute-start.13 = (bf16[8,32,128]{2,1,0:T(8,128)(2,1)S(1)}, bf16[8,32,128]{2,1,0:T(8,128)(2,1)S(1)}, u32[]{:S(2)}, u32[]{:S(2)}) collective-permute-start(bf16[8,32,128]{2,1,0:T(8,128)(2,1)S(1)} %add_convert_fusion.agg), channel_id=1, source_target_pairs={{0,3},{1,0},{2,1},{3,2},{4,7},{5,4},{6,5},{7,6},{8,11},{9,8},{10,9... | collective-permute-start | bytes 196616 | tf_op jit(solution)/shard_map/ppermute | solution.py:214
  65.0 5.6 %collective-permute-start.12 = (bf16[8,32,128]{2,1,0:T(8,128)(2,1)S(1)}, bf16[8,32,128]{2,1,0:T(8,128)(2,1)S(1)}, u32[]{:S(2)}, u32[]{:S(2)}) collective-permute-start(bf16[8,32,128]{2,1,0:T(8,128)(2,1)S(1)} %add_convert_fusion.agg), channel_id=1, source_target_pairs={{0,1},{1,2},{2,3},{3,0},{4,5},{5,6},{6,7},{7,4},{8,9},{9,10},{10,1... | collective-permute-start | bytes 196616 | tf_op jit(solution)/shard_map/ppermute | solution.py:214
  78.5 2.7 %collective-permute-start.15 = (bf16[4,1056,128]{2,1,0:T(8,128)(2,1)S(1)}, bf16[4,1056,128]{2,1,0:T(8,128)(2,1)S(1)}, u32[]{:S(2)}, u32[]{:S(2)}) collective-permute-start(bf16[4,1056,128]{2,1,0:T(8,128)(2,1)S(1)} %get-tuple-element.22), channel_id=1, source_target_pairs={{0,8},{8,0},{1,9},{9,1},{2,10},{10,2},{3,11},{11,3},{4,12},{12,4},... | collective-permute-start | bytes 3244040 | tf_op jit(solution)/shard_map/ppermute | solution.py:226
  81.4 10.6 %collective-permute-start.16 = (bf16[1056,128]{1,0:T(8,128)(2,1)S(1)}, bf16[1056,128]{1,0:T(8,128)(2,1)S(1)}, u32[]{:S(2)}, u32[]{:S(2)}) collective-permute-start(bf16[1056,128]{1,0:T(8,128)(2,1)S(1)} %get-tuple-element.24), channel_id=1, source_target_pairs={{0,128},{128,4},{4,132},{132,0},{1,129},{129,5},{5,133},{133,1},{2... | collective-permute-start | bytes 811016 | tf_op jit(solution)/shard_map/ppermute | solution.py:222
  81.8 15.2 %collective-permute-start.17 = (bf16[1056,128]{1,0:T(8,128)(2,1)S(1)}, bf16[1056,128]{1,0:T(8,128)(2,1)S(1)}, u32[]{:S(2)}, u32[]{:S(2)}) collective-permute-start(bf16[1056,128]{1,0:T(8,128)(2,1)S(1)} %get-tuple-element.25), channel_id=1, source_target_pairs={{0,4},{128,132},{4,0},{132,128},{1,5},{129,133},{5,1},{133,129},{2... | collective-permute-start | bytes 811016 | tf_op jit(solution)/shard_map/ppermute | solution.py:222
  84.7 12.9 %collective-permute-start.18 = (bf16[1056,128]{1,0:T(8,128)(2,1)S(1)}, bf16[1056,128]{1,0:T(8,128)(2,1)S(1)}, u32[]{:S(2)}, u32[]{:S(2)}) collective-permute-start(bf16[1056,128]{1,0:T(8,128)(2,1)S(1)} %get-tuple-element.26), channel_id=1, source_target_pairs={{0,132},{128,0},{4,128},{132,4},{1,133},{129,1},{5,129},{133,5},{2... | collective-permute-start | bytes 811016 | tf_op jit(solution)/shard_map/ppermute | solution.py:222

commit v3 on v2

--- a/solution.py
+++ b/solution.py
@@ -27,10 +27,10 @@
 LAST = BLOCK_HALF * THIN
 GRADS = THIN // 2
 EXTRA = 32
-SWAPS = 4
+SWAPS = 2
 PIECE = NZ * LAST
-META = 128
-RELAY_COST = pl.CostEstimate(flops=20 * 10**9, bytes_accessed=60 * 10**6, transcendentals=0)
+META = 4 * SLOTS
+RELAY_COST = pl.CostEstimate(flops=14 * 10**9, bytes_accessed=42 * 10**6, transcendentals=0)
 UNROLL = 16
 
 F32 = jnp.float32
@@ -55,55 +55,46 @@
             out[p, t * THIN : (t + 1) * THIN, :] = part
 
 
-def each_group(tile_refs, work):
-    for ref, source, skip in tile_refs:
-        lax.fori_loop(
-            0, ref.shape[0] // UNROLL, lambda g, _, a=ref, b=source, c=skip: work(a, b, c, g), 0
-        )
-
-
-def relay_kernel(left, right, own_meta, meta_l, meta_r, meta_f, out_a, out_b, meta):
+def every_slot(tile_refs, work):
+    for ref, meta, skip in tile_refs:
+        prods = [work(ref[s], meta, skip + s) for s in range(ref.shape[0])]
+        for target, index, prod in prods:
+            target[index] += prod
+
+
+def relay_kernel(left, right, meta_l, meta_r, meta_f, out_a, out_b, out_l, out_r, out_f):
     out_a[...] = left[0:HALF]
     out_b[...] = right[HALF:SLOTS]
-    for k, part in enumerate((own_meta, meta_l, meta_r, meta_f)):
-        meta[k : k + 1, :] = part[...]
-
-
-def forward_kernel(ids, meta, own, left, right, far_a, far_b, mine, *rest):
-    others, out = rest[:SWAPS], rest[SWAPS]
-    out[...] = jnp.zeros_like(out)
-    my_core = ids[1]
-    per = NP * ROW_TILES // SWAPS
-
-    def work(tiles, source, skip, g):
-        at = source * META
-        rows, prods = [], []
-        for u in range(UNROLL):
-            s = g * UNROLL + u
-            row = meta[at + skip + s]
-            col = meta[at + SLOTS + skip + s]
-            live = skip + s < meta[at + 2 * SLOTS]
-            owner = col // ROW_TILES
-            place = (owner // 2) * ROW_TILES + col % ROW_TILES
-            src, inner = mine[place], place % per
-            for k, other in enumerate(others):
-                here = (owner % 2 != my_core) & (place // per == k)
-                src = jnp.where(here, other[inner], src)
-            src = jnp.where(live, src, jnp.zeros_like(src))
-            prods.append(mul(src, tiles[s], CONTRACT_LAST))
-            rows.append(row)
-        for row, prod in zip(rows, prods):
-            out[row] += prod
-        return 0
-
-    each_group([(own, 0, 0), (left, 1, 0), (right, 2, 0), (far_a, 3, 0), (far_b, 3, HALF)], work)
+    out_l[...] = meta_l[...]
+    out_r[...] = meta_r[...]
+    out_f[...] = meta_f[...]
+
+
+def forward_kernel(meta, meta_l, meta_r, meta_f, own, left, right, far_a, far_b, mine, *rest):
+    others, (out, table, acc) = rest[:SWAPS], rest[SWAPS:]
+    acc[...] = jnp.zeros_like(acc)
+    half = NP * ROW_TILES
+    table[0:half] = mine[...]
+    for k, other in enumerate(others):
+        per = half // SWAPS
+        table[half + k * per : half + (k + 1) * per] = other[...]
+    table[2 * half] = jnp.zeros((THIN, TILE), BF16)
+
+    def work(tile, meta, s):
+        return acc, meta[s], mul(tile, table[meta[SLOTS + s]], CONTRACT_LAST)
+
+    groups = [(own, meta, 0), (left, meta_l, 0), (right, meta_r, 0), (far_a, meta_f, 0)]
+    every_slot(groups + [(far_b, meta_f, HALF)], work)
+    for t in range(ROW_TILES):
+        out[t] = acc[t].T
 
 
 def backward_kernel(
-    ids, meta, own, left, right, far_a, far_b, agg, agg_l, agg_r, agg_f, weight, bias, cot,
-    act, keep, send, acc, back, full, slopes, wsum,
+    ids, meta, meta_l, meta_r, meta_f, own, left, right, far_a, far_b, agg, agg_l, agg_r, agg_f, weight, bias, cot,
+    act, keep, *rest,
 ):
-    x, my_core, yl, yh = ids[0], ids[1], ids[2], ids[3]
+    send, acc, back, full, slopes, wsum = rest
+    x, yl, yh = ids[0], ids[2], ids[3]
     acc[...] = jnp.zeros_like(acc)
     for t in range(ROW_TILES):
         for k, part in ((0, agg), (1, agg_l), (3, agg_r), (2, agg_f)):
@@ -142,27 +133,13 @@
         keep[k, PIECE:, :] = extra
         send[k, PIECE:, :] = extra
 
-    def work(tiles, source, skip, g):
-        at = source * META
-        places, prods = [], []
-        for u in range(UNROLL):
-            s = g * UNROLL + u
-            row = meta[at + skip + s]
-            col = meta[at + SLOTS + skip + s]
-            live = skip + s < meta[at + 2 * SLOTS]
-            owner, block = col // ROW_TILES, col % ROW_TILES
-            core, z, to_yl = owner % 2, (owner // 2) % NZ, owner // (2 * NZ)
-            k = ((block // BLOCK_HALF) * 2 + to_yl - y + NY) % NY
-            place = jnp.where(core == my_core, 0, NY) + k
-            place = (place * NZ + z) * BLOCK_HALF + block % BLOCK_HALF
-            src = jnp.where(live, back[row], jnp.zeros((THIN, TILE), BF16))
-            prods.append(mul(src, tiles[s], PLAIN))
-            places.append(place)
-        for place, prod in zip(places, prods):
-            acc[place] += prod
-        return 0
-
-    each_group([(own, 0, 0), (left, 1, 0), (right, 2, 0), (far_a, 3, 0), (far_b, 3, HALF)], work)
+    back[ROW_TILES] = jnp.zeros((THIN, TILE), BF16)
+
+    def work(tile, meta, s):
+        return acc, meta[3 * SLOTS + s], mul(back[meta[2 * SLOTS + s]], tile, PLAIN)
+
+    groups = [(own, meta, 0), (left, meta_l, 0), (right, meta_r, 0), (far_a, meta_f, 0)]
+    every_slot(groups + [(far_b, meta_f, HALF)], work)
     per = NZ * BLOCK_HALF
     for k in range(NY):
         for i in range(per):
@@ -208,6 +185,25 @@
             to = x * THIN + yh * GRADS
             wgrad[to : to + GRADS, :] = got[yh * NX + x, LAST : LAST + GRADS, :].astype(F32)
     bgrad[...] = got[0, LAST + GRADS : LAST + EXTRA, :].astype(F32)[0:1, :]
+
+
+def slot_meta(rows, cols, count, core, y):
+    live = lax.broadcasted_iota(jnp.int32, rows.shape, 1) < count
+    owner, block = cols // ROW_TILES, cols % ROW_TILES
+    apart = jnp.where(owner % 2 == core, 0, 1)
+    peer = owner // 2
+    source = (apart * NP + peer) * ROW_TILES + block
+    step = ((block // BLOCK_HALF) * 2 + peer // NZ - y + NY) % NY
+    target = ((apart * NY + step) * NZ + peer % NZ) * BLOCK_HALF + block % BLOCK_HALF
+    return jnp.concatenate(
+        [
+            rows,
+            jnp.where(live, source, 2 * NP * ROW_TILES),
+            jnp.where(live, rows, ROW_TILES),
+            target,
+        ],
+        axis=1,
+    )
 
 
 def rotate(value, step):
@@ -256,37 +252,40 @@
     own = tile_values[0, 0]
     left = rotate(own, 1)
     right = rotate(own, NX - 1)
-    count = jnp.broadcast_to(tile_count, (1, META - 2 * SLOTS))
-    own_meta = jnp.concatenate([tile_rows[0], tile_cols[0], count], axis=1)
+    own_meta = slot_meta(tile_rows[0], tile_cols[0], tile_count, core, yh * 2 + yl)
     half = ((HALF, TILE, TILE), BF16)
-    pass_a, pass_b, meta = kernel_call(
+    line = ((1, META), jnp.int32)
+    pass_a, pass_b, *metas = kernel_call(
         relay_kernel,
         "relay",
-        [half, half, ((NX, META), jnp.int32)],
+        [half, half, line, line, line],
         0,
         [],
-        16,
+        6,
         left,
         right,
-        own_meta,
         rotate(own_meta, 1),
         rotate(own_meta, NX - 1),
         rotate(own_meta, 2),
         cost=RELAY_COST,
     )
-    meta = meta.reshape(NX * META)
+    metas = [m.reshape(META) for m in (own_meta, *metas)]
     far_a, far_b = rotate(pass_a, 1), rotate(pass_b, NX - 1)
     tiles = (own, left, right, far_a, far_b)
 
-    copies = kernel_call(prep_kernel, "prep", ((NP, MAIN, TILE), BF16), 1, [], 16, ids, features)
+    copies = kernel_call(prep_kernel, "prep", ((NP, MAIN, TILE), BF16), 1, [], 6, ids, features)
     mine = exchange(copies, PEERS)
     mine = mine.reshape(NP * ROW_TILES, THIN, TILE)
     per = NP * ROW_TILES // SWAPS
     others = [swap(mine[k * per : (k + 1) * per], "c") for k in range(SWAPS)]
 
     thin = (ROW_TILES, THIN, TILE)
+    scratch = [
+        pltpu.VMEM((2 * NP * ROW_TILES + 1, THIN, TILE), BF16),
+        pltpu.VMEM((ROW_TILES, TILE, THIN), F32),
+    ]
     part = kernel_call(
-        forward_kernel, "forward", (thin, F32), 2, [], 40, ids, meta, *tiles, mine, *others
+        forward_kernel, "forward", (thin, F32), 4, scratch, 16, *metas, *tiles, mine, *others
     )
     agg = (part + swap(part, "yh")).astype(BF16)
     agg_l, agg_r, agg_f = rotate(agg, 1), rotate(agg, NX - 1), rotate(agg, 2)
@@ -297,17 +296,17 @@
         backward_kernel,
         "backward",
         [((ROW_TILES * TILE, WIDE), BF16), ((NY, piece, TILE), BF16), ((NY, piece, TILE), BF16)],
-        2,
+        5,
         [
             pltpu.VMEM((2 * NY * NZ * BLOCK_HALF, THIN, TILE), F32),
-            pltpu.VMEM(thin, BF16),
+            pltpu.VMEM((ROW_TILES + 1, THIN, TILE), BF16),
             pltpu.VMEM(square, BF16),
             pltpu.VMEM(square, BF16),
             pltpu.VMEM((THIN, WIDE), F32),
         ],
-        40,
+        20,
         ids,
-        meta,
+        *metas,
         *tiles,
         agg,
         agg_l,
@@ -319,12 +318,12 @@
     )
     got = swap(send, "c")
     stay, one, two, three = kernel_call(
-        pair_kernel, "pair", [((piece, TILE), BF16)] * NY, 0, [], 16, keep, got
+        pair_kernel, "pair", [((piece, TILE), BF16)] * NY, 0, [], 12, keep, got
     )
     before, across, after = along_y(one, 1), along_y(two, 2), along_y(three, 3)
     last = LAST + EXTRA
     summed = kernel_call(
-        y_sum_kernel, "y_sum", ((NZ, last, TILE), BF16), 0, [], 16, stay, before, across, after
+        y_sum_kernel, "y_sum", ((NZ, last, TILE), BF16), 0, [], 12, stay, before, across, after
     )
     got = exchange(summed, "z")
     shared = kernel_call(z_sum_kernel, "z_sum", ((NR, last, TILE), BF16), 0, [], 16, got)

time: 131 us -> 125 us (0.954)
  waiting for transfers between devices: 44.2 us -> 36.7 us
  Pallas kernels: 16.9 us -> 11.6 us
  blocking collectives: 30.8 us -> 35.9 us
  starting transfers between devices: 32.5 us -> 35.3 us
    all_to_all x1, waiting for transfers between devices: 15.7 us -> 8.76 us  [exchange(): return lax.all_to_all(value, axes, 0, 0, tiled=True)]
    pallas_call x8, Pallas kernels: 16.9 us -> 11.6 us  [kernel_call(): pl.pallas_call(body, out_shape=[jax.ShapeDtypeStruct(s, d) for s, d in sh...]
    all_to_all x2, blocking collectives: 30.8 us -> 35.9 us  [exchange(): return lax.all_to_all(value, axes, 0, 0, tiled=True)]
    ppermute x10, starting transfers between devices: 13.3 us -> 16.3 us  [rotate(): return lax.ppermute(value, 'x', [(k, (k + step) % NX) for k in range(NX)])]
    ppermute x6 -> x4, waiting for transfers between devices: 8.47 us -> 7.48 us  [swap(): return lax.ppermute(value, axis, [(0, 1), (1, 0)])]
    ppermute x6 -> x4, starting transfers between devices: 4.06 us -> 3.57 us  [swap(): return lax.ppermute(value, axis, [(0, 1), (1, 0)])]
    unnamed x16 -> x20, local copies, waits for them, and re-layouts: 2.91 us -> 2.93 us
  transfers between devices with their start and end apart: 20 -> 18, of which waited for: 14 -> 11; matrix products, arithmetic and copies ran while one was open for 1% -> 0% of each run, Pallas kernels for 1% -> 1%
where the time goes in v3:
time: 125 us; the launch traced here: 124 us
  waiting for transfers between devices  36.7 us (29%)
  blocking collectives  35.9 us (29%)
  starting transfers between devices  35.3 us (28%)
  Pallas kernels  11.6 us (9%)
  local copies, waits for them, and re-layouts  3.01 us (2%)
  between operations  1.41 us (1%)
    all_to_all x2, blocking collectives, exchange(): return lax.all_to_all(value, axes, 0, 0, tiled=True)  35.9 us
    ppermute x10, starting transfers between devices, rotate(): return lax.ppermute(value, 'x', [(k, (k + step) % NX) for k in range(NX)])  16.3 us
    pallas_call x8, Pallas kernels, kernel_call(): pl.pallas_call(body, out_shape=[jax.ShapeDtypeStruct(s, d) for s, d in sh...  11.6 us
    ppermute x3, waiting for transfers between devices, along_y(): return lax.ppermute(value, ('yl', 'yh'), pairs)  10.9 us
    ppermute x10, waiting for transfers between devices, rotate(): return lax.ppermute(value, 'x', [(k, (k + step) % NX) for k in range(NX)])  9.48 us
    all_to_all x1, starting transfers between devices, exchange(): return lax.all_to_all(value, axes, 0, 0, tiled=True)  9.47 us
    all_to_all x1, waiting for transfers between devices, exchange(): return lax.all_to_all(value, axes, 0, 0, tiled=True)  8.76 us
    ppermute x4, waiting for transfers between devices, swap(): return lax.ppermute(value, axis, [(0, 1), (1, 0)])  7.48 us
  transfers between devices with their start and end apart: 18, of which 11 were waited for; matrix products, arithmetic and copies ran while one was open for 0% of the time, Pallas kernels for 1%

profile of v3, /device:TPU:2, one launch (start us, length us, event | category | flops | bytes accessed | tf_op | source)
XLA Modules:
  0.0 124.1 jit_solution(10485596164261035538)
XLA Ops:
  0.6 2.3 %collective-permute-start.1 = (bf16[32,128,128]{2,1,0:T(8,128)(2,1)}, bf16[32,128,128]{2,1,0:T(8,128)(2,1)S(1)}, u32[]{:S(2)}, u32[]{:S(2)}) collective-permute-start(bf16[32,128,128]{2,1,0:T(8,128)(2,1)} %bitcast.36), channel_id=1, source_target_pairs={{0,3},{1,0},{2,1},{3,2},{4,7},{5,4},{6,5},{7,6},{8,11},{9,8},{10,9... | collective-permute-start | bytes 3145736 | tf_op jit(solution)/shard_map/ppermute | solution.py:210
  3.0 0.0 collective-permute-start
  3.0 0.1 pad_add_fusion.ids
  3.1 0.9 copy-done.4
  4.0 0.8 prep.1
  4.8 1.0 copy-done.3
  5.8 9.5 %all-to-all-start = ((bf16[16,256,128]{2,1,0:T(8,128)(2,1)}), bf16[16,256,128]{2,1,0:T(8,128)(2,1)S(1)}, u32[]{:S(2)}, u32[]{:S(2)}) async-start(bf16[16,256,128]{2,1,0:T(8,128)(2,1)} %copy-done.3), calls=%async_computation | async-start | bytes 2097152 | tf_op jit(solution)/shard_map/all_to_all | solution.py:226
  16.0 0.1 pad_add_fusion.1
  16.1 3.4 %collective-permute-start.4 = (s32[1,128]{1,0:T(1,128)S(1)}, s32[1,128]{1,0:T(1,128)S(1)}, u32[]{:S(2)}, u32[]{:S(2)}) collective-permute-start(s32[1,128]{1,0:T(1,128)S(1)} %pad_add_fusion.1), channel_id=1, source_target_pairs={{0,2},{1,3},{2,0},{3,1},{4,6},{5,7},{6,4},{7,5},{8,10},{9,11},{10,... | collective-permute-start | bytes 1544 | tf_op jit(solution)/shard_map/ppermute | solution.py:210
  19.5 0.2 collective-permute-start.3
  19.7 1.8 %collective-permute-start.2 = (s32[1,128]{1,0:T(1,128)S(1)}, s32[1,128]{1,0:T(1,128)S(1)}, u32[]{:S(2)}, u32[]{:S(2)}) collective-permute-start(s32[1,128]{1,0:T(1,128)S(1)} %pad_add_fusion.1), channel_id=1, source_target_pairs={{0,1},{1,2},{2,3},{3,0},{4,5},{5,6},{6,7},{7,4},{8,9},{9,10},{10,1... | collective-permute-start | bytes 1544 | tf_op jit(solution)/shard_map/ppermute | solution.py:210
  21.5 5.3 %collective-permute-done.4.meta_f = s32[1,128]{1,0:T(1,128)S(1)} collective-permute-done((s32[1,128]{1,0:T(1,128)S(1)}, s32[1,128]{1,0:T(1,128)S(1)}, u32[]{:S(2)}, u32[]{:S(2)}) %collective-permute-start.4) | collective-permute-done | bytes 544 | tf_op jit(solution)/shard_map/ppermute | solution.py:210
  26.7 0.5 collective-permute-done.2.meta_l
  27.2 0.0 collective-permute-done.1.right
  27.2 0.0 collective-permute-done.left
  27.2 1.0 relay.1
  28.3 1.0 copy-done.1
  29.2 1.4 %collective-permute-start.5 = (bf16[16,128,128]{2,1,0:T(8,128)(2,1)}, bf16[16,128,128]{2,1,0:T(8,128)(2,1)}, u32[]{:S(2)}, u32[]{:S(2)}) collective-permute-start(bf16[16,128,128]{2,1,0:T(8,128)(2,1)} %get-tuple-element.22), channel_id=1, source_target_pairs={{0,1},{1,2},{2,3},{3,0},{4,5},{5,6},{6,7},{7,4},{8,9},{9,10},{10,1... | collective-permute-start | bytes 1572872 | tf_op jit(solution)/shard_map/ppermute | solution.py:210
  30.6 1.5 %collective-permute-start.6 = (bf16[16,128,128]{2,1,0:T(8,128)(2,1)}, bf16[16,128,128]{2,1,0:T(8,128)(2,1)}, u32[]{:S(2)}, u32[]{:S(2)}) collective-permute-start(bf16[16,128,128]{2,1,0:T(8,128)(2,1)} %get-tuple-element.23), channel_id=1, source_target_pairs={{0,3},{1,0},{2,1},{3,2},{4,7},{5,4},{6,5},{7,6},{8,11},{9,8},{10,9... | collective-permute-start | bytes 1572872 | tf_op jit(solution)/shard_map/ppermute | solution.py:210
  32.2 8.8 %all-to-all-done = bf16[16,256,128]{2,1,0:T(8,128)(2,1)S(1)} async-done(((bf16[16,256,128]{2,1,0:T(8,128)(2,1)}), bf16[16,256,128]{2,1,0:T(8,128)(2,1)S(1)}, u32[]{:S(2)}, u32[]{:S(2)}) %all-to-all-start) | async-done | bytes 1048608 | tf_op jit(solution)/shard_map/all_to_all | solution.py:226
  40.9 0.1 fusion.4
  41.0 0.1 collective-permute-start.7
  41.1 0.5 collective-permute-start.8
  41.6 1.5 %collective-permute-done.5.far_a = bf16[16,128,128]{2,1,0:T(8,128)(2,1)} collective-permute-done((bf16[16,128,128]{2,1,0:T(8,128)(2,1)}, bf16[16,128,128]{2,1,0:T(8,128)(2,1)}, u32[]{:S(2)}, u32[]{:S(2)}) %collective-permute-start.5) | collective-permute-done | bytes 524320 | tf_op jit(solution)/shard_map/ppermute | solution.py:210
  43.1 0.0 collective-permute-done.6.far_b
  43.1 0.0 collective-permute-done.7.rest_0_
  43.1 0.6 collective-permute-done.8.rest_1_
  43.8 0.0 copy-start.7
  43.8 3.4 %forward.1 = f32[8,32,128]{2,1,0:T(8,128)S(1)} custom-call(s32[128]{0:T(128)S(1)} %bitcast.40, s32[128]{0:T(128)S(1)} %bitcast.42, s32[128]{0:T(128)S(1)} %bitcast.44, s32[128]{0:T(128)S(1)} %bitcast.46, bf16[32,128,128]{2,1,0:T(8,128)(2,1)S(1)} %bitcast.38, bf16[32,128,128]{2,1,0:T(8,128)(2,1)S(1)} %copy-done.2, ...), custom_call_target="tpu_custom_call" | custom-call | tf_op jit(solution)/shard_map/forward/pallas_call | solution.py:232
  47.2 3.0 %collective-permute-start.9 = (f32[8,32,128]{2,1,0:T(8,128)S(1)}, f32[8,32,128]{2,1,0:T(8,128)S(1)}, u32[]{:S(2)}, u32[]{:S(2)}) collective-permute-start(f32[8,32,128]{2,1,0:T(8,128)S(1)} %forward.1), channel_id=1, source_target_pairs={{0,4},{4,0},{1,5},{5,1},{2,6},{6,2},{3,7},{7,3},{8,12},{12,8},{9,1... | collective-permute-start | bytes 393224 | tf_op jit(solution)/shard_map/ppermute | solution.py:222
  50.2 4.1 %collective-permute-done.9 = f32[8,32,128]{2,1,0:T(8,128)S(1)} collective-permute-done((f32[8,32,128]{2,1,0:T(8,128)S(1)}, f32[8,32,128]{2,1,0:T(8,128)S(1)}, u32[]{:S(2)}, u32[]{:S(2)}) %collective-permute-start.9) | collective-permute-done | bytes 131104 | tf_op jit(solution)/shard_map/ppermute | solution.py:222
  54.3 3.7 %collective-permute-start.12 = (bf16[8,32,128]{2,1,0:T(8,128)(2,1)S(1)}, bf16[8,32,128]{2,1,0:T(8,128)(2,1)S(1)}, u32[]{:S(2)}, u32[]{:S(2)}) collective-permute-start(bf16[8,32,128]{2,1,0:T(8,128)(2,1)S(1)} %add_convert_fusion.agg), channel_id=1, source_target_pairs={{0,2},{1,3},{2,0},{3,1},{4,6},{5,7},{6,4},{7,5},{8,10},{9,11},{10,... | collective-permute-start | bytes 196616 | tf_op jit(solution)/shard_map/ppermute | solution.py:210
  58.0 2.0 %collective-permute-start.10 = (bf16[8,32,128]{2,1,0:T(8,128)(2,1)S(1)}, bf16[8,32,128]{2,1,0:T(8,128)(2,1)S(1)}, u32[]{:S(2)}, u32[]{:S(2)}) collective-permute-start(bf16[8,32,128]{2,1,0:T(8,128)(2,1)S(1)} %add_convert_fusion.agg), channel_id=1, source_target_pairs={{0,1},{1,2},{2,3},{3,0},{4,5},{5,6},{6,7},{7,4},{8,9},{9,10},{10,1... | collective-permute-start | bytes 196616 | tf_op jit(solution)/shard_map/ppermute | solution.py:210
  60.0 0.2 collective-permute-done.12.agg_f
  60.2 2.0 %collective-permute-done.11.agg_r = bf16[8,32,128]{2,1,0:T(8,128)(2,1)S(1)} collective-permute-done((bf16[8,32,128]{2,1,0:T(8,128)(2,1)S(1)}, bf16[8,32,128]{2,1,0:T(8,128)(2,1)S(1)}, u32[]{:S(2)}, u32[]{:S(2)}) %collective-permute-start.11) | collective-permute-done | bytes 65568 | tf_op jit(solution)/shard_map/ppermute | solution.py:210
  62.2 0.0 collective-permute-done.10.agg_l
  62.3 5.0 %backward.1 = (bf16[1024,128]{1,0:T(8,128)(2,1)}, bf16[4,1056,128]{2,1,0:T(8,128)(2,1)S(1)}, bf16[4,1056,128]{2,1,0:T(8,128)(2,1)S(1)}) custom-call(s32[4]{0:T(128)S(1)} %pad_add_fusion.ids, s32[128]{0:T(128)S(1)} %bitcast.41, s32[128]{0:T(128)S(1)} %bitcast.43, s32[128]{0:T(128)S(1)} %bitcast.45, s32[128]{0:T(128)S(1)} %bitcast.47, ...), custom_call_target="tpu_custom_call" | custom-call | tf_op jit(solution)/shard_map/backward/pallas_call | solution.py:232
  67.3 2.7 %collective-permute-done.13.got = bf16[4,1056,128]{2,1,0:T(8,128)(2,1)S(1)} collective-permute-done((bf16[4,1056,128]{2,1,0:T(8,128)(2,1)S(1)}, bf16[4,1056,128]{2,1,0:T(8,128)(2,1)S(1)}, u32[]{:S(2)}, u32[]{:S(2)}) %collective-permute-start.13) | collective-permute-done | bytes 1081376 | tf_op jit(solution)/shard_map/ppermute | solution.py:222
  70.0 0.2 pair.1
  70.2 1.7 %collective-permute-start.14 = (bf16[1056,128]{1,0:T(8,128)(2,1)S(1)}, bf16[1056,128]{1,0:T(8,128)(2,1)S(1)}, u32[]{:S(2)}, u32[]{:S(2)}) collective-permute-start(bf16[1056,128]{1,0:T(8,128)(2,1)S(1)} %get-tuple-element.28), channel_id=1, source_target_pairs={{0,128},{128,4},{4,132},{132,0},{1,129},{129,5},{5,133},{133,1},{2... | collective-permute-start | bytes 811016 | tf_op jit(solution)/shard_map/ppermute | solution.py:218
  71.9 2.9 %collective-permute-start.15 = (bf16[1056,128]{1,0:T(8,128)(2,1)S(1)}, bf16[1056,128]{1,0:T(8,128)(2,1)S(1)}, u32[]{:S(2)}, u32[]{:S(2)}) collective-permute-start(bf16[1056,128]{1,0:T(8,128)(2,1)S(1)} %get-tuple-element.29), channel_id=1, source_target_pairs={{0,4},{128,132},{4,0},{132,128},{1,5},{129,133},{5,1},{133,129},{2... | collective-permute-start | bytes 811016 | tf_op jit(solution)/shard_map/ppermute | solution.py:218
  74.8 1.3 %collective-permute-start.16 = (bf16[1056,128]{1,0:T(8,128)(2,1)S(1)}, bf16[1056,128]{1,0:T(8,128)(2,1)S(1)}, u32[]{:S(2)}, u32[]{:S(2)}) collective-permute-start(bf16[1056,128]{1,0:T(8,128)(2,1)S(1)} %get-tuple-element.30), channel_id=1, source_target_pairs={{0,132},{128,0},{4,128},{132,4},{1,133},{129,1},{5,129},{133,5},{2... | collective-permute-start | bytes 811016 | tf_op jit(solution)/shard_map/ppermute | solution.py:218
  76.1 4.0 %collective-permute-done.14.before = bf16[1056,128]{1,0:T(8,128)(2,1)S(1)} collective-permute-done((bf16[1056,128]{1,0:T(8,128)(2,1)S(1)}, bf16[1056,128]{1,0:T(8,128)(2,1)S(1)}, u32[]{:S(2)}, u32[]{:S(2)}) %collective-permute-start.14) | collective-permute-done | bytes 270368 | tf_op jit(solution)/shard_map/ppermute | solution.py:218
  80.1 7.0 %collective-permute-done.15.across = bf16[1056,128]{1,0:T(8,128)(2,1)S(1)} collective-permute-done((bf16[1056,128]{1,0:T(8,128)(2,1)S(1)}, bf16[1056,128]{1,0:T(8,128)(2,1)S(1)}, u32[]{:S(2)}, u32[]{:S(2)}) %collective-permute-start.15) | collective-permute-done | bytes 270368 | tf_op jit(solution)/shard_map/ppermute | solution.py:218
  87.1 0.1 y_sum.1
  87.2 21.0 %all_to_all.15.got = bf16[8,160,128]{2,1,0:T(8,128)(2,1)S(1)} all-to-all(bf16[8,160,128]{2,1,0:T(8,128)(2,1)S(1)} %y_sum.1), channel_id=1, replica_groups=mesh['yl'=2,'z'=8,'c'=2,'yh'=2,'x'=4] {'z'}, dimensions={0} | all-to-all | bytes 655360 | tf_op jit(solution)/shard_map/all_to_all | solution.py:226
  108.3 14.9 %all_to_all.16.got = bf16[8,160,128]{2,1,0:T(8,128)(2,1)S(1)} all-to-all(bf16[8,160,128]{2,1,0:T(8,128)(2,1)S(1)} %z_sum.1), channel_id=1, replica_groups=mesh['yl'=2,'z'=8,'c'=2,'yh'=2,'x'=4] {'yh','x'}, dimensions={0} | all-to-all | bytes 655360 | tf_op jit(solution)/shard_map/all_to_all | solution.py:226
  123.2 0.9 finish.1
  (24 shorter events, 0.2 us)
Async XLA Ops:
  0.6 26.6 %collective-permute-start.1 = (bf16[32,128,128]{2,1,0:T(8,128)(2,1)}, bf16[32,128,128]{2,1,0:T(8,128)(2,1)S(1)}, u32[]{:S(2)}, u32[]{:S(2)}) collective-permute-start(bf16[32,128,128]{2,1,0:T(8,128)(2,1)} %bitcast.36), channel_id=1, source_target_pairs={{0,3},{1,0},{2,1},{3,2},{4,7},{5,4},{6,5},{7,6},{8,11},{9,8},{10,9... | collective-permute-start | bytes 3145736 | tf_op jit(solution)/shard_map/ppermute | solution.py:210
  3.0 24.2 %collective-permute-start = (bf16[32,128,128]{2,1,0:T(8,128)(2,1)}, bf16[32,128,128]{2,1,0:T(8,128)(2,1)S(1)}, u32[]{:S(2)}, u32[]{:S(2)}) collective-permute-start(bf16[32,128,128]{2,1,0:T(8,128)(2,1)} %bitcast.37), channel_id=1, source_target_pairs={{0,1},{1,2},{2,3},{3,0},{4,5},{5,6},{6,7},{7,4},{8,9},{9,10},{10,1... | collective-permute-start | bytes 3145736 | tf_op jit(solution)/shard_map/ppermute | solution.py:210
  3.1 1.0 copy-start.4
  4.8 1.0 copy-start.3
  5.8 10.1 %copy-start.8 = (s32[1,1,32]{2,1,0:T(1,128)S(1)}, s32[1,1,32]{2,1,0:T(1,128)}, u32[]{:S(2)}) copy-start(s32[1,1,32]{2,1,0:T(1,128)} %param.11) | copy-start | bytes 388
  5.8 10.1 %copy-start.9 = (s32[1,1,32]{2,1,0:T(1,128)S(1)}, s32[1,1,32]{2,1,0:T(1,128)}, u32[]{:S(2)}) copy-start(s32[1,1,32]{2,1,0:T(1,128)} %param.10) | copy-start | bytes 388
  5.8 35.1 %all-to-all-start = ((bf16[16,256,128]{2,1,0:T(8,128)(2,1)}), bf16[16,256,128]{2,1,0:T(8,128)(2,1)S(1)}, u32[]{:S(2)}, u32[]{:S(2)}) async-start(bf16[16,256,128]{2,1,0:T(8,128)(2,1)} %copy-done.3), calls=%async_computation | async-start | bytes 2097152 | tf_op jit(solution)/shard_map/all_to_all | solution.py:226
  16.1 10.6 %collective-permute-start.4 = (s32[1,128]{1,0:T(1,128)S(1)}, s32[1,128]{1,0:T(1,128)S(1)}, u32[]{:S(2)}, u32[]{:S(2)}) collective-permute-start(s32[1,128]{1,0:T(1,128)S(1)} %pad_add_fusion.1), channel_id=1, source_target_pairs={{0,2},{1,3},{2,0},{3,1},{4,6},{5,7},{6,4},{7,5},{8,10},{9,11},{10,... | collective-permute-start | bytes 1544 | tf_op jit(solution)/shard_map/ppermute | solution.py:210
  19.5 7.3 %collective-permute-start.3 = (s32[1,128]{1,0:T(1,128)S(1)}, s32[1,128]{1,0:T(1,128)S(1)}, u32[]{:S(2)}, u32[]{:S(2)}) collective-permute-start(s32[1,128]{1,0:T(1,128)S(1)} %pad_add_fusion.1), channel_id=1, source_target_pairs={{0,3},{1,0},{2,1},{3,2},{4,7},{5,4},{6,5},{7,6},{8,11},{9,8},{10,9... | collective-permute-start | bytes 1544 | tf_op jit(solution)/shard_map/ppermute | solution.py:210
  19.7 7.5 %collective-permute-start.2 = (s32[1,128]{1,0:T(1,128)S(1)}, s32[1,128]{1,0:T(1,128)S(1)}, u32[]{:S(2)}, u32[]{:S(2)}) collective-permute-start(s32[1,128]{1,0:T(1,128)S(1)} %pad_add_fusion.1), channel_id=1, source_target_pairs={{0,1},{1,2},{2,3},{3,0},{4,5},{5,6},{6,7},{7,4},{8,9},{9,10},{10,1... | collective-permute-start | bytes 1544 | tf_op jit(solution)/shard_map/ppermute | solution.py:210
  28.2 1.0 copy-start.1
  29.2 14.5 %copy-start = (bf16[1,1,32,128,128]{4,3,2,1,0:T(8,128)(2,1)S(1)}, bf16[1,1,32,128,128]{4,3,2,1,0:T(8,128)(2,1)}, u32[]{:S(2)}) copy-start(bf16[1,1,32,128,128]{4,3,2,1,0:T(8,128)(2,1)} %param.9) | copy-start | bytes 3145732
  29.2 13.9 %collective-permute-start.5 = (bf16[16,128,128]{2,1,0:T(8,128)(2,1)}, bf16[16,128,128]{2,1,0:T(8,128)(2,1)}, u32[]{:S(2)}, u32[]{:S(2)}) collective-permute-start(bf16[16,128,128]{2,1,0:T(8,128)(2,1)} %get-tuple-element.22), channel_id=1, source_target_pairs={{0,1},{1,2},{2,3},{3,0},{4,5},{5,6},{6,7},{7,4},{8,9},{9,10},{10,1... | collective-permute-start | bytes 1572872 | tf_op jit(solution)/shard_map/ppermute | solution.py:210
  30.6 12.5 %collective-permute-start.6 = (bf16[16,128,128]{2,1,0:T(8,128)(2,1)}, bf16[16,128,128]{2,1,0:T(8,128)(2,1)}, u32[]{:S(2)}, u32[]{:S(2)}) collective-permute-start(bf16[16,128,128]{2,1,0:T(8,128)(2,1)} %get-tuple-element.23), channel_id=1, source_target_pairs={{0,3},{1,0},{2,1},{3,2},{4,7},{5,4},{6,5},{7,6},{8,11},{9,8},{10,9... | collective-permute-start | bytes 1572872 | tf_op jit(solution)/shard_map/ppermute | solution.py:210
  40.9 2.9 %copy-start.2 = (bf16[32,128,128]{2,1,0:T(8,128)(2,1)S(1)}, bf16[32,128,128]{2,1,0:T(8,128)(2,1)}, u32[]{:S(2)}) copy-start(bf16[32,128,128]{2,1,0:T(8,128)(2,1)} %copy-done.1) | copy-start | bytes 3145732
  41.0 2.1 %collective-permute-start.7 = (bf16[64,32,128]{2,1,0:T(8,128)(2,1)S(1)}, bf16[64,32,128]{2,1,0:T(8,128)(2,1)S(1)}, u32[]{:S(2)}, u32[]{:S(2)}) collective-permute-start(bf16[64,32,128]{2,1,0:T(8,128)(2,1)S(1)} %bitcast.50), channel_id=1, source_target_pairs={{0,8},{8,0},{1,9},{9,1},{2,10},{10,2},{3,11},{11,3},{4,12},{12,4},... | collective-permute-start | bytes 1572872 | tf_op jit(solution)/shard_map/ppermute | solution.py:222
  41.1 2.6 %collective-permute-start.8 = (bf16[64,32,128]{2,1,0:T(8,128)(2,1)S(1)}, bf16[64,32,128]{2,1,0:T(8,128)(2,1)S(1)}, u32[]{:S(2)}, u32[]{:S(2)}) collective-permute-start(bf16[64,32,128]{2,1,0:T(8,128)(2,1)S(1)} %bitcast.49), channel_id=1, source_target_pairs={{0,8},{8,0},{1,9},{9,1},{2,10},{10,2},{3,11},{11,3},{4,12},{12,4},... | collective-permute-start | bytes 1572872 | tf_op jit(solution)/shard_map/ppermute | solution.py:222
  43.8 18.5 %copy-start.5 = (bf16[1024,128]{1,0:T(8,128)(2,1)S(1)}, bf16[1024,128]{1,0:T(8,128)(2,1)}, u32[]{:S(2)}) copy-start(bf16[1024,128]{1,0:T(8,128)(2,1)} %cot.1) | copy-start | bytes 786436
  43.8 18.5 %copy-start.6 = (bf16[128,128]{1,0:T(8,128)(2,1)S(1)}, bf16[128,128]{1,0:T(8,128)(2,1)}, u32[]{:S(2)}) copy-start(bf16[128,128]{1,0:T(8,128)(2,1)} %weight.1) | copy-start | bytes 98308
  43.8 18.5 %copy-start.7 = (f32[128]{0:T(128)S(1)}, f32[128]{0:T(128)}, u32[]{:S(2)}) copy-start(f32[128]{0:T(128)} %param.14) | copy-start | bytes 1540
  47.2 7.1 %collective-permute-start.9 = (f32[8,32,128]{2,1,0:T(8,128)S(1)}, f32[8,32,128]{2,1,0:T(8,128)S(1)}, u32[]{:S(2)}, u32[]{:S(2)}) collective-permute-start(f32[8,32,128]{2,1,0:T(8,128)S(1)} %forward.1), channel_id=1, source_target_pairs={{0,4},{4,0},{1,5},{5,1},{2,6},{6,2},{3,7},{7,3},{8,12},{12,8},{9,1... | collective-permute-start | bytes 393224 | tf_op jit(solution)/shard_map/ppermute | solution.py:222
  54.3 5.9 %collective-permute-start.12 = (bf16[8,32,128]{2,1,0:T(8,128)(2,1)S(1)}, bf16[8,32,128]{2,1,0:T(8,128)(2,1)S(1)}, u32[]{:S(2)}, u32[]{:S(2)}) collective-permute-start(bf16[8,32,128]{2,1,0:T(8,128)(2,1)S(1)} %add_convert_fusion.agg), channel_id=1, source_target_pairs={{0,2},{1,3},{2,0},{3,1},{4,6},{5,7},{6,4},{7,5},{8,10},{9,11},{10,... | collective-permute-start | bytes 196616 | tf_op jit(solution)/shard_map/ppermute | solution.py:210
  58.0 4.3 %collective-permute-start.11 = (bf16[8,32,128]{2,1,0:T(8,128)(2,1)S(1)}, bf16[8,32,128]{2,1,0:T(8,128)(2,1)S(1)}, u32[]{:S(2)}, u32[]{:S(2)}) collective-permute-start(bf16[8,32,128]{2,1,0:T(8,128)(2,1)S(1)} %add_convert_fusion.agg), channel_id=1, source_target_pairs={{0,3},{1,0},{2,1},{3,2},{4,7},{5,4},{6,5},{7,6},{8,11},{9,8},{10,9... | collective-permute-start | bytes 196616 | tf_op jit(solution)/shard_map/ppermute | solution.py:210
  58.0 4.3 %collective-permute-start.10 = (bf16[8,32,128]{2,1,0:T(8,128)(2,1)S(1)}, bf16[8,32,128]{2,1,0:T(8,128)(2,1)S(1)}, u32[]{:S(2)}, u32[]{:S(2)}) collective-permute-start(bf16[8,32,128]{2,1,0:T(8,128)(2,1)S(1)} %add_convert_fusion.agg), channel_id=1, source_target_pairs={{0,1},{1,2},{2,3},{3,0},{4,5},{5,6},{6,7},{7,4},{8,9},{9,10},{10,1... | collective-permute-start | bytes 196616 | tf_op jit(solution)/shard_map/ppermute | solution.py:210
  67.3 2.7 %collective-permute-start.13 = (bf16[4,1056,128]{2,1,0:T(8,128)(2,1)S(1)}, bf16[4,1056,128]{2,1,0:T(8,128)(2,1)S(1)}, u32[]{:S(2)}, u32[]{:S(2)}) collective-permute-start(bf16[4,1056,128]{2,1,0:T(8,128)(2,1)S(1)} %get-tuple-element.26), channel_id=1, source_target_pairs={{0,8},{8,0},{1,9},{9,1},{2,10},{10,2},{3,11},{11,3},{4,12},{12,4},... | collective-permute-start | bytes 3244040 | tf_op jit(solution)/shard_map/ppermute | solution.py:222
  70.2 9.9 %collective-permute-start.14 = (bf16[1056,128]{1,0:T(8,128)(2,1)S(1)}, bf16[1056,128]{1,0:T(8,128)(2,1)S(1)}, u32[]{:S(2)}, u32[]{:S(2)}) collective-permute-start(bf16[1056,128]{1,0:T(8,128)(2,1)S(1)} %get-tuple-element.28), channel_id=1, source_target_pairs={{0,128},{128,4},{4,132},{132,0},{1,129},{129,5},{5,133},{133,1},{2... | collective-permute-start | bytes 811016 | tf_op jit(solution)/shard_map/ppermute | solution.py:218
  71.9 15.2 %collective-permute-start.15 = (bf16[1056,128]{1,0:T(8,128)(2,1)S(1)}, bf16[1056,128]{1,0:T(8,128)(2,1)S(1)}, u32[]{:S(2)}, u32[]{:S(2)}) collective-permute-start(bf16[1056,128]{1,0:T(8,128)(2,1)S(1)} %get-tuple-element.29), channel_id=1, source_target_pairs={{0,4},{128,132},{4,0},{132,128},{1,5},{129,133},{5,1},{133,129},{2... | collective-permute-start | bytes 811016 | tf_op jit(solution)/shard_map/ppermute | solution.py:218
  74.8 12.3 %collective-permute-start.16 = (bf16[1056,128]{1,0:T(8,128)(2,1)S(1)}, bf16[1056,128]{1,0:T(8,128)(2,1)S(1)}, u32[]{:S(2)}, u32[]{:S(2)}) collective-permute-start(bf16[1056,128]{1,0:T(8,128)(2,1)S(1)} %get-tuple-element.30), channel_id=1, source_target_pairs={{0,132},{128,0},{4,128},{132,4},{1,133},{129,1},{5,129},{133,5},{2... | collective-permute-start | bytes 811016 | tf_op jit(solution)/shard_map/ppermute | solution.py:218

commit v4 on v3

--- a/solution.py
+++ b/solution.py
@@ -1,3 +1,5 @@
+import functools
+
 import jax
 import jax.numpy as jnp
 from jax import lax
@@ -70,8 +72,18 @@
     out_f[...] = meta_f[...]
 
 
+def fetch_far(far_a, far_b, far, far_sem):
+    copies = [
+        pltpu.make_async_copy(ref, far.at[k], far_sem.at[k]) for k, ref in enumerate((far_a, far_b))
+    ]
+    for copy in copies:
+        copy.start()
+    return copies
+
+
 def forward_kernel(meta, meta_l, meta_r, meta_f, own, left, right, far_a, far_b, mine, *rest):
-    others, (out, table, acc) = rest[:SWAPS], rest[SWAPS:]
+    others, (out, table, acc, far, far_sem) = rest[:SWAPS], rest[SWAPS:]
+    fetch = fetch_far(far_a, far_b, far, far_sem)
     acc[...] = jnp.zeros_like(acc)
     half = NP * ROW_TILES
     table[0:half] = mine[...]
@@ -83,8 +95,10 @@
     def work(tile, meta, s):
         return acc, meta[s], mul(tile, table[meta[SLOTS + s]], CONTRACT_LAST)
 
-    groups = [(own, meta, 0), (left, meta_l, 0), (right, meta_r, 0), (far_a, meta_f, 0)]
-    every_slot(groups + [(far_b, meta_f, HALF)], work)
+    every_slot([(own, meta, 0), (left, meta_l, 0), (right, meta_r, 0)], work)
+    for copy in fetch:
+        copy.wait()
+    every_slot([(far.at[0], meta_f, 0), (far.at[1], meta_f, HALF)], work)
     for t in range(ROW_TILES):
         out[t] = acc[t].T
 
@@ -93,7 +107,9 @@
     ids, meta, meta_l, meta_r, meta_f, own, left, right, far_a, far_b, agg, agg_l, agg_r, agg_f, weight, bias, cot,
     act, keep, *rest,
 ):
-    send, acc, back, full, slopes, wsum = rest
+    send_a, send_b, acc, back, full, slopes, wsum, far, act_in, far_sem, act_sem = rest
+    sends = {1: send_a.at[0], 2: send_a.at[1], 3: send_b.at[0], 0: send_b.at[1]}
+    fetch = fetch_far(far_a, far_b, far, far_sem)
     x, yl, yh = ids[0], ids[2], ids[3]
     acc[...] = jnp.zeros_like(acc)
     for t in range(ROW_TILES):
@@ -105,13 +121,15 @@
         sq = pre * pre
         th = jnp.tanh(0.7978845608028654 * pre * (1.0 + 0.044715 * sq))
         half = 0.5 * (1.0 + th)
-        act[t * TILE : (t + 1) * TILE, :] = (pre * half).astype(BF16)
+        act_in[t * TILE : (t + 1) * TILE, :] = (pre * half).astype(BF16)
         slope = half + 0.5 * pre * (1.0 - th * th) * (
             0.7978845608028654 * (1.0 + (3 * 0.044715) * sq)
         )
         delta = (cot[t * TILE : (t + 1) * TILE, :].astype(F32) * slope).astype(BF16)
         slopes[t] = delta
         back[t] = mul(w_rows, delta, CONTRACT_LAST).astype(BF16)
+    give = pltpu.make_async_copy(act_in, act, act_sem)
+    give.start()
     bsum = jnp.zeros((1, WIDE), F32)
     wpart = jnp.zeros((THIN, WIDE), F32)
     for t in range(BLOCK_HALF):
@@ -131,25 +149,28 @@
         some = wsum[pl.ds(pl.multiple_of(there * GRADS, GRADS), GRADS), :]
         extra = jnp.concatenate([some, rest], axis=0).astype(BF16)
         keep[k, PIECE:, :] = extra
-        send[k, PIECE:, :] = extra
+        sends[k][PIECE:, :] = extra
 
     back[ROW_TILES] = jnp.zeros((THIN, TILE), BF16)
 
     def work(tile, meta, s):
         return acc, meta[3 * SLOTS + s], mul(back[meta[2 * SLOTS + s]], tile, PLAIN)
 
-    groups = [(own, meta, 0), (left, meta_l, 0), (right, meta_r, 0), (far_a, meta_f, 0)]
-    every_slot(groups + [(far_b, meta_f, HALF)], work)
+    every_slot([(own, meta, 0), (left, meta_l, 0), (right, meta_r, 0)], work)
+    for copy in fetch:
+        copy.wait()
+    every_slot([(far.at[0], meta_f, 0), (far.at[1], meta_f, HALF)], work)
     per = NZ * BLOCK_HALF
     for k in range(NY):
         for i in range(per):
             keep[k, i * THIN : (i + 1) * THIN, :] = acc[k * per + i].astype(BF16)
-            send[k, i * THIN : (i + 1) * THIN, :] = acc[(NY + k) * per + i].astype(BF16)
-
-
-def pair_kernel(keep, got, *outs):
-    for k, out in enumerate(outs):
-        out[...] = (keep[k].astype(F32) + got[k].astype(F32)).astype(BF16)
+            sends[k][i * THIN : (i + 1) * THIN, :] = acc[(NY + k) * per + i].astype(BF16)
+    give.wait()
+
+
+def pair_kernel(which, keep, got, *outs):
+    for at, (k, out) in enumerate(zip(which, outs)):
+        out[...] = (keep[k].astype(F32) + got[at].astype(F32)).astype(BF16)
 
 
 def y_sum_kernel(own, before, across, after, out):
@@ -226,7 +247,11 @@
     return lax.all_to_all(value, axes, 0, 0, tiled=True)
 
 
-def kernel_call(body, name, outs, scalars, scratch, mb, *args, cost=None):
+def place(loose):
+    return pl.BlockSpec(memory_space=pl.ANY if loose else pltpu.VMEM)
+
+
+def kernel_call(body, name, outs, scalars, scratch, mb, *args, cost=None, loose_in=(), loose_out=()):
     one = isinstance(outs, tuple)
     shapes = [outs] if one else outs
     result = pl.pallas_call(
@@ -235,8 +260,8 @@
         grid_spec=pltpu.PrefetchScalarGridSpec(
             num_scalar_prefetch=scalars,
             grid=(),
-            in_specs=[pl.BlockSpec(memory_space=pltpu.VMEM)] * (len(args) - scalars),
-            out_specs=[pl.BlockSpec(memory_space=pltpu.VMEM)] * len(shapes),
+            in_specs=[place(i in loose_in) for i in range(len(args) - scalars)],
+            out_specs=[place(i in loose_out) for i in range(len(shapes))],
             scratch_shapes=scratch,
         ),
         compiler_params=pltpu.CompilerParams(vmem_limit_bytes=mb * 1024 * 1024),
@@ -244,6 +269,11 @@
         name=name,
     )(*args)
     return result[0] if one else result
+
+
+def pair(which, keep, got):
+    outs = [(got.shape[1:], BF16)] * 2
+    return kernel_call(functools.partial(pair_kernel, which), "pair", outs, 0, [], 12, keep, got)
 
 
 def shards(features, tile_values, tile_rows, tile_cols, tile_count, weight, bias, cotangent):
@@ -283,19 +313,21 @@
     scratch = [
         pltpu.VMEM((2 * NP * ROW_TILES + 1, THIN, TILE), BF16),
         pltpu.VMEM((ROW_TILES, TILE, THIN), F32),
+        pltpu.VMEM((2, HALF, TILE, TILE), BF16),
+        pltpu.SemaphoreType.DMA((2,)),
     ]
     part = kernel_call(
-        forward_kernel, "forward", (thin, F32), 4, scratch, 16, *metas, *tiles, mine, *others
+        forward_kernel, "forward", (thin, F32), 4, scratch, 16, *metas, *tiles, mine, *others, loose_in=(3, 4)
     )
     agg = (part + swap(part, "yh")).astype(BF16)
     agg_l, agg_r, agg_f = rotate(agg, 1), rotate(agg, NX - 1), rotate(agg, 2)
 
     piece = PIECE + EXTRA
     square = (ROW_TILES, TILE, WIDE)
-    activations, keep, send = kernel_call(
+    activations, keep, send_a, send_b = kernel_call(
         backward_kernel,
         "backward",
-        [((ROW_TILES * TILE, WIDE), BF16), ((NY, piece, TILE), BF16), ((NY, piece, TILE), BF16)],
+        [((ROW_TILES * TILE, WIDE), BF16), ((NY, piece, TILE), BF16)] + [((2, piece, TILE), BF16)] * 2,
         5,
         [
             pltpu.VMEM((2 * NY * NZ * BLOCK_HALF, THIN, TILE), F32),
@@ -303,6 +335,10 @@
             pltpu.VMEM(square, BF16),
             pltpu.VMEM(square, BF16),
             pltpu.VMEM((THIN, WIDE), F32),
+            pltpu.VMEM((2, HALF, TILE, TILE), BF16),
+            pltpu.VMEM((ROW_TILES * TILE, WIDE), BF16),
+            pltpu.SemaphoreType.DMA((2,)),
+            pltpu.SemaphoreType.DMA(()),
         ],
         20,
         ids,
@@ -315,11 +351,11 @@
         weight,
         bias.reshape(1, WIDE),
         cotangent,
-    )
-    got = swap(send, "c")
-    stay, one, two, three = kernel_call(
-        pair_kernel, "pair", [((piece, TILE), BF16)] * NY, 0, [], 12, keep, got
-    )
+        loose_in=(3, 4),
+        loose_out=(0,),
+    )
+    one, two = pair((1, 2), keep, swap(send_a, "c"))
+    three, stay = pair((3, 0), keep, swap(send_b, "c"))
     before, across, after = along_y(one, 1), along_y(two, 2), along_y(three, 3)
     last = LAST + EXTRA
     summed = kernel_call(

time: 125 us -> 123 us (0.984)
  blocking collectives: 35.9 us -> 34.1 us
    ppermute x3, waiting for transfers between devices: 10.9 us -> 13 us  [along_y(): return lax.ppermute(value, ('yl', 'yh'), pairs)]
    all_to_all x2, blocking collectives: 35.9 us -> 34.1 us  [exchange(): return lax.all_to_all(value, axes, 0, 0, tiled=True)]
    ppermute x4 -> x5, waiting for transfers between devices: 7.48 us -> 6.16 us  [swap(): return lax.ppermute(value, axis, [(0, 1), (1, 0)])]
    ppermute x4 -> x5, starting transfers between devices: 3.57 us -> 4.18 us  [swap(): return lax.ppermute(value, axis, [(0, 1), (1, 0)])]
    pallas_call x8 -> x9, Pallas kernels: 11.6 us -> 11.4 us  [kernel_call(): pl.pallas_call(body, out_shape=[jax.ShapeDtypeStruct(s, d) for s, d in sh...]
  transfers between devices with their start and end apart: 18 -> 19, of which waited for: 11 -> 11; matrix products, arithmetic and copies ran while one was open for 0% -> 0% of each run, Pallas kernels for 1% -> 2%
where the time goes in v4:
time: 123 us
  waiting for transfers between devices  37.5 us (30%)
  starting transfers between devices  35.4 us (29%)
  blocking collectives  34.1 us (28%)
  Pallas kernels  11.4 us (9%)
  local copies, waits for them, and re-layouts  2.98 us (2%)
  between operations  1.44 us (1%)
    all_to_all x2, blocking collectives, exchange(): return lax.all_to_all(value, axes, 0, 0, tiled=True)  34.1 us
    ppermute x10, starting transfers between devices, rotate(): return lax.ppermute(value, 'x', [(k, (k + step) % NX) for k in range(NX)])  16.4 us
    ppermute x3, waiting for transfers between devices, along_y(): return lax.ppermute(value, ('yl', 'yh'), pairs)  13 us
    pallas_call x9, Pallas kernels, kernel_call(): pl.pallas_call(body, out_shape=[jax.ShapeDtypeStruct(s, d) for s, d in sh...  11.4 us
    ppermute x10, waiting for transfers between devices, rotate(): return lax.ppermute(value, 'x', [(k, (k + step) % NX) for k in range(NX)])  9.51 us
    all_to_all x1, starting transfers between devices, exchange(): return lax.all_to_all(value, axes, 0, 0, tiled=True)  9.47 us
    all_to_all x1, waiting for transfers between devices, exchange(): return lax.all_to_all(value, axes, 0, 0, tiled=True)  8.75 us
    ppermute x5, waiting for transfers between devices, swap(): return lax.ppermute(value, axis, [(0, 1), (1, 0)])  6.16 us
  transfers between devices with their start and end apart: 19, of which 11 were waited for; matrix products, arithmetic and copies ran while one was open for 0% of the time, Pallas kernels for 2%

profile of v4, /device:TPU:2, one launch (start us, length us, event | category | flops | bytes accessed | tf_op | source)
XLA Modules:
  0.0 123.1 jit_solution(11264915878921879388)
XLA Ops:
  0.6 2.3 %collective-permute-start.1 = (bf16[32,128,128]{2,1,0:T(8,128)(2,1)}, bf16[32,128,128]{2,1,0:T(8,128)(2,1)S(1)}, u32[]{:S(2)}, u32[]{:S(2)}) collective-permute-start(bf16[32,128,128]{2,1,0:T(8,128)(2,1)} %bitcast.36), channel_id=1, source_target_pairs={{0,3},{1,0},{2,1},{3,2},{4,7},{5,4},{6,5},{7,6},{8,11},{9,8},{10,9... | collective-permute-start | bytes 3145736 | tf_op jit(solution)/shard_map/ppermute | solution.py:231
  3.0 0.1 pad_add_fusion.ids
  3.1 0.9 copy-done.4
  4.0 0.8 prep.1
  4.8 0.9 copy-done.3
  5.8 9.5 %all-to-all-start = ((bf16[16,256,128]{2,1,0:T(8,128)(2,1)}), bf16[16,256,128]{2,1,0:T(8,128)(2,1)S(1)}, u32[]{:S(2)}, u32[]{:S(2)}) async-start(bf16[16,256,128]{2,1,0:T(8,128)(2,1)} %copy-done.3), calls=%async_computation | async-start | bytes 2097152 | tf_op jit(solution)/shard_map/all_to_all | solution.py:247
  16.0 0.1 pad_add_fusion.1
  16.1 3.4 %collective-permute-start.4 = (s32[1,128]{1,0:T(1,128)S(1)}, s32[1,128]{1,0:T(1,128)S(1)}, u32[]{:S(2)}, u32[]{:S(2)}) collective-permute-start(s32[1,128]{1,0:T(1,128)S(1)} %pad_add_fusion.1), channel_id=1, source_target_pairs={{0,2},{1,3},{2,0},{3,1},{4,6},{5,7},{6,4},{7,5},{8,10},{9,11},{10,... | collective-permute-start | bytes 1544 | tf_op jit(solution)/shard_map/ppermute | solution.py:231
  19.4 0.2 collective-permute-start.3
  19.7 1.8 %collective-permute-start.2 = (s32[1,128]{1,0:T(1,128)S(1)}, s32[1,128]{1,0:T(1,128)S(1)}, u32[]{:S(2)}, u32[]{:S(2)}) collective-permute-start(s32[1,128]{1,0:T(1,128)S(1)} %pad_add_fusion.1), channel_id=1, source_target_pairs={{0,1},{1,2},{2,3},{3,0},{4,5},{5,6},{6,7},{7,4},{8,9},{9,10},{10,1... | collective-permute-start | bytes 1544 | tf_op jit(solution)/shard_map/ppermute | solution.py:231
  21.5 5.3 %collective-permute-done.4.meta_f = s32[1,128]{1,0:T(1,128)S(1)} collective-permute-done((s32[1,128]{1,0:T(1,128)S(1)}, s32[1,128]{1,0:T(1,128)S(1)}, u32[]{:S(2)}, u32[]{:S(2)}) %collective-permute-start.4) | collective-permute-done | bytes 544 | tf_op jit(solution)/shard_map/ppermute | solution.py:231
  26.7 0.0 collective-permute-done.3.meta_r
  26.7 0.5 collective-permute-done.2.meta_l
  27.2 1.1 relay.1
  28.3 1.0 copy-done.1
  29.2 1.4 %collective-permute-start.5 = (bf16[16,128,128]{2,1,0:T(8,128)(2,1)}, bf16[16,128,128]{2,1,0:T(8,128)(2,1)}, u32[]{:S(2)}, u32[]{:S(2)}) collective-permute-start(bf16[16,128,128]{2,1,0:T(8,128)(2,1)} %get-tuple-element.23), channel_id=1, source_target_pairs={{0,1},{1,2},{2,3},{3,0},{4,5},{5,6},{6,7},{7,4},{8,9},{9,10},{10,1... | collective-permute-start | bytes 1572872 | tf_op jit(solution)/shard_map/ppermute | solution.py:231
  30.6 1.5 %collective-permute-start.6 = (bf16[16,128,128]{2,1,0:T(8,128)(2,1)}, bf16[16,128,128]{2,1,0:T(8,128)(2,1)}, u32[]{:S(2)}, u32[]{:S(2)}) collective-permute-start(bf16[16,128,128]{2,1,0:T(8,128)(2,1)} %get-tuple-element.24), channel_id=1, source_target_pairs={{0,3},{1,0},{2,1},{3,2},{4,7},{5,4},{6,5},{7,6},{8,11},{9,8},{10,9... | collective-permute-start | bytes 1572872 | tf_op jit(solution)/shard_map/ppermute | solution.py:231
  32.2 8.8 %all-to-all-done = bf16[16,256,128]{2,1,0:T(8,128)(2,1)S(1)} async-done(((bf16[16,256,128]{2,1,0:T(8,128)(2,1)}), bf16[16,256,128]{2,1,0:T(8,128)(2,1)S(1)}, u32[]{:S(2)}, u32[]{:S(2)}) %all-to-all-start) | async-done | bytes 1048608 | tf_op jit(solution)/shard_map/all_to_all | solution.py:247
  40.9 0.1 fusion.4
  41.0 0.1 collective-permute-start.7
  41.1 0.5 collective-permute-start.8
  41.6 1.5 %collective-permute-done.5.far_a = bf16[16,128,128]{2,1,0:T(8,128)(2,1)} collective-permute-done((bf16[16,128,128]{2,1,0:T(8,128)(2,1)}, bf16[16,128,128]{2,1,0:T(8,128)(2,1)}, u32[]{:S(2)}, u32[]{:S(2)}) %collective-permute-start.5) | collective-permute-done | bytes 524320 | tf_op jit(solution)/shard_map/ppermute | solution.py:231
  43.1 0.0 collective-permute-done.6.far_b
  43.1 0.6 collective-permute-done.8.rest_1_
  43.8 0.0 copy-start.7
  43.8 3.4 %forward.1 = f32[8,32,128]{2,1,0:T(8,128)S(1)} custom-call(s32[128]{0:T(128)S(1)} %bitcast.40, s32[128]{0:T(128)S(1)} %bitcast.42, s32[128]{0:T(128)S(1)} %bitcast.44, s32[128]{0:T(128)S(1)} %bitcast.46, bf16[32,128,128]{2,1,0:T(8,128)(2,1)S(1)} %bitcast.38, bf16[32,128,128]{2,1,0:T(8,128)(2,1)S(1)} %copy-done.2, ...), custom_call_target="tpu_custom_call" | custom-call | tf_op jit(solution)/shard_map/forward/pallas_call | solution.py:257
  47.2 3.0 %collective-permute-start.9 = (f32[8,32,128]{2,1,0:T(8,128)S(1)}, f32[8,32,128]{2,1,0:T(8,128)S(1)}, u32[]{:S(2)}, u32[]{:S(2)}) collective-permute-start(f32[8,32,128]{2,1,0:T(8,128)S(1)} %forward.1), channel_id=1, source_target_pairs={{0,4},{4,0},{1,5},{5,1},{2,6},{6,2},{3,7},{7,3},{8,12},{12,8},{9,1... | collective-permute-start | bytes 393224 | tf_op jit(solution)/shard_map/ppermute | solution.py:243
  50.2 4.1 %collective-permute-done.9 = f32[8,32,128]{2,1,0:T(8,128)S(1)} collective-permute-done((f32[8,32,128]{2,1,0:T(8,128)S(1)}, f32[8,32,128]{2,1,0:T(8,128)S(1)}, u32[]{:S(2)}, u32[]{:S(2)}) %collective-permute-start.9) | collective-permute-done | bytes 131104 | tf_op jit(solution)/shard_map/ppermute | solution.py:243
  54.3 3.7 %collective-permute-start.12 = (bf16[8,32,128]{2,1,0:T(8,128)(2,1)S(1)}, bf16[8,32,128]{2,1,0:T(8,128)(2,1)S(1)}, u32[]{:S(2)}, u32[]{:S(2)}) collective-permute-start(bf16[8,32,128]{2,1,0:T(8,128)(2,1)S(1)} %add_convert_fusion.agg), channel_id=1, source_target_pairs={{0,2},{1,3},{2,0},{3,1},{4,6},{5,7},{6,4},{7,5},{8,10},{9,11},{10,... | collective-permute-start | bytes 196616 | tf_op jit(solution)/shard_map/ppermute | solution.py:231
  58.0 2.0 %collective-permute-start.10 = (bf16[8,32,128]{2,1,0:T(8,128)(2,1)S(1)}, bf16[8,32,128]{2,1,0:T(8,128)(2,1)S(1)}, u32[]{:S(2)}, u32[]{:S(2)}) collective-permute-start(bf16[8,32,128]{2,1,0:T(8,128)(2,1)S(1)} %add_convert_fusion.agg), channel_id=1, source_target_pairs={{0,1},{1,2},{2,3},{3,0},{4,5},{5,6},{6,7},{7,4},{8,9},{9,10},{10,1... | collective-permute-start | bytes 196616 | tf_op jit(solution)/shard_map/ppermute | solution.py:231
  60.0 0.2 collective-permute-done.12.agg_f
  60.3 2.0 %collective-permute-done.11.agg_r = bf16[8,32,128]{2,1,0:T(8,128)(2,1)S(1)} collective-permute-done((bf16[8,32,128]{2,1,0:T(8,128)(2,1)S(1)}, bf16[8,32,128]{2,1,0:T(8,128)(2,1)S(1)}, u32[]{:S(2)}, u32[]{:S(2)}) %collective-permute-start.11) | collective-permute-done | bytes 65568 | tf_op jit(solution)/shard_map/ppermute | solution.py:231
  62.3 0.0 collective-permute-done.10.agg_l
  62.3 4.7 %backward.1 = (bf16[1024,128]{1,0:T(8,128)(2,1)}, bf16[4,1056,128]{2,1,0:T(8,128)(2,1)S(1)}, bf16[2,1056,128]{2,1,0:T(8,128)(2,1)S(1)}, bf16[2,1056,128]{2,1,0:T(8,128)(2,1)S(1)}) custom-call(s32[4]{0:T(128)S(1)} %pad_add_fusion.ids, s32[128]{0:T(128)S(1)} %bitcast.41, s32[128]{0:T(128)S(1)} %bitcast.43, s32[128]{0:T(128)S(1)} %bitcast.45, s32[128]{0:T(128)S(1)} %bitcast.47, ...), custom_call_target="tpu_custom_call" | custom-call | tf_op jit(solution)/shard_map/backward/pallas_call | solution.py:257
  67.0 0.1 collective-permute-start.13
  67.1 0.5 collective-permute-start.14
  67.6 1.4 %collective-permute-done.13.got = bf16[2,1056,128]{2,1,0:T(8,128)(2,1)S(1)} collective-permute-done((bf16[2,1056,128]{2,1,0:T(8,128)(2,1)S(1)}, bf16[2,1056,128]{2,1,0:T(8,128)(2,1)S(1)}, u32[]{:S(2)}, u32[]{:S(2)}) %collective-permute-start.13) | collective-permute-done | bytes 540704 | tf_op jit(solution)/shard_map/ppermute | solution.py:243
  69.0 0.2 pair.2
  69.2 3.1 %collective-permute-start.17 = (bf16[1056,128]{1,0:T(8,128)(2,1)S(1)}, bf16[1056,128]{1,0:T(8,128)(2,1)S(1)}, u32[]{:S(2)}, u32[]{:S(2)}) collective-permute-start(bf16[1056,128]{1,0:T(8,128)(2,1)S(1)} %get-tuple-element.32), channel_id=1, source_target_pairs={{0,132},{128,0},{4,128},{132,4},{1,133},{129,1},{5,129},{133,5},{2... | collective-permute-start | bytes 811016 | tf_op jit(solution)/shard_map/ppermute | solution.py:239
  72.3 0.2 pair.3
  72.5 0.1 collective-permute-start.15
  72.6 2.2 %collective-permute-start.16 = (bf16[1056,128]{1,0:T(8,128)(2,1)S(1)}, bf16[1056,128]{1,0:T(8,128)(2,1)S(1)}, u32[]{:S(2)}, u32[]{:S(2)}) collective-permute-start(bf16[1056,128]{1,0:T(8,128)(2,1)S(1)} %get-tuple-element.31), channel_id=1, source_target_pairs={{0,4},{128,132},{4,0},{132,128},{1,5},{129,133},{5,1},{133,129},{2... | collective-permute-start | bytes 811016 | tf_op jit(solution)/shard_map/ppermute | solution.py:239
  74.7 9.4 %collective-permute-done.17.after = bf16[1056,128]{1,0:T(8,128)(2,1)S(1)} collective-permute-done((bf16[1056,128]{1,0:T(8,128)(2,1)S(1)}, bf16[1056,128]{1,0:T(8,128)(2,1)S(1)}, u32[]{:S(2)}, u32[]{:S(2)}) %collective-permute-start.17) | collective-permute-done | bytes 270368 | tf_op jit(solution)/shard_map/ppermute | solution.py:239
  84.1 3.7 %collective-permute-done.15.before = bf16[1056,128]{1,0:T(8,128)(2,1)S(1)} collective-permute-done((bf16[1056,128]{1,0:T(8,128)(2,1)S(1)}, bf16[1056,128]{1,0:T(8,128)(2,1)S(1)}, u32[]{:S(2)}, u32[]{:S(2)}) %collective-permute-start.15) | collective-permute-done | bytes 270368 | tf_op jit(solution)/shard_map/ppermute | solution.py:239
  87.8 0.1 y_sum.1
  87.9 19.8 %all_to_all.15.got = bf16[8,160,128]{2,1,0:T(8,128)(2,1)S(1)} all-to-all(bf16[8,160,128]{2,1,0:T(8,128)(2,1)S(1)} %y_sum.1), channel_id=1, replica_groups=mesh['yl'=2,'z'=8,'c'=2,'yh'=2,'x'=4] {'z'}, dimensions={0} | all-to-all | bytes 655360 | tf_op jit(solution)/shard_map/all_to_all | solution.py:247
  107.8 14.3 %all_to_all.16.got = bf16[8,160,128]{2,1,0:T(8,128)(2,1)S(1)} all-to-all(bf16[8,160,128]{2,1,0:T(8,128)(2,1)S(1)} %z_sum.1), channel_id=1, replica_groups=mesh['yl'=2,'z'=8,'c'=2,'yh'=2,'x'=4] {'yh','x'}, dimensions={0} | all-to-all | bytes 655360 | tf_op jit(solution)/shard_map/all_to_all | solution.py:247
  122.1 0.9 finish.1
  (27 shorter events, 0.2 us)
Async XLA Ops:
  0.6 26.6 %collective-permute-start.1 = (bf16[32,128,128]{2,1,0:T(8,128)(2,1)}, bf16[32,128,128]{2,1,0:T(8,128)(2,1)S(1)}, u32[]{:S(2)}, u32[]{:S(2)}) collective-permute-start(bf16[32,128,128]{2,1,0:T(8,128)(2,1)} %bitcast.36), channel_id=1, source_target_pairs={{0,3},{1,0},{2,1},{3,2},{4,7},{5,4},{6,5},{7,6},{8,11},{9,8},{10,9... | collective-permute-start | bytes 3145736 | tf_op jit(solution)/shard_map/ppermute | solution.py:231
  3.0 24.2 %collective-permute-start = (bf16[32,128,128]{2,1,0:T(8,128)(2,1)}, bf16[32,128,128]{2,1,0:T(8,128)(2,1)S(1)}, u32[]{:S(2)}, u32[]{:S(2)}) collective-permute-start(bf16[32,128,128]{2,1,0:T(8,128)(2,1)} %bitcast.37), channel_id=1, source_target_pairs={{0,1},{1,2},{2,3},{3,0},{4,5},{5,6},{6,7},{7,4},{8,9},{9,10},{10,1... | collective-permute-start | bytes 3145736 | tf_op jit(solution)/shard_map/ppermute | solution.py:231
  3.1 1.0 copy-start.4
  4.8 1.0 copy-start.3
  5.8 10.1 %copy-start.8 = (s32[1,1,32]{2,1,0:T(1,128)S(1)}, s32[1,1,32]{2,1,0:T(1,128)}, u32[]{:S(2)}) copy-start(s32[1,1,32]{2,1,0:T(1,128)} %param.11) | copy-start | bytes 388
  5.8 10.1 %copy-start.9 = (s32[1,1,32]{2,1,0:T(1,128)S(1)}, s32[1,1,32]{2,1,0:T(1,128)}, u32[]{:S(2)}) copy-start(s32[1,1,32]{2,1,0:T(1,128)} %param.10) | copy-start | bytes 388
  5.8 35.1 %all-to-all-start = ((bf16[16,256,128]{2,1,0:T(8,128)(2,1)}), bf16[16,256,128]{2,1,0:T(8,128)(2,1)S(1)}, u32[]{:S(2)}, u32[]{:S(2)}) async-start(bf16[16,256,128]{2,1,0:T(8,128)(2,1)} %copy-done.3), calls=%async_computation | async-start | bytes 2097152 | tf_op jit(solution)/shard_map/all_to_all | solution.py:247
  16.1 10.7 %collective-permute-start.4 = (s32[1,128]{1,0:T(1,128)S(1)}, s32[1,128]{1,0:T(1,128)S(1)}, u32[]{:S(2)}, u32[]{:S(2)}) collective-permute-start(s32[1,128]{1,0:T(1,128)S(1)} %pad_add_fusion.1), channel_id=1, source_target_pairs={{0,2},{1,3},{2,0},{3,1},{4,6},{5,7},{6,4},{7,5},{8,10},{9,11},{10,... | collective-permute-start | bytes 1544 | tf_op jit(solution)/shard_map/ppermute | solution.py:231
  19.4 7.3 %collective-permute-start.3 = (s32[1,128]{1,0:T(1,128)S(1)}, s32[1,128]{1,0:T(1,128)S(1)}, u32[]{:S(2)}, u32[]{:S(2)}) collective-permute-start(s32[1,128]{1,0:T(1,128)S(1)} %pad_add_fusion.1), channel_id=1, source_target_pairs={{0,3},{1,0},{2,1},{3,2},{4,7},{5,4},{6,5},{7,6},{8,11},{9,8},{10,9... | collective-permute-start | bytes 1544 | tf_op jit(solution)/shard_map/ppermute | solution.py:231
  19.7 7.5 %collective-permute-start.2 = (s32[1,128]{1,0:T(1,128)S(1)}, s32[1,128]{1,0:T(1,128)S(1)}, u32[]{:S(2)}, u32[]{:S(2)}) collective-permute-start(s32[1,128]{1,0:T(1,128)S(1)} %pad_add_fusion.1), channel_id=1, source_target_pairs={{0,1},{1,2},{2,3},{3,0},{4,5},{5,6},{6,7},{7,4},{8,9},{9,10},{10,1... | collective-permute-start | bytes 1544 | tf_op jit(solution)/shard_map/ppermute | solution.py:231
  28.3 1.0 copy-start.1
  29.2 14.5 %copy-start = (bf16[1,1,32,128,128]{4,3,2,1,0:T(8,128)(2,1)S(1)}, bf16[1,1,32,128,128]{4,3,2,1,0:T(8,128)(2,1)}, u32[]{:S(2)}) copy-start(bf16[1,1,32,128,128]{4,3,2,1,0:T(8,128)(2,1)} %param.9) | copy-start | bytes 3145732
  29.2 13.9 %collective-permute-start.5 = (bf16[16,128,128]{2,1,0:T(8,128)(2,1)}, bf16[16,128,128]{2,1,0:T(8,128)(2,1)}, u32[]{:S(2)}, u32[]{:S(2)}) collective-permute-start(bf16[16,128,128]{2,1,0:T(8,128)(2,1)} %get-tuple-element.23), channel_id=1, source_target_pairs={{0,1},{1,2},{2,3},{3,0},{4,5},{5,6},{6,7},{7,4},{8,9},{9,10},{10,1... | collective-permute-start | bytes 1572872 | tf_op jit(solution)/shard_map/ppermute | solution.py:231
  30.6 12.5 %collective-permute-start.6 = (bf16[16,128,128]{2,1,0:T(8,128)(2,1)}, bf16[16,128,128]{2,1,0:T(8,128)(2,1)}, u32[]{:S(2)}, u32[]{:S(2)}) collective-permute-start(bf16[16,128,128]{2,1,0:T(8,128)(2,1)} %get-tuple-element.24), channel_id=1, source_target_pairs={{0,3},{1,0},{2,1},{3,2},{4,7},{5,4},{6,5},{7,6},{8,11},{9,8},{10,9... | collective-permute-start | bytes 1572872 | tf_op jit(solution)/shard_map/ppermute | solution.py:231
  40.9 2.8 %copy-start.2 = (bf16[32,128,128]{2,1,0:T(8,128)(2,1)S(1)}, bf16[32,128,128]{2,1,0:T(8,128)(2,1)}, u32[]{:S(2)}) copy-start(bf16[32,128,128]{2,1,0:T(8,128)(2,1)} %copy-done.1) | copy-start | bytes 3145732
  41.0 2.1 %collective-permute-start.7 = (bf16[64,32,128]{2,1,0:T(8,128)(2,1)S(1)}, bf16[64,32,128]{2,1,0:T(8,128)(2,1)S(1)}, u32[]{:S(2)}, u32[]{:S(2)}) collective-permute-start(bf16[64,32,128]{2,1,0:T(8,128)(2,1)S(1)} %bitcast.50), channel_id=1, source_target_pairs={{0,8},{8,0},{1,9},{9,1},{2,10},{10,2},{3,11},{11,3},{4,12},{12,4},... | collective-permute-start | bytes 1572872 | tf_op jit(solution)/shard_map/ppermute | solution.py:243
  41.1 2.6 %collective-permute-start.8 = (bf16[64,32,128]{2,1,0:T(8,128)(2,1)S(1)}, bf16[64,32,128]{2,1,0:T(8,128)(2,1)S(1)}, u32[]{:S(2)}, u32[]{:S(2)}) collective-permute-start(bf16[64,32,128]{2,1,0:T(8,128)(2,1)S(1)} %bitcast.49), channel_id=1, source_target_pairs={{0,8},{8,0},{1,9},{9,1},{2,10},{10,2},{3,11},{11,3},{4,12},{12,4},... | collective-permute-start | bytes 1572872 | tf_op jit(solution)/shard_map/ppermute | solution.py:243
  43.8 18.5 %copy-start.5 = (bf16[1024,128]{1,0:T(8,128)(2,1)S(1)}, bf16[1024,128]{1,0:T(8,128)(2,1)}, u32[]{:S(2)}) copy-start(bf16[1024,128]{1,0:T(8,128)(2,1)} %cot.1) | copy-start | bytes 786436
  43.8 18.5 %copy-start.6 = (bf16[128,128]{1,0:T(8,128)(2,1)S(1)}, bf16[128,128]{1,0:T(8,128)(2,1)}, u32[]{:S(2)}) copy-start(bf16[128,128]{1,0:T(8,128)(2,1)} %weight.1) | copy-start | bytes 98308
  43.8 18.5 %copy-start.7 = (f32[128]{0:T(128)S(1)}, f32[128]{0:T(128)}, u32[]{:S(2)}) copy-start(f32[128]{0:T(128)} %param.14) | copy-start | bytes 1540
  47.2 7.1 %collective-permute-start.9 = (f32[8,32,128]{2,1,0:T(8,128)S(1)}, f32[8,32,128]{2,1,0:T(8,128)S(1)}, u32[]{:S(2)}, u32[]{:S(2)}) collective-permute-start(f32[8,32,128]{2,1,0:T(8,128)S(1)} %forward.1), channel_id=1, source_target_pairs={{0,4},{4,0},{1,5},{5,1},{2,6},{6,2},{3,7},{7,3},{8,12},{12,8},{9,1... | collective-permute-start | bytes 393224 | tf_op jit(solution)/shard_map/ppermute | solution.py:243
  54.3 5.9 %collective-permute-start.12 = (bf16[8,32,128]{2,1,0:T(8,128)(2,1)S(1)}, bf16[8,32,128]{2,1,0:T(8,128)(2,1)S(1)}, u32[]{:S(2)}, u32[]{:S(2)}) collective-permute-start(bf16[8,32,128]{2,1,0:T(8,128)(2,1)S(1)} %add_convert_fusion.agg), channel_id=1, source_target_pairs={{0,2},{1,3},{2,0},{3,1},{4,6},{5,7},{6,4},{7,5},{8,10},{9,11},{10,... | collective-permute-start | bytes 196616 | tf_op jit(solution)/shard_map/ppermute | solution.py:231
  58.0 4.3 %collective-permute-start.11 = (bf16[8,32,128]{2,1,0:T(8,128)(2,1)S(1)}, bf16[8,32,128]{2,1,0:T(8,128)(2,1)S(1)}, u32[]{:S(2)}, u32[]{:S(2)}) collective-permute-start(bf16[8,32,128]{2,1,0:T(8,128)(2,1)S(1)} %add_convert_fusion.agg), channel_id=1, source_target_pairs={{0,3},{1,0},{2,1},{3,2},{4,7},{5,4},{6,5},{7,6},{8,11},{9,8},{10,9... | collective-permute-start | bytes 196616 | tf_op jit(solution)/shard_map/ppermute | solution.py:231
  58.0 4.3 %collective-permute-start.10 = (bf16[8,32,128]{2,1,0:T(8,128)(2,1)S(1)}, bf16[8,32,128]{2,1,0:T(8,128)(2,1)S(1)}, u32[]{:S(2)}, u32[]{:S(2)}) collective-permute-start(bf16[8,32,128]{2,1,0:T(8,128)(2,1)S(1)} %add_convert_fusion.agg), channel_id=1, source_target_pairs={{0,1},{1,2},{2,3},{3,0},{4,5},{5,6},{6,7},{7,4},{8,9},{9,10},{10,1... | collective-permute-start | bytes 196616 | tf_op jit(solution)/shard_map/ppermute | solution.py:231
  67.0 2.0 %collective-permute-start.13 = (bf16[2,1056,128]{2,1,0:T(8,128)(2,1)S(1)}, bf16[2,1056,128]{2,1,0:T(8,128)(2,1)S(1)}, u32[]{:S(2)}, u32[]{:S(2)}) collective-permute-start(bf16[2,1056,128]{2,1,0:T(8,128)(2,1)S(1)} %get-tuple-element.27), channel_id=1, source_target_pairs={{0,8},{8,0},{1,9},{9,1},{2,10},{10,2},{3,11},{11,3},{4,12},{12,4},... | collective-permute-start | bytes 1622024 | tf_op jit(solution)/shard_map/ppermute | solution.py:243
  67.1 5.2 %collective-permute-start.14 = (bf16[2,1056,128]{2,1,0:T(8,128)(2,1)S(1)}, bf16[2,1056,128]{2,1,0:T(8,128)(2,1)S(1)}, u32[]{:S(2)}, u32[]{:S(2)}) collective-permute-start(bf16[2,1056,128]{2,1,0:T(8,128)(2,1)S(1)} %get-tuple-element.29), channel_id=1, source_target_pairs={{0,8},{8,0},{1,9},{9,1},{2,10},{10,2},{3,11},{11,3},{4,12},{12,4},... | collective-permute-start | bytes 1622024 | tf_op jit(solution)/shard_map/ppermute | solution.py:243
  69.2 14.9 %collective-permute-start.17 = (bf16[1056,128]{1,0:T(8,128)(2,1)S(1)}, bf16[1056,128]{1,0:T(8,128)(2,1)S(1)}, u32[]{:S(2)}, u32[]{:S(2)}) collective-permute-start(bf16[1056,128]{1,0:T(8,128)(2,1)S(1)} %get-tuple-element.32), channel_id=1, source_target_pairs={{0,132},{128,0},{4,128},{132,4},{1,133},{129,1},{5,129},{133,5},{2... | collective-permute-start | bytes 811016 | tf_op jit(solution)/shard_map/ppermute | solution.py:239
  72.5 15.3 %collective-permute-start.15 = (bf16[1056,128]{1,0:T(8,128)(2,1)S(1)}, bf16[1056,128]{1,0:T(8,128)(2,1)S(1)}, u32[]{:S(2)}, u32[]{:S(2)}) collective-permute-start(bf16[1056,128]{1,0:T(8,128)(2,1)S(1)} %get-tuple-element.30), channel_id=1, source_target_pairs={{0,128},{128,4},{4,132},{132,0},{1,129},{129,5},{5,133},{133,1},{2... | collective-permute-start | bytes 811016 | tf_op jit(solution)/shard_map/ppermute | solution.py:239
  72.6 15.2 %collective-permute-start.16 = (bf16[1056,128]{1,0:T(8,128)(2,1)S(1)}, bf16[1056,128]{1,0:T(8,128)(2,1)S(1)}, u32[]{:S(2)}, u32[]{:S(2)}) collective-permute-start(bf16[1056,128]{1,0:T(8,128)(2,1)S(1)} %get-tuple-element.31), channel_id=1, source_target_pairs={{0,4},{128,132},{4,0},{132,128},{1,5},{129,133},{5,1},{133,129},{2... | collective-permute-start | bytes 811016 | tf_op jit(solution)/shard_map/ppermute | solution.py:239

commit v5 on v4

--- a/solution.py
+++ b/solution.py
@@ -30,6 +30,7 @@
 GRADS = THIN // 2
 EXTRA = 32
 SWAPS = 2
+PARTS = 4
 PIECE = NZ * LAST
 META = 4 * SLOTS
 RELAY_COST = pl.CostEstimate(flops=14 * 10**9, bytes_accessed=42 * 10**6, transcendentals=0)
@@ -64,12 +65,21 @@
             target[index] += prod
 
 
-def relay_kernel(left, right, meta_l, meta_r, meta_f, out_a, out_b, out_l, out_r, out_f):
-    out_a[...] = left[0:HALF]
-    out_b[...] = right[HALF:SLOTS]
+def relay_kernel(left, right, meta_l, meta_r, meta_f, out_a, out_b, out_l, out_r, out_f, sem):
+    copies = []
+    step = HALF // PARTS
+    for k in range(PARTS):
+        to = pl.ds(k * step, step)
+        from_b = pl.ds(HALF + k * step, step)
+        copies.append(pltpu.make_async_copy(left.at[to], out_a.at[to], sem.at[0, k]))
+        copies.append(pltpu.make_async_copy(right.at[from_b], out_b.at[to], sem.at[1, k]))
+    for copy in copies:
+        copy.start()
     out_l[...] = meta_l[...]
     out_r[...] = meta_r[...]
     out_f[...] = meta_f[...]
+    for copy in copies:
+        copy.wait()
 
 
 def fetch_far(far_a, far_b, far, far_sem):
@@ -193,19 +203,26 @@
         out[r] = total
 
 
-def finish_kernel(got, grad, wgrad, bgrad):
+def finish_kernel(got, grad, wgrad, bgrad, blocks, sem):
+    copies = []
     for t in range(ROW_TILES):
         first = (t // BLOCK_HALF) * NX
         at = (t % BLOCK_HALF) * THIN
         block = jnp.concatenate(
             [got[first + x, at : at + THIN, :].astype(F32) for x in range(NX)], axis=0
         )
-        grad[t * TILE : (t + 1) * TILE, :] = block.T
+        blocks[t] = block.T
+        copies.append(
+            pltpu.make_async_copy(blocks.at[t], grad.at[pl.ds(t * TILE, TILE)], sem.at[t])
+        )
+        copies[t].start()
     for yh in range(2):
         for x in range(NX):
             to = x * THIN + yh * GRADS
             wgrad[to : to + GRADS, :] = got[yh * NX + x, LAST : LAST + GRADS, :].astype(F32)
     bgrad[...] = got[0, LAST + GRADS : LAST + EXTRA, :].astype(F32)[0:1, :]
+    for copy in copies:
+        copy.wait()
 
 
 def slot_meta(rows, cols, count, core, y):
@@ -290,7 +307,7 @@
         "relay",
         [half, half, line, line, line],
         0,
-        [],
+        [pltpu.SemaphoreType.DMA((2, PARTS))],
         6,
         left,
         right,
@@ -298,6 +315,8 @@
         rotate(own_meta, NX - 1),
         rotate(own_meta, 2),
         cost=RELAY_COST,
+        loose_in=(0, 1),
+        loose_out=(0, 1),
     )
     metas = [m.reshape(META) for m in (own_meta, *metas)]
     far_a, far_b = rotate(pass_a, 1), rotate(pass_b, NX - 1)
@@ -369,9 +388,10 @@
         "finish",
         [((ROW_TILES * TILE, WIDE), F32), ((WIDE, WIDE), F32), ((1, WIDE), F32)],
         0,
-        [],
+        [pltpu.VMEM((ROW_TILES, TILE, WIDE), F32), pltpu.SemaphoreType.DMA((ROW_TILES,))],
         16,
         got,
+        loose_out=(0,),
     )
     return (activations, feature_grad, weight_grad, bias_grad.reshape(WIDE))
 

time: 123 us -> 124 us (level)
  no operation moved by 1% of the time
where the time goes in v5:
time: 124 us
  waiting for transfers between devices  37.5 us (30%)
  starting transfers between devices  35.4 us (29%)
  blocking collectives  34.2 us (28%)
  Pallas kernels  12 us (10%)
  local copies, waits for them, and re-layouts  2.98 us (2%)
  between operations  1.62 us (1%)
    all_to_all x2, blocking collectives, exchange(): return lax.all_to_all(value, axes, 0, 0, tiled=True)  34.2 us
    ppermute x10, starting transfers between devices, rotate(): return lax.ppermute(value, 'x', [(k, (k + step) % NX) for k in range(NX)])  16.3 us
    ppermute x3, waiting for transfers between devices, along_y(): return lax.ppermute(value, ('yl', 'yh'), pairs)  13 us
    pallas_call x9, Pallas kernels, kernel_call(): pl.pallas_call(body, out_shape=[jax.ShapeDtypeStruct(s, d) for s, d in sh...  12 us
    ppermute x10, waiting for transfers between devices, rotate(): return lax.ppermute(value, 'x', [(k, (k + step) % NX) for k in range(NX)])  9.5 us
    all_to_all x1, starting transfers between devices, exchange(): return lax.all_to_all(value, axes, 0, 0, tiled=True)  9.47 us
    all_to_all x1, waiting for transfers between devices, exchange(): return lax.all_to_all(value, axes, 0, 0, tiled=True)  8.76 us
    ppermute x5, waiting for transfers between devices, swap(): return lax.ppermute(value, axis, [(0, 1), (1, 0)])  6.17 us
  transfers between devices with their start and end apart: 19, of which 11 were waited for; matrix products, arithmetic and copies ran while one was open for 0% of the time, Pallas kernels for 2%

profile of v5, /device:TPU:2, one launch (start us, length us, event | category | flops | bytes accessed | tf_op | source)
XLA Modules:
  0.0 123.9 jit_solution(8449289072397311343)
XLA Ops:
  0.6 2.3 %collective-permute-start.1 = (bf16[32,128,128]{2,1,0:T(8,128)(2,1)}, bf16[32,128,128]{2,1,0:T(8,128)(2,1)S(1)}, u32[]{:S(2)}, u32[]{:S(2)}) collective-permute-start(bf16[32,128,128]{2,1,0:T(8,128)(2,1)} %bitcast.36), channel_id=1, source_target_pairs={{0,3},{1,0},{2,1},{3,2},{4,7},{5,4},{6,5},{7,6},{8,11},{9,8},{10,9... | collective-permute-start | bytes 3145736 | tf_op jit(solution)/shard_map/ppermute | solution.py:248
  3.0 0.0 collective-permute-start
  3.0 0.1 pad_add_fusion.ids
  3.1 0.9 copy-done.4
  4.0 0.8 prep.1
  4.8 0.9 copy-done.3
  5.8 9.5 %all-to-all-start = ((bf16[16,256,128]{2,1,0:T(8,128)(2,1)}), bf16[16,256,128]{2,1,0:T(8,128)(2,1)S(1)}, u32[]{:S(2)}, u32[]{:S(2)}) async-start(bf16[16,256,128]{2,1,0:T(8,128)(2,1)} %copy-done.3), calls=%async_computation | async-start | bytes 2097152 | tf_op jit(solution)/shard_map/all_to_all | solution.py:264
  16.0 0.1 pad_add_fusion.1
  16.1 3.4 %collective-permute-start.4 = (s32[1,128]{1,0:T(1,128)S(1)}, s32[1,128]{1,0:T(1,128)S(1)}, u32[]{:S(2)}, u32[]{:S(2)}) collective-permute-start(s32[1,128]{1,0:T(1,128)S(1)} %pad_add_fusion.1), channel_id=1, source_target_pairs={{0,2},{1,3},{2,0},{3,1},{4,6},{5,7},{6,4},{7,5},{8,10},{9,11},{10,... | collective-permute-start | bytes 1544 | tf_op jit(solution)/shard_map/ppermute | solution.py:248
  19.4 0.2 collective-permute-start.3
  19.7 1.8 %collective-permute-start.2 = (s32[1,128]{1,0:T(1,128)S(1)}, s32[1,128]{1,0:T(1,128)S(1)}, u32[]{:S(2)}, u32[]{:S(2)}) collective-permute-start(s32[1,128]{1,0:T(1,128)S(1)} %pad_add_fusion.1), channel_id=1, source_target_pairs={{0,1},{1,2},{2,3},{3,0},{4,5},{5,6},{6,7},{7,4},{8,9},{9,10},{10,1... | collective-permute-start | bytes 1544 | tf_op jit(solution)/shard_map/ppermute | solution.py:248
  21.5 5.3 %collective-permute-done.4.meta_f = s32[1,128]{1,0:T(1,128)S(1)} collective-permute-done((s32[1,128]{1,0:T(1,128)S(1)}, s32[1,128]{1,0:T(1,128)S(1)}, u32[]{:S(2)}, u32[]{:S(2)}) %collective-permute-start.4) | collective-permute-done | bytes 544 | tf_op jit(solution)/shard_map/ppermute | solution.py:248
  26.7 0.5 collective-permute-done.2.meta_l
  27.2 0.0 collective-permute-done.1.right
  27.2 1.0 relay.1
  28.3 1.0 copy-done.1
  29.2 1.4 %collective-permute-start.5 = (bf16[16,128,128]{2,1,0:T(8,128)(2,1)}, bf16[16,128,128]{2,1,0:T(8,128)(2,1)}, u32[]{:S(2)}, u32[]{:S(2)}) collective-permute-start(bf16[16,128,128]{2,1,0:T(8,128)(2,1)} %get-tuple-element.23), channel_id=1, source_target_pairs={{0,1},{1,2},{2,3},{3,0},{4,5},{5,6},{6,7},{7,4},{8,9},{9,10},{10,1... | collective-permute-start | bytes 1572872 | tf_op jit(solution)/shard_map/ppermute | solution.py:248
  30.6 1.5 %collective-permute-start.6 = (bf16[16,128,128]{2,1,0:T(8,128)(2,1)}, bf16[16,128,128]{2,1,0:T(8,128)(2,1)}, u32[]{:S(2)}, u32[]{:S(2)}) collective-permute-start(bf16[16,128,128]{2,1,0:T(8,128)(2,1)} %get-tuple-element.24), channel_id=1, source_target_pairs={{0,3},{1,0},{2,1},{3,2},{4,7},{5,4},{6,5},{7,6},{8,11},{9,8},{10,9... | collective-permute-start | bytes 1572872 | tf_op jit(solution)/shard_map/ppermute | solution.py:248
  32.2 8.8 %all-to-all-done = bf16[16,256,128]{2,1,0:T(8,128)(2,1)S(1)} async-done(((bf16[16,256,128]{2,1,0:T(8,128)(2,1)}), bf16[16,256,128]{2,1,0:T(8,128)(2,1)S(1)}, u32[]{:S(2)}, u32[]{:S(2)}) %all-to-all-start) | async-done | bytes 1048608 | tf_op jit(solution)/shard_map/all_to_all | solution.py:264
  40.9 0.1 fusion.4
  41.0 0.1 collective-permute-start.7
  41.1 0.5 collective-permute-start.8
  41.6 1.5 %collective-permute-done.5.far_a = bf16[16,128,128]{2,1,0:T(8,128)(2,1)} collective-permute-done((bf16[16,128,128]{2,1,0:T(8,128)(2,1)}, bf16[16,128,128]{2,1,0:T(8,128)(2,1)}, u32[]{:S(2)}, u32[]{:S(2)}) %collective-permute-start.5) | collective-permute-done | bytes 524320 | tf_op jit(solution)/shard_map/ppermute | solution.py:248
  43.1 0.6 collective-permute-done.8.rest_1_
  43.8 0.0 copy-start.7
  43.8 3.4 %forward.1 = f32[8,32,128]{2,1,0:T(8,128)S(1)} custom-call(s32[128]{0:T(128)S(1)} %bitcast.40, s32[128]{0:T(128)S(1)} %bitcast.42, s32[128]{0:T(128)S(1)} %bitcast.44, s32[128]{0:T(128)S(1)} %bitcast.46, bf16[32,128,128]{2,1,0:T(8,128)(2,1)S(1)} %bitcast.38, bf16[32,128,128]{2,1,0:T(8,128)(2,1)S(1)} %copy-done.2, ...), custom_call_target="tpu_custom_call" | custom-call | tf_op jit(solution)/shard_map/forward/pallas_call | solution.py:274
  47.2 3.0 %collective-permute-start.9 = (f32[8,32,128]{2,1,0:T(8,128)S(1)}, f32[8,32,128]{2,1,0:T(8,128)S(1)}, u32[]{:S(2)}, u32[]{:S(2)}) collective-permute-start(f32[8,32,128]{2,1,0:T(8,128)S(1)} %forward.1), channel_id=1, source_target_pairs={{0,4},{4,0},{1,5},{5,1},{2,6},{6,2},{3,7},{7,3},{8,12},{12,8},{9,1... | collective-permute-start | bytes 393224 | tf_op jit(solution)/shard_map/ppermute | solution.py:260
  50.2 4.1 %collective-permute-done.9 = f32[8,32,128]{2,1,0:T(8,128)S(1)} collective-permute-done((f32[8,32,128]{2,1,0:T(8,128)S(1)}, f32[8,32,128]{2,1,0:T(8,128)S(1)}, u32[]{:S(2)}, u32[]{:S(2)}) %collective-permute-start.9) | collective-permute-done | bytes 131104 | tf_op jit(solution)/shard_map/ppermute | solution.py:260
  54.3 3.7 %collective-permute-start.12 = (bf16[8,32,128]{2,1,0:T(8,128)(2,1)S(1)}, bf16[8,32,128]{2,1,0:T(8,128)(2,1)S(1)}, u32[]{:S(2)}, u32[]{:S(2)}) collective-permute-start(bf16[8,32,128]{2,1,0:T(8,128)(2,1)S(1)} %add_convert_fusion.agg), channel_id=1, source_target_pairs={{0,2},{1,3},{2,0},{3,1},{4,6},{5,7},{6,4},{7,5},{8,10},{9,11},{10,... | collective-permute-start | bytes 196616 | tf_op jit(solution)/shard_map/ppermute | solution.py:248
  58.0 2.0 %collective-permute-start.10 = (bf16[8,32,128]{2,1,0:T(8,128)(2,1)S(1)}, bf16[8,32,128]{2,1,0:T(8,128)(2,1)S(1)}, u32[]{:S(2)}, u32[]{:S(2)}) collective-permute-start(bf16[8,32,128]{2,1,0:T(8,128)(2,1)S(1)} %add_convert_fusion.agg), channel_id=1, source_target_pairs={{0,1},{1,2},{2,3},{3,0},{4,5},{5,6},{6,7},{7,4},{8,9},{9,10},{10,1... | collective-permute-start | bytes 196616 | tf_op jit(solution)/shard_map/ppermute | solution.py:248
  60.0 0.2 collective-permute-done.12.agg_f
  60.3 2.0 %collective-permute-done.11.agg_r = bf16[8,32,128]{2,1,0:T(8,128)(2,1)S(1)} collective-permute-done((bf16[8,32,128]{2,1,0:T(8,128)(2,1)S(1)}, bf16[8,32,128]{2,1,0:T(8,128)(2,1)S(1)}, u32[]{:S(2)}, u32[]{:S(2)}) %collective-permute-start.11) | collective-permute-done | bytes 65568 | tf_op jit(solution)/shard_map/ppermute | solution.py:248
  62.3 0.0 collective-permute-done.10.agg_l
  62.3 4.7 %backward.1 = (bf16[1024,128]{1,0:T(8,128)(2,1)}, bf16[4,1056,128]{2,1,0:T(8,128)(2,1)S(1)}, bf16[2,1056,128]{2,1,0:T(8,128)(2,1)S(1)}, bf16[2,1056,128]{2,1,0:T(8,128)(2,1)S(1)}) custom-call(s32[4]{0:T(128)S(1)} %pad_add_fusion.ids, s32[128]{0:T(128)S(1)} %bitcast.41, s32[128]{0:T(128)S(1)} %bitcast.43, s32[128]{0:T(128)S(1)} %bitcast.45, s32[128]{0:T(128)S(1)} %bitcast.47, ...), custom_call_target="tpu_custom_call" | custom-call | tf_op jit(solution)/shard_map/backward/pallas_call | solution.py:274
  67.0 0.1 collective-permute-start.13
  67.1 0.5 collective-permute-start.14
  67.6 1.4 %collective-permute-done.13.got = bf16[2,1056,128]{2,1,0:T(8,128)(2,1)S(1)} collective-permute-done((bf16[2,1056,128]{2,1,0:T(8,128)(2,1)S(1)}, bf16[2,1056,128]{2,1,0:T(8,128)(2,1)S(1)}, u32[]{:S(2)}, u32[]{:S(2)}) %collective-permute-start.13) | collective-permute-done | bytes 540704 | tf_op jit(solution)/shard_map/ppermute | solution.py:260
  69.0 0.2 pair.2
  69.2 3.1 %collective-permute-start.17 = (bf16[1056,128]{1,0:T(8,128)(2,1)S(1)}, bf16[1056,128]{1,0:T(8,128)(2,1)S(1)}, u32[]{:S(2)}, u32[]{:S(2)}) collective-permute-start(bf16[1056,128]{1,0:T(8,128)(2,1)S(1)} %get-tuple-element.32), channel_id=1, source_target_pairs={{0,132},{128,0},{4,128},{132,4},{1,133},{129,1},{5,129},{133,5},{2... | collective-permute-start | bytes 811016 | tf_op jit(solution)/shard_map/ppermute | solution.py:256
  72.3 0.2 pair.3
  72.4 0.1 collective-permute-start.15
  72.5 2.2 %collective-permute-start.16 = (bf16[1056,128]{1,0:T(8,128)(2,1)S(1)}, bf16[1056,128]{1,0:T(8,128)(2,1)S(1)}, u32[]{:S(2)}, u32[]{:S(2)}) collective-permute-start(bf16[1056,128]{1,0:T(8,128)(2,1)S(1)} %get-tuple-element.31), channel_id=1, source_target_pairs={{0,4},{128,132},{4,0},{132,128},{1,5},{129,133},{5,1},{133,129},{2... | collective-permute-start | bytes 811016 | tf_op jit(solution)/shard_map/ppermute | solution.py:256
  74.7 9.4 %collective-permute-done.17.after = bf16[1056,128]{1,0:T(8,128)(2,1)S(1)} collective-permute-done((bf16[1056,128]{1,0:T(8,128)(2,1)S(1)}, bf16[1056,128]{1,0:T(8,128)(2,1)S(1)}, u32[]{:S(2)}, u32[]{:S(2)}) %collective-permute-start.17) | collective-permute-done | bytes 270368 | tf_op jit(solution)/shard_map/ppermute | solution.py:256
  84.1 3.7 %collective-permute-done.15.before = bf16[1056,128]{1,0:T(8,128)(2,1)S(1)} collective-permute-done((bf16[1056,128]{1,0:T(8,128)(2,1)S(1)}, bf16[1056,128]{1,0:T(8,128)(2,1)S(1)}, u32[]{:S(2)}, u32[]{:S(2)}) %collective-permute-start.15) | collective-permute-done | bytes 270368 | tf_op jit(solution)/shard_map/ppermute | solution.py:256
  87.8 0.1 y_sum.1
  87.9 19.8 %all_to_all.15.got = bf16[8,160,128]{2,1,0:T(8,128)(2,1)S(1)} all-to-all(bf16[8,160,128]{2,1,0:T(8,128)(2,1)S(1)} %y_sum.1), channel_id=1, replica_groups=mesh['yl'=2,'z'=8,'c'=2,'yh'=2,'x'=4] {'z'}, dimensions={0} | all-to-all | bytes 655360 | tf_op jit(solution)/shard_map/all_to_all | solution.py:264
  107.8 14.3 %all_to_all.16.got = bf16[8,160,128]{2,1,0:T(8,128)(2,1)S(1)} all-to-all(bf16[8,160,128]{2,1,0:T(8,128)(2,1)S(1)} %z_sum.1), channel_id=1, replica_groups=mesh['yl'=2,'z'=8,'c'=2,'yh'=2,'x'=4] {'yh','x'}, dimensions={0} | all-to-all | bytes 655360 | tf_op jit(solution)/shard_map/all_to_all | solution.py:264
  122.1 1.6 %finish.1 = (f32[1024,128]{1,0:T(8,128)}, f32[128,128]{1,0:T(8,128)}, f32[1,128]{1,0:T(1,128)}) custom-call(bf16[8,160,128]{2,1,0:T(8,128)(2,1)S(1)} %all_to_all.16.got), custom_call_target="tpu_custom_call" | custom-call | tf_op jit(solution)/shard_map/finish/pallas_call | solution.py:274
  (27 shorter events, 0.2 us)
Async XLA Ops:
  0.6 26.6 %collective-permute-start.1 = (bf16[32,128,128]{2,1,0:T(8,128)(2,1)}, bf16[32,128,128]{2,1,0:T(8,128)(2,1)S(1)}, u32[]{:S(2)}, u32[]{:S(2)}) collective-permute-start(bf16[32,128,128]{2,1,0:T(8,128)(2,1)} %bitcast.36), channel_id=1, source_target_pairs={{0,3},{1,0},{2,1},{3,2},{4,7},{5,4},{6,5},{7,6},{8,11},{9,8},{10,9... | collective-permute-start | bytes 3145736 | tf_op jit(solution)/shard_map/ppermute | solution.py:248
  3.0 24.2 %collective-permute-start = (bf16[32,128,128]{2,1,0:T(8,128)(2,1)}, bf16[32,128,128]{2,1,0:T(8,128)(2,1)S(1)}, u32[]{:S(2)}, u32[]{:S(2)}) collective-permute-start(bf16[32,128,128]{2,1,0:T(8,128)(2,1)} %bitcast.37), channel_id=1, source_target_pairs={{0,1},{1,2},{2,3},{3,0},{4,5},{5,6},{6,7},{7,4},{8,9},{9,10},{10,1... | collective-permute-start | bytes 3145736 | tf_op jit(solution)/shard_map/ppermute | solution.py:248
  3.1 1.0 copy-start.4
  4.8 1.0 copy-start.3
  5.8 10.1 %copy-start.8 = (s32[1,1,32]{2,1,0:T(1,128)S(1)}, s32[1,1,32]{2,1,0:T(1,128)}, u32[]{:S(2)}) copy-start(s32[1,1,32]{2,1,0:T(1,128)} %param.11) | copy-start | bytes 388
  5.8 10.1 %copy-start.9 = (s32[1,1,32]{2,1,0:T(1,128)S(1)}, s32[1,1,32]{2,1,0:T(1,128)}, u32[]{:S(2)}) copy-start(s32[1,1,32]{2,1,0:T(1,128)} %param.10) | copy-start | bytes 388
  5.8 35.1 %all-to-all-start = ((bf16[16,256,128]{2,1,0:T(8,128)(2,1)}), bf16[16,256,128]{2,1,0:T(8,128)(2,1)S(1)}, u32[]{:S(2)}, u32[]{:S(2)}) async-start(bf16[16,256,128]{2,1,0:T(8,128)(2,1)} %copy-done.3), calls=%async_computation | async-start | bytes 2097152 | tf_op jit(solution)/shard_map/all_to_all | solution.py:264
  16.1 10.7 %collective-permute-start.4 = (s32[1,128]{1,0:T(1,128)S(1)}, s32[1,128]{1,0:T(1,128)S(1)}, u32[]{:S(2)}, u32[]{:S(2)}) collective-permute-start(s32[1,128]{1,0:T(1,128)S(1)} %pad_add_fusion.1), channel_id=1, source_target_pairs={{0,2},{1,3},{2,0},{3,1},{4,6},{5,7},{6,4},{7,5},{8,10},{9,11},{10,... | collective-permute-start | bytes 1544 | tf_op jit(solution)/shard_map/ppermute | solution.py:248
  19.4 7.3 %collective-permute-start.3 = (s32[1,128]{1,0:T(1,128)S(1)}, s32[1,128]{1,0:T(1,128)S(1)}, u32[]{:S(2)}, u32[]{:S(2)}) collective-permute-start(s32[1,128]{1,0:T(1,128)S(1)} %pad_add_fusion.1), channel_id=1, source_target_pairs={{0,3},{1,0},{2,1},{3,2},{4,7},{5,4},{6,5},{7,6},{8,11},{9,8},{10,9... | collective-permute-start | bytes 1544 | tf_op jit(solution)/shard_map/ppermute | solution.py:248
  19.7 7.5 %collective-permute-start.2 = (s32[1,128]{1,0:T(1,128)S(1)}, s32[1,128]{1,0:T(1,128)S(1)}, u32[]{:S(2)}, u32[]{:S(2)}) collective-permute-start(s32[1,128]{1,0:T(1,128)S(1)} %pad_add_fusion.1), channel_id=1, source_target_pairs={{0,1},{1,2},{2,3},{3,0},{4,5},{5,6},{6,7},{7,4},{8,9},{9,10},{10,1... | collective-permute-start | bytes 1544 | tf_op jit(solution)/shard_map/ppermute | solution.py:248
  28.2 1.0 copy-start.1
  29.2 14.5 %copy-start = (bf16[1,1,32,128,128]{4,3,2,1,0:T(8,128)(2,1)S(1)}, bf16[1,1,32,128,128]{4,3,2,1,0:T(8,128)(2,1)}, u32[]{:S(2)}) copy-start(bf16[1,1,32,128,128]{4,3,2,1,0:T(8,128)(2,1)} %param.9) | copy-start | bytes 3145732
  29.2 13.9 %collective-permute-start.5 = (bf16[16,128,128]{2,1,0:T(8,128)(2,1)}, bf16[16,128,128]{2,1,0:T(8,128)(2,1)}, u32[]{:S(2)}, u32[]{:S(2)}) collective-permute-start(bf16[16,128,128]{2,1,0:T(8,128)(2,1)} %get-tuple-element.23), channel_id=1, source_target_pairs={{0,1},{1,2},{2,3},{3,0},{4,5},{5,6},{6,7},{7,4},{8,9},{9,10},{10,1... | collective-permute-start | bytes 1572872 | tf_op jit(solution)/shard_map/ppermute | solution.py:248
  30.6 12.5 %collective-permute-start.6 = (bf16[16,128,128]{2,1,0:T(8,128)(2,1)}, bf16[16,128,128]{2,1,0:T(8,128)(2,1)}, u32[]{:S(2)}, u32[]{:S(2)}) collective-permute-start(bf16[16,128,128]{2,1,0:T(8,128)(2,1)} %get-tuple-element.24), channel_id=1, source_target_pairs={{0,3},{1,0},{2,1},{3,2},{4,7},{5,4},{6,5},{7,6},{8,11},{9,8},{10,9... | collective-permute-start | bytes 1572872 | tf_op jit(solution)/shard_map/ppermute | solution.py:248
  40.9 2.8 %copy-start.2 = (bf16[32,128,128]{2,1,0:T(8,128)(2,1)S(1)}, bf16[32,128,128]{2,1,0:T(8,128)(2,1)}, u32[]{:S(2)}) copy-start(bf16[32,128,128]{2,1,0:T(8,128)(2,1)} %copy-done.1) | copy-start | bytes 3145732
  41.0 2.1 %collective-permute-start.7 = (bf16[64,32,128]{2,1,0:T(8,128)(2,1)S(1)}, bf16[64,32,128]{2,1,0:T(8,128)(2,1)S(1)}, u32[]{:S(2)}, u32[]{:S(2)}) collective-permute-start(bf16[64,32,128]{2,1,0:T(8,128)(2,1)S(1)} %bitcast.50), channel_id=1, source_target_pairs={{0,8},{8,0},{1,9},{9,1},{2,10},{10,2},{3,11},{11,3},{4,12},{12,4},... | collective-permute-start | bytes 1572872 | tf_op jit(solution)/shard_map/ppermute | solution.py:260
  41.1 2.6 %collective-permute-start.8 = (bf16[64,32,128]{2,1,0:T(8,128)(2,1)S(1)}, bf16[64,32,128]{2,1,0:T(8,128)(2,1)S(1)}, u32[]{:S(2)}, u32[]{:S(2)}) collective-permute-start(bf16[64,32,128]{2,1,0:T(8,128)(2,1)S(1)} %bitcast.49), channel_id=1, source_target_pairs={{0,8},{8,0},{1,9},{9,1},{2,10},{10,2},{3,11},{11,3},{4,12},{12,4},... | collective-permute-start | bytes 1572872 | tf_op jit(solution)/shard_map/ppermute | solution.py:260
  43.8 18.5 %copy-start.5 = (bf16[1024,128]{1,0:T(8,128)(2,1)S(1)}, bf16[1024,128]{1,0:T(8,128)(2,1)}, u32[]{:S(2)}) copy-start(bf16[1024,128]{1,0:T(8,128)(2,1)} %cot.1) | copy-start | bytes 786436
  43.8 18.5 %copy-start.6 = (bf16[128,128]{1,0:T(8,128)(2,1)S(1)}, bf16[128,128]{1,0:T(8,128)(2,1)}, u32[]{:S(2)}) copy-start(bf16[128,128]{1,0:T(8,128)(2,1)} %weight.1) | copy-start | bytes 98308
  43.8 18.5 %copy-start.7 = (f32[128]{0:T(128)S(1)}, f32[128]{0:T(128)}, u32[]{:S(2)}) copy-start(f32[128]{0:T(128)} %param.14) | copy-start | bytes 1540
  47.2 7.1 %collective-permute-start.9 = (f32[8,32,128]{2,1,0:T(8,128)S(1)}, f32[8,32,128]{2,1,0:T(8,128)S(1)}, u32[]{:S(2)}, u32[]{:S(2)}) collective-permute-start(f32[8,32,128]{2,1,0:T(8,128)S(1)} %forward.1), channel_id=1, source_target_pairs={{0,4},{4,0},{1,5},{5,1},{2,6},{6,2},{3,7},{7,3},{8,12},{12,8},{9,1... | collective-permute-start | bytes 393224 | tf_op jit(solution)/shard_map/ppermute | solution.py:260
  54.3 5.9 %collective-permute-start.12 = (bf16[8,32,128]{2,1,0:T(8,128)(2,1)S(1)}, bf16[8,32,128]{2,1,0:T(8,128)(2,1)S(1)}, u32[]{:S(2)}, u32[]{:S(2)}) collective-permute-start(bf16[8,32,128]{2,1,0:T(8,128)(2,1)S(1)} %add_convert_fusion.agg), channel_id=1, source_target_pairs={{0,2},{1,3},{2,0},{3,1},{4,6},{5,7},{6,4},{7,5},{8,10},{9,11},{10,... | collective-permute-start | bytes 196616 | tf_op jit(solution)/shard_map/ppermute | solution.py:248
  58.0 4.3 %collective-permute-start.11 = (bf16[8,32,128]{2,1,0:T(8,128)(2,1)S(1)}, bf16[8,32,128]{2,1,0:T(8,128)(2,1)S(1)}, u32[]{:S(2)}, u32[]{:S(2)}) collective-permute-start(bf16[8,32,128]{2,1,0:T(8,128)(2,1)S(1)} %add_convert_fusion.agg), channel_id=1, source_target_pairs={{0,3},{1,0},{2,1},{3,2},{4,7},{5,4},{6,5},{7,6},{8,11},{9,8},{10,9... | collective-permute-start | bytes 196616 | tf_op jit(solution)/shard_map/ppermute | solution.py:248
  58.0 4.3 %collective-permute-start.10 = (bf16[8,32,128]{2,1,0:T(8,128)(2,1)S(1)}, bf16[8,32,128]{2,1,0:T(8,128)(2,1)S(1)}, u32[]{:S(2)}, u32[]{:S(2)}) collective-permute-start(bf16[8,32,128]{2,1,0:T(8,128)(2,1)S(1)} %add_convert_fusion.agg), channel_id=1, source_target_pairs={{0,1},{1,2},{2,3},{3,0},{4,5},{5,6},{6,7},{7,4},{8,9},{9,10},{10,1... | collective-permute-start | bytes 196616 | tf_op jit(solution)/shard_map/ppermute | solution.py:248
  67.0 2.0 %collective-permute-start.13 = (bf16[2,1056,128]{2,1,0:T(8,128)(2,1)S(1)}, bf16[2,1056,128]{2,1,0:T(8,128)(2,1)S(1)}, u32[]{:S(2)}, u32[]{:S(2)}) collective-permute-start(bf16[2,1056,128]{2,1,0:T(8,128)(2,1)S(1)} %get-tuple-element.27), channel_id=1, source_target_pairs={{0,8},{8,0},{1,9},{9,1},{2,10},{10,2},{3,11},{11,3},{4,12},{12,4},... | collective-permute-start | bytes 1622024 | tf_op jit(solution)/shard_map/ppermute | solution.py:260
  67.1 5.2 %collective-permute-start.14 = (bf16[2,1056,128]{2,1,0:T(8,128)(2,1)S(1)}, bf16[2,1056,128]{2,1,0:T(8,128)(2,1)S(1)}, u32[]{:S(2)}, u32[]{:S(2)}) collective-permute-start(bf16[2,1056,128]{2,1,0:T(8,128)(2,1)S(1)} %get-tuple-element.29), channel_id=1, source_target_pairs={{0,8},{8,0},{1,9},{9,1},{2,10},{10,2},{3,11},{11,3},{4,12},{12,4},... | collective-permute-start | bytes 1622024 | tf_op jit(solution)/shard_map/ppermute | solution.py:260
  69.2 14.9 %collective-permute-start.17 = (bf16[1056,128]{1,0:T(8,128)(2,1)S(1)}, bf16[1056,128]{1,0:T(8,128)(2,1)S(1)}, u32[]{:S(2)}, u32[]{:S(2)}) collective-permute-start(bf16[1056,128]{1,0:T(8,128)(2,1)S(1)} %get-tuple-element.32), channel_id=1, source_target_pairs={{0,132},{128,0},{4,128},{132,4},{1,133},{129,1},{5,129},{133,5},{2... | collective-permute-start | bytes 811016 | tf_op jit(solution)/shard_map/ppermute | solution.py:256
  72.4 15.3 %collective-permute-start.15 = (bf16[1056,128]{1,0:T(8,128)(2,1)S(1)}, bf16[1056,128]{1,0:T(8,128)(2,1)S(1)}, u32[]{:S(2)}, u32[]{:S(2)}) collective-permute-start(bf16[1056,128]{1,0:T(8,128)(2,1)S(1)} %get-tuple-element.30), channel_id=1, source_target_pairs={{0,128},{128,4},{4,132},{132,0},{1,129},{129,5},{5,133},{133,1},{2... | collective-permute-start | bytes 811016 | tf_op jit(solution)/shard_map/ppermute | solution.py:256
  72.5 15.2 %collective-permute-start.16 = (bf16[1056,128]{1,0:T(8,128)(2,1)S(1)}, bf16[1056,128]{1,0:T(8,128)(2,1)S(1)}, u32[]{:S(2)}, u32[]{:S(2)}) collective-permute-start(bf16[1056,128]{1,0:T(8,128)(2,1)S(1)} %get-tuple-element.31), channel_id=1, source_target_pairs={{0,4},{128,132},{4,0},{132,128},{1,5},{129,133},{5,1},{133,129},{2... | collective-permute-start | bytes 811016 | tf_op jit(solution)/shard_map/ppermute | solution.py:256

commit v6 on v4

--- a/solution.py
+++ b/solution.py
@@ -107,8 +107,8 @@
     ids, meta, meta_l, meta_r, meta_f, own, left, right, far_a, far_b, agg, agg_l, agg_r, agg_f, weight, bias, cot,
     act, keep, *rest,
 ):
-    send_a, send_b, acc, back, full, slopes, wsum, far, act_in, far_sem, act_sem = rest
-    sends = {1: send_a.at[0], 2: send_a.at[1], 3: send_b.at[0], 0: send_b.at[1]}
+    send_a, send_b, send_c, acc, back, full, slopes, wsum, far, act_in, far_sem, act_sem = rest
+    sends = {1: send_a.at[0], 2: send_a.at[1], 3: send_b.at[0], 0: send_c.at[0]}
     fetch = fetch_far(far_a, far_b, far, far_sem)
     x, yl, yh = ids[0], ids[2], ids[3]
     acc[...] = jnp.zeros_like(acc)
@@ -173,9 +173,10 @@
         out[...] = (keep[k].astype(F32) + got[at].astype(F32)).astype(BF16)
 
 
-def y_sum_kernel(own, before, across, after, out):
+def y_sum_kernel(keep, got, before, across, after, out):
     def total(rows):
-        near = own[rows, :].astype(F32) + across[rows, :].astype(F32)
+        own = (keep[0, rows, :].astype(F32) + got[0, rows, :].astype(F32)).astype(BF16)
+        near = own.astype(F32) + across[rows, :].astype(F32)
         return (near + (before[rows, :].astype(F32) + after[rows, :].astype(F32))).astype(BF16)
 
     extra = total(slice(PIECE, PIECE + EXTRA))
@@ -272,7 +273,7 @@
 
 
 def pair(which, keep, got):
-    outs = [(got.shape[1:], BF16)] * 2
+    outs = [(got.shape[1:], BF16)] * len(which)
     return kernel_call(functools.partial(pair_kernel, which), "pair", outs, 0, [], 12, keep, got)
 
 
@@ -324,10 +325,11 @@
 
     piece = PIECE + EXTRA
     square = (ROW_TILES, TILE, WIDE)
-    activations, keep, send_a, send_b = kernel_call(
+    activations, keep, send_a, send_b, send_c = kernel_call(
         backward_kernel,
         "backward",
-        [((ROW_TILES * TILE, WIDE), BF16), ((NY, piece, TILE), BF16)] + [((2, piece, TILE), BF16)] * 2,
+        [((ROW_TILES * TILE, WIDE), BF16), ((NY, piece, TILE), BF16)]
+        + [((n, piece, TILE), BF16) for n in (2, 1, 1)],
         5,
         [
             pltpu.VMEM((2 * NY * NZ * BLOCK_HALF, THIN, TILE), F32),
@@ -355,11 +357,12 @@
         loose_out=(0,),
     )
     one, two = pair((1, 2), keep, swap(send_a, "c"))
-    three, stay = pair((3, 0), keep, swap(send_b, "c"))
+    (three,) = pair((3,), keep, swap(send_b, "c"))
+    stay = swap(send_c, "c")
     before, across, after = along_y(one, 1), along_y(two, 2), along_y(three, 3)
     last = LAST + EXTRA
     summed = kernel_call(
-        y_sum_kernel, "y_sum", ((NZ, last, TILE), BF16), 0, [], 12, stay, before, across, after
+        y_sum_kernel, "y_sum", ((NZ, last, TILE), BF16), 0, [], 12, keep, stay, before, across, after
     )
     got = exchange(summed, "z")
     shared = kernel_call(z_sum_kernel, "z_sum", ((NR, last, TILE), BF16), 0, [], 16, got)

time: 123 us -> 124 us (level)
    ppermute x5 -> x6, waiting for transfers between devices: 6.16 us -> 6.44 us  [swap(): return lax.ppermute(value, axis, [(0, 1), (1, 0)])]
    ppermute x5 -> x6, starting transfers between devices: 4.18 us -> 4.29 us  [swap(): return lax.ppermute(value, axis, [(0, 1), (1, 0)])]
  transfers between devices with their start and end apart: 19 -> 20, of which waited for: 11 -> 11; matrix products, arithmetic and copies ran while one was open for 0% -> 0% of each run, Pallas kernels for 2% -> 2%
where the time goes in v6:
time: 124 us; the launch traced here: 123 us
  waiting for transfers between devices  37.7 us (30%)
  starting transfers between devices  35.5 us (29%)
  blocking collectives  34.2 us (28%)
  Pallas kernels  11.3 us (9%)
  local copies, waits for them, and re-layouts  2.98 us (2%)
  between operations  1.44 us (1%)
    all_to_all x2, blocking collectives, exchange(): return lax.all_to_all(value, axes, 0, 0, tiled=True)  34.2 us
    ppermute x10, starting transfers between devices, rotate(): return lax.ppermute(value, 'x', [(k, (k + step) % NX) for k in range(NX)])  16.4 us
    ppermute x3, waiting for transfers between devices, along_y(): return lax.ppermute(value, ('yl', 'yh'), pairs)  13 us
    pallas_call x9, Pallas kernels, kernel_call(): pl.pallas_call(body, out_shape=[jax.ShapeDtypeStruct(s, d) for s, d in sh...  11.3 us
    ppermute x10, waiting for transfers between devices, rotate(): return lax.ppermute(value, 'x', [(k, (k + step) % NX) for k in range(NX)])  9.51 us
    all_to_all x1, starting transfers between devices, exchange(): return lax.all_to_all(value, axes, 0, 0, tiled=True)  9.47 us
    all_to_all x1, waiting for transfers between devices, exchange(): return lax.all_to_all(value, axes, 0, 0, tiled=True)  8.75 us
    ppermute x6, waiting for transfers between devices, swap(): return lax.ppermute(value, axis, [(0, 1), (1, 0)])  6.44 us
  transfers between devices with their start and end apart: 20, of which 11 were waited for; matrix products, arithmetic and copies ran while one was open for 0% of the time, Pallas kernels for 2%

profile of v6, /device:TPU:2, one launch (start us, length us, event | category | flops | bytes accessed | tf_op | source)
XLA Modules:
  0.0 123.4 jit_solution(1134160497903971978)
XLA Ops:
  0.6 2.3 %collective-permute-start.1 = (bf16[32,128,128]{2,1,0:T(8,128)(2,1)}, bf16[32,128,128]{2,1,0:T(8,128)(2,1)S(1)}, u32[]{:S(2)}, u32[]{:S(2)}) collective-permute-start(bf16[32,128,128]{2,1,0:T(8,128)(2,1)} %bitcast.36), channel_id=1, source_target_pairs={{0,3},{1,0},{2,1},{3,2},{4,7},{5,4},{6,5},{7,6},{8,11},{9,8},{10,9... | collective-permute-start | bytes 3145736 | tf_op jit(solution)/shard_map/ppermute | solution.py:232
  3.0 0.1 pad_add_fusion.ids
  3.1 0.9 copy-done.4
  4.0 0.8 prep.1
  4.8 0.9 copy-done.3
  5.8 9.5 %all-to-all-start = ((bf16[16,256,128]{2,1,0:T(8,128)(2,1)}), bf16[16,256,128]{2,1,0:T(8,128)(2,1)S(1)}, u32[]{:S(2)}, u32[]{:S(2)}) async-start(bf16[16,256,128]{2,1,0:T(8,128)(2,1)} %copy-done.3), calls=%async_computation | async-start | bytes 2097152 | tf_op jit(solution)/shard_map/all_to_all | solution.py:248
  16.0 0.1 pad_add_fusion.1
  16.1 3.4 %collective-permute-start.4 = (s32[1,128]{1,0:T(1,128)S(1)}, s32[1,128]{1,0:T(1,128)S(1)}, u32[]{:S(2)}, u32[]{:S(2)}) collective-permute-start(s32[1,128]{1,0:T(1,128)S(1)} %pad_add_fusion.1), channel_id=1, source_target_pairs={{0,2},{1,3},{2,0},{3,1},{4,6},{5,7},{6,4},{7,5},{8,10},{9,11},{10,... | collective-permute-start | bytes 1544 | tf_op jit(solution)/shard_map/ppermute | solution.py:232
  19.4 0.2 collective-permute-start.3
  19.7 1.8 %collective-permute-start.2 = (s32[1,128]{1,0:T(1,128)S(1)}, s32[1,128]{1,0:T(1,128)S(1)}, u32[]{:S(2)}, u32[]{:S(2)}) collective-permute-start(s32[1,128]{1,0:T(1,128)S(1)} %pad_add_fusion.1), channel_id=1, source_target_pairs={{0,1},{1,2},{2,3},{3,0},{4,5},{5,6},{6,7},{7,4},{8,9},{9,10},{10,1... | collective-permute-start | bytes 1544 | tf_op jit(solution)/shard_map/ppermute | solution.py:232
  21.5 5.3 %collective-permute-done.4.meta_f = s32[1,128]{1,0:T(1,128)S(1)} collective-permute-done((s32[1,128]{1,0:T(1,128)S(1)}, s32[1,128]{1,0:T(1,128)S(1)}, u32[]{:S(2)}, u32[]{:S(2)}) %collective-permute-start.4) | collective-permute-done | bytes 544 | tf_op jit(solution)/shard_map/ppermute | solution.py:232
  26.7 0.0 collective-permute-done.3.meta_r
  26.7 0.5 collective-permute-done.2.meta_l
  27.2 1.1 relay.1
  28.3 1.0 copy-done.1
  29.2 1.4 %collective-permute-start.5 = (bf16[16,128,128]{2,1,0:T(8,128)(2,1)}, bf16[16,128,128]{2,1,0:T(8,128)(2,1)}, u32[]{:S(2)}, u32[]{:S(2)}) collective-permute-start(bf16[16,128,128]{2,1,0:T(8,128)(2,1)} %get-tuple-element.22), channel_id=1, source_target_pairs={{0,1},{1,2},{2,3},{3,0},{4,5},{5,6},{6,7},{7,4},{8,9},{9,10},{10,1... | collective-permute-start | bytes 1572872 | tf_op jit(solution)/shard_map/ppermute | solution.py:232
  30.6 1.5 %collective-permute-start.6 = (bf16[16,128,128]{2,1,0:T(8,128)(2,1)}, bf16[16,128,128]{2,1,0:T(8,128)(2,1)}, u32[]{:S(2)}, u32[]{:S(2)}) collective-permute-start(bf16[16,128,128]{2,1,0:T(8,128)(2,1)} %get-tuple-element.23), channel_id=1, source_target_pairs={{0,3},{1,0},{2,1},{3,2},{4,7},{5,4},{6,5},{7,6},{8,11},{9,8},{10,9... | collective-permute-start | bytes 1572872 | tf_op jit(solution)/shard_map/ppermute | solution.py:232
  32.2 8.8 %all-to-all-done = bf16[16,256,128]{2,1,0:T(8,128)(2,1)S(1)} async-done(((bf16[16,256,128]{2,1,0:T(8,128)(2,1)}), bf16[16,256,128]{2,1,0:T(8,128)(2,1)S(1)}, u32[]{:S(2)}, u32[]{:S(2)}) %all-to-all-start) | async-done | bytes 1048608 | tf_op jit(solution)/shard_map/all_to_all | solution.py:248
  40.9 0.1 fusion.4
  41.0 0.1 collective-permute-start.7
  41.1 0.5 collective-permute-start.8
  41.6 1.5 %collective-permute-done.5.far_a = bf16[16,128,128]{2,1,0:T(8,128)(2,1)} collective-permute-done((bf16[16,128,128]{2,1,0:T(8,128)(2,1)}, bf16[16,128,128]{2,1,0:T(8,128)(2,1)}, u32[]{:S(2)}, u32[]{:S(2)}) %collective-permute-start.5) | collective-permute-done | bytes 524320 | tf_op jit(solution)/shard_map/ppermute | solution.py:232
  43.1 0.6 collective-permute-done.8.rest_1_
  43.8 0.0 copy-start.7
  43.8 3.4 %forward.1 = f32[8,32,128]{2,1,0:T(8,128)S(1)} custom-call(s32[128]{0:T(128)S(1)} %bitcast.40, s32[128]{0:T(128)S(1)} %bitcast.42, s32[128]{0:T(128)S(1)} %bitcast.44, s32[128]{0:T(128)S(1)} %bitcast.46, bf16[32,128,128]{2,1,0:T(8,128)(2,1)S(1)} %bitcast.38, bf16[32,128,128]{2,1,0:T(8,128)(2,1)S(1)} %copy-done.2, ...), custom_call_target="tpu_custom_call" | custom-call | tf_op jit(solution)/shard_map/forward/pallas_call | solution.py:258
  47.2 3.0 %collective-permute-start.9 = (f32[8,32,128]{2,1,0:T(8,128)S(1)}, f32[8,32,128]{2,1,0:T(8,128)S(1)}, u32[]{:S(2)}, u32[]{:S(2)}) collective-permute-start(f32[8,32,128]{2,1,0:T(8,128)S(1)} %forward.1), channel_id=1, source_target_pairs={{0,4},{4,0},{1,5},{5,1},{2,6},{6,2},{3,7},{7,3},{8,12},{12,8},{9,1... | collective-permute-start | bytes 393224 | tf_op jit(solution)/shard_map/ppermute | solution.py:244
  50.2 4.1 %collective-permute-done.9 = f32[8,32,128]{2,1,0:T(8,128)S(1)} collective-permute-done((f32[8,32,128]{2,1,0:T(8,128)S(1)}, f32[8,32,128]{2,1,0:T(8,128)S(1)}, u32[]{:S(2)}, u32[]{:S(2)}) %collective-permute-start.9) | collective-permute-done | bytes 131104 | tf_op jit(solution)/shard_map/ppermute | solution.py:244
  54.3 3.7 %collective-permute-start.12 = (bf16[8,32,128]{2,1,0:T(8,128)(2,1)S(1)}, bf16[8,32,128]{2,1,0:T(8,128)(2,1)S(1)}, u32[]{:S(2)}, u32[]{:S(2)}) collective-permute-start(bf16[8,32,128]{2,1,0:T(8,128)(2,1)S(1)} %add_convert_fusion.agg), channel_id=1, source_target_pairs={{0,2},{1,3},{2,0},{3,1},{4,6},{5,7},{6,4},{7,5},{8,10},{9,11},{10,... | collective-permute-start | bytes 196616 | tf_op jit(solution)/shard_map/ppermute | solution.py:232
  58.0 2.0 %collective-permute-start.10 = (bf16[8,32,128]{2,1,0:T(8,128)(2,1)S(1)}, bf16[8,32,128]{2,1,0:T(8,128)(2,1)S(1)}, u32[]{:S(2)}, u32[]{:S(2)}) collective-permute-start(bf16[8,32,128]{2,1,0:T(8,128)(2,1)S(1)} %add_convert_fusion.agg), channel_id=1, source_target_pairs={{0,1},{1,2},{2,3},{3,0},{4,5},{5,6},{6,7},{7,4},{8,9},{9,10},{10,1... | collective-permute-start | bytes 196616 | tf_op jit(solution)/shard_map/ppermute | solution.py:232
  60.0 0.2 collective-permute-done.12.agg_f
  60.3 2.0 %collective-permute-done.11.agg_r = bf16[8,32,128]{2,1,0:T(8,128)(2,1)S(1)} collective-permute-done((bf16[8,32,128]{2,1,0:T(8,128)(2,1)S(1)}, bf16[8,32,128]{2,1,0:T(8,128)(2,1)S(1)}, u32[]{:S(2)}, u32[]{:S(2)}) %collective-permute-start.11) | collective-permute-done | bytes 65568 | tf_op jit(solution)/shard_map/ppermute | solution.py:232
  62.3 0.0 collective-permute-done.10.agg_l
  62.3 4.7 %backward.1 = (bf16[1024,128]{1,0:T(8,128)(2,1)}, bf16[4,1056,128]{2,1,0:T(8,128)(2,1)S(1)}, bf16[2,1056,128]{2,1,0:T(8,128)(2,1)S(1)}, bf16[1,1056,128]{2,1,0:T(8,128)(2,1)S(1)}, bf16[1,1056,128]{2,1,0:T(8,128)(2,1)S(1)}) custom-call(s32[4]{0:T(128)S(1)} %pad_add_fusion.ids, s32[128]{0:T(128)S(1)} %bitcast.41, s32[128]{0:T(128)S(1)} %bitcast.43, ...), custom_call_target="tpu_custom_call" | custom-call | tf_op jit(solution)/shard_map/backward/pallas_call | solution.py:258
  67.0 0.1 collective-permute-start.14
  67.1 0.5 collective-permute-start.17
  67.6 0.1 collective-permute-start.13
  67.7 1.7 %collective-permute-done.17.got = bf16[1,1056,128]{2,1,0:T(8,128)(2,1)S(1)} collective-permute-done((bf16[1,1056,128]{2,1,0:T(8,128)(2,1)S(1)}, bf16[1,1056,128]{2,1,0:T(8,128)(2,1)S(1)}, u32[]{:S(2)}, u32[]{:S(2)}) %collective-permute-start.17) | collective-permute-done | bytes 270368 | tf_op jit(solution)/shard_map/ppermute | solution.py:244
  69.4 0.1 pair.3
  69.5 3.1 %collective-permute-start.18 = (bf16[1056,128]{1,0:T(8,128)(2,1)S(1)}, bf16[1056,128]{1,0:T(8,128)(2,1)S(1)}, u32[]{:S(2)}, u32[]{:S(2)}) collective-permute-start(bf16[1056,128]{1,0:T(8,128)(2,1)S(1)} %pair.3), channel_id=1, source_target_pairs={{0,132},{128,0},{4,128},{132,4},{1,133},{129,1},{5,129},{133,5},{2... | collective-permute-start | bytes 811016 | tf_op jit(solution)/shard_map/ppermute | solution.py:240
  72.6 0.2 pair.2
  72.7 0.1 collective-permute-start.15
  72.8 2.2 %collective-permute-start.16 = (bf16[1056,128]{1,0:T(8,128)(2,1)S(1)}, bf16[1056,128]{1,0:T(8,128)(2,1)S(1)}, u32[]{:S(2)}, u32[]{:S(2)}) collective-permute-start(bf16[1056,128]{1,0:T(8,128)(2,1)S(1)} %get-tuple-element.29), channel_id=1, source_target_pairs={{0,4},{128,132},{4,0},{132,128},{1,5},{129,133},{5,1},{133,129},{2... | collective-permute-start | bytes 811016 | tf_op jit(solution)/shard_map/ppermute | solution.py:240
  75.0 9.4 %collective-permute-done.18.after = bf16[1056,128]{1,0:T(8,128)(2,1)S(1)} collective-permute-done((bf16[1056,128]{1,0:T(8,128)(2,1)S(1)}, bf16[1056,128]{1,0:T(8,128)(2,1)S(1)}, u32[]{:S(2)}, u32[]{:S(2)}) %collective-permute-start.18) | collective-permute-done | bytes 270368 | tf_op jit(solution)/shard_map/ppermute | solution.py:240
  84.4 3.7 %collective-permute-done.15.before = bf16[1056,128]{1,0:T(8,128)(2,1)S(1)} collective-permute-done((bf16[1056,128]{1,0:T(8,128)(2,1)S(1)}, bf16[1056,128]{1,0:T(8,128)(2,1)S(1)}, u32[]{:S(2)}, u32[]{:S(2)}) %collective-permute-start.15) | collective-permute-done | bytes 270368 | tf_op jit(solution)/shard_map/ppermute | solution.py:240
  88.1 0.2 y_sum.1
  88.3 19.7 %all_to_all.15.got = bf16[8,160,128]{2,1,0:T(8,128)(2,1)S(1)} all-to-all(bf16[8,160,128]{2,1,0:T(8,128)(2,1)S(1)} %y_sum.1), channel_id=1, replica_groups=mesh['yl'=2,'z'=8,'c'=2,'yh'=2,'x'=4] {'z'}, dimensions={0} | all-to-all | bytes 655360 | tf_op jit(solution)/shard_map/all_to_all | solution.py:248
  108.0 14.4 %all_to_all.16.got = bf16[8,160,128]{2,1,0:T(8,128)(2,1)S(1)} all-to-all(bf16[8,160,128]{2,1,0:T(8,128)(2,1)S(1)} %z_sum.1), channel_id=1, replica_groups=mesh['yl'=2,'z'=8,'c'=2,'yh'=2,'x'=4] {'yh','x'}, dimensions={0} | all-to-all | bytes 655360 | tf_op jit(solution)/shard_map/all_to_all | solution.py:248
  122.5 0.9 finish.1
  (29 shorter events, 0.2 us)
Async XLA Ops:
  0.6 26.6 %collective-permute-start.1 = (bf16[32,128,128]{2,1,0:T(8,128)(2,1)}, bf16[32,128,128]{2,1,0:T(8,128)(2,1)S(1)}, u32[]{:S(2)}, u32[]{:S(2)}) collective-permute-start(bf16[32,128,128]{2,1,0:T(8,128)(2,1)} %bitcast.36), channel_id=1, source_target_pairs={{0,3},{1,0},{2,1},{3,2},{4,7},{5,4},{6,5},{7,6},{8,11},{9,8},{10,9... | collective-permute-start | bytes 3145736 | tf_op jit(solution)/shard_map/ppermute | solution.py:232
  3.0 24.2 %collective-permute-start = (bf16[32,128,128]{2,1,0:T(8,128)(2,1)}, bf16[32,128,128]{2,1,0:T(8,128)(2,1)S(1)}, u32[]{:S(2)}, u32[]{:S(2)}) collective-permute-start(bf16[32,128,128]{2,1,0:T(8,128)(2,1)} %bitcast.37), channel_id=1, source_target_pairs={{0,1},{1,2},{2,3},{3,0},{4,5},{5,6},{6,7},{7,4},{8,9},{9,10},{10,1... | collective-permute-start | bytes 3145736 | tf_op jit(solution)/shard_map/ppermute | solution.py:232
  3.1 1.0 copy-start.4
  4.8 1.0 copy-start.3
  5.8 10.1 %copy-start.8 = (s32[1,1,32]{2,1,0:T(1,128)S(1)}, s32[1,1,32]{2,1,0:T(1,128)}, u32[]{:S(2)}) copy-start(s32[1,1,32]{2,1,0:T(1,128)} %param.11) | copy-start | bytes 388
  5.8 10.1 %copy-start.9 = (s32[1,1,32]{2,1,0:T(1,128)S(1)}, s32[1,1,32]{2,1,0:T(1,128)}, u32[]{:S(2)}) copy-start(s32[1,1,32]{2,1,0:T(1,128)} %param.10) | copy-start | bytes 388
  5.8 35.1 %all-to-all-start = ((bf16[16,256,128]{2,1,0:T(8,128)(2,1)}), bf16[16,256,128]{2,1,0:T(8,128)(2,1)S(1)}, u32[]{:S(2)}, u32[]{:S(2)}) async-start(bf16[16,256,128]{2,1,0:T(8,128)(2,1)} %copy-done.3), calls=%async_computation | async-start | bytes 2097152 | tf_op jit(solution)/shard_map/all_to_all | solution.py:248
  16.1 10.7 %collective-permute-start.4 = (s32[1,128]{1,0:T(1,128)S(1)}, s32[1,128]{1,0:T(1,128)S(1)}, u32[]{:S(2)}, u32[]{:S(2)}) collective-permute-start(s32[1,128]{1,0:T(1,128)S(1)} %pad_add_fusion.1), channel_id=1, source_target_pairs={{0,2},{1,3},{2,0},{3,1},{4,6},{5,7},{6,4},{7,5},{8,10},{9,11},{10,... | collective-permute-start | bytes 1544 | tf_op jit(solution)/shard_map/ppermute | solution.py:232
  19.4 7.3 %collective-permute-start.3 = (s32[1,128]{1,0:T(1,128)S(1)}, s32[1,128]{1,0:T(1,128)S(1)}, u32[]{:S(2)}, u32[]{:S(2)}) collective-permute-start(s32[1,128]{1,0:T(1,128)S(1)} %pad_add_fusion.1), channel_id=1, source_target_pairs={{0,3},{1,0},{2,1},{3,2},{4,7},{5,4},{6,5},{7,6},{8,11},{9,8},{10,9... | collective-permute-start | bytes 1544 | tf_op jit(solution)/shard_map/ppermute | solution.py:232
  19.7 7.5 %collective-permute-start.2 = (s32[1,128]{1,0:T(1,128)S(1)}, s32[1,128]{1,0:T(1,128)S(1)}, u32[]{:S(2)}, u32[]{:S(2)}) collective-permute-start(s32[1,128]{1,0:T(1,128)S(1)} %pad_add_fusion.1), channel_id=1, source_target_pairs={{0,1},{1,2},{2,3},{3,0},{4,5},{5,6},{6,7},{7,4},{8,9},{9,10},{10,1... | collective-permute-start | bytes 1544 | tf_op jit(solution)/shard_map/ppermute | solution.py:232
  28.3 1.0 copy-start.1
  29.2 14.5 %copy-start = (bf16[1,1,32,128,128]{4,3,2,1,0:T(8,128)(2,1)S(1)}, bf16[1,1,32,128,128]{4,3,2,1,0:T(8,128)(2,1)}, u32[]{:S(2)}) copy-start(bf16[1,1,32,128,128]{4,3,2,1,0:T(8,128)(2,1)} %param.9) | copy-start | bytes 3145732
  29.2 13.9 %collective-permute-start.5 = (bf16[16,128,128]{2,1,0:T(8,128)(2,1)}, bf16[16,128,128]{2,1,0:T(8,128)(2,1)}, u32[]{:S(2)}, u32[]{:S(2)}) collective-permute-start(bf16[16,128,128]{2,1,0:T(8,128)(2,1)} %get-tuple-element.22), channel_id=1, source_target_pairs={{0,1},{1,2},{2,3},{3,0},{4,5},{5,6},{6,7},{7,4},{8,9},{9,10},{10,1... | collective-permute-start | bytes 1572872 | tf_op jit(solution)/shard_map/ppermute | solution.py:232
  30.6 12.5 %collective-permute-start.6 = (bf16[16,128,128]{2,1,0:T(8,128)(2,1)}, bf16[16,128,128]{2,1,0:T(8,128)(2,1)}, u32[]{:S(2)}, u32[]{:S(2)}) collective-permute-start(bf16[16,128,128]{2,1,0:T(8,128)(2,1)} %get-tuple-element.23), channel_id=1, source_target_pairs={{0,3},{1,0},{2,1},{3,2},{4,7},{5,4},{6,5},{7,6},{8,11},{9,8},{10,9... | collective-permute-start | bytes 1572872 | tf_op jit(solution)/shard_map/ppermute | solution.py:232
  40.9 2.8 %copy-start.2 = (bf16[32,128,128]{2,1,0:T(8,128)(2,1)S(1)}, bf16[32,128,128]{2,1,0:T(8,128)(2,1)}, u32[]{:S(2)}) copy-start(bf16[32,128,128]{2,1,0:T(8,128)(2,1)} %copy-done.1) | copy-start | bytes 3145732
  41.0 2.1 %collective-permute-start.7 = (bf16[64,32,128]{2,1,0:T(8,128)(2,1)S(1)}, bf16[64,32,128]{2,1,0:T(8,128)(2,1)S(1)}, u32[]{:S(2)}, u32[]{:S(2)}) collective-permute-start(bf16[64,32,128]{2,1,0:T(8,128)(2,1)S(1)} %bitcast.50), channel_id=1, source_target_pairs={{0,8},{8,0},{1,9},{9,1},{2,10},{10,2},{3,11},{11,3},{4,12},{12,4},... | collective-permute-start | bytes 1572872 | tf_op jit(solution)/shard_map/ppermute | solution.py:244
  41.1 2.6 %collective-permute-start.8 = (bf16[64,32,128]{2,1,0:T(8,128)(2,1)S(1)}, bf16[64,32,128]{2,1,0:T(8,128)(2,1)S(1)}, u32[]{:S(2)}, u32[]{:S(2)}) collective-permute-start(bf16[64,32,128]{2,1,0:T(8,128)(2,1)S(1)} %bitcast.49), channel_id=1, source_target_pairs={{0,8},{8,0},{1,9},{9,1},{2,10},{10,2},{3,11},{11,3},{4,12},{12,4},... | collective-permute-start | bytes 1572872 | tf_op jit(solution)/shard_map/ppermute | solution.py:244
  43.8 18.5 %copy-start.5 = (bf16[1024,128]{1,0:T(8,128)(2,1)S(1)}, bf16[1024,128]{1,0:T(8,128)(2,1)}, u32[]{:S(2)}) copy-start(bf16[1024,128]{1,0:T(8,128)(2,1)} %cot.1) | copy-start | bytes 786436
  43.8 18.5 %copy-start.6 = (bf16[128,128]{1,0:T(8,128)(2,1)S(1)}, bf16[128,128]{1,0:T(8,128)(2,1)}, u32[]{:S(2)}) copy-start(bf16[128,128]{1,0:T(8,128)(2,1)} %weight.1) | copy-start | bytes 98308
  43.8 18.5 %copy-start.7 = (f32[128]{0:T(128)S(1)}, f32[128]{0:T(128)}, u32[]{:S(2)}) copy-start(f32[128]{0:T(128)} %param.14) | copy-start | bytes 1540
  47.2 7.1 %collective-permute-start.9 = (f32[8,32,128]{2,1,0:T(8,128)S(1)}, f32[8,32,128]{2,1,0:T(8,128)S(1)}, u32[]{:S(2)}, u32[]{:S(2)}) collective-permute-start(f32[8,32,128]{2,1,0:T(8,128)S(1)} %forward.1), channel_id=1, source_target_pairs={{0,4},{4,0},{1,5},{5,1},{2,6},{6,2},{3,7},{7,3},{8,12},{12,8},{9,1... | collective-permute-start | bytes 393224 | tf_op jit(solution)/shard_map/ppermute | solution.py:244
  54.3 5.9 %collective-permute-start.12 = (bf16[8,32,128]{2,1,0:T(8,128)(2,1)S(1)}, bf16[8,32,128]{2,1,0:T(8,128)(2,1)S(1)}, u32[]{:S(2)}, u32[]{:S(2)}) collective-permute-start(bf16[8,32,128]{2,1,0:T(8,128)(2,1)S(1)} %add_convert_fusion.agg), channel_id=1, source_target_pairs={{0,2},{1,3},{2,0},{3,1},{4,6},{5,7},{6,4},{7,5},{8,10},{9,11},{10,... | collective-permute-start | bytes 196616 | tf_op jit(solution)/shard_map/ppermute | solution.py:232
  58.0 4.3 %collective-permute-start.11 = (bf16[8,32,128]{2,1,0:T(8,128)(2,1)S(1)}, bf16[8,32,128]{2,1,0:T(8,128)(2,1)S(1)}, u32[]{:S(2)}, u32[]{:S(2)}) collective-permute-start(bf16[8,32,128]{2,1,0:T(8,128)(2,1)S(1)} %add_convert_fusion.agg), channel_id=1, source_target_pairs={{0,3},{1,0},{2,1},{3,2},{4,7},{5,4},{6,5},{7,6},{8,11},{9,8},{10,9... | collective-permute-start | bytes 196616 | tf_op jit(solution)/shard_map/ppermute | solution.py:232
  58.0 4.3 %collective-permute-start.10 = (bf16[8,32,128]{2,1,0:T(8,128)(2,1)S(1)}, bf16[8,32,128]{2,1,0:T(8,128)(2,1)S(1)}, u32[]{:S(2)}, u32[]{:S(2)}) collective-permute-start(bf16[8,32,128]{2,1,0:T(8,128)(2,1)S(1)} %add_convert_fusion.agg), channel_id=1, source_target_pairs={{0,1},{1,2},{2,3},{3,0},{4,5},{5,6},{6,7},{7,4},{8,9},{9,10},{10,1... | collective-permute-start | bytes 196616 | tf_op jit(solution)/shard_map/ppermute | solution.py:232
  67.0 5.6 %collective-permute-start.14 = (bf16[2,1056,128]{2,1,0:T(8,128)(2,1)S(1)}, bf16[2,1056,128]{2,1,0:T(8,128)(2,1)S(1)}, u32[]{:S(2)}, u32[]{:S(2)}) collective-permute-start(bf16[2,1056,128]{2,1,0:T(8,128)(2,1)S(1)} %get-tuple-element.27), channel_id=1, source_target_pairs={{0,8},{8,0},{1,9},{9,1},{2,10},{10,2},{3,11},{11,3},{4,12},{12,4},... | collective-permute-start | bytes 1622024 | tf_op jit(solution)/shard_map/ppermute | solution.py:244
  67.1 2.3 %collective-permute-start.17 = (bf16[1,1056,128]{2,1,0:T(8,128)(2,1)S(1)}, bf16[1,1056,128]{2,1,0:T(8,128)(2,1)S(1)}, u32[]{:S(2)}, u32[]{:S(2)}) collective-permute-start(bf16[1,1056,128]{2,1,0:T(8,128)(2,1)S(1)} %get-tuple-element.30), channel_id=1, source_target_pairs={{0,8},{8,0},{1,9},{9,1},{2,10},{10,2},{3,11},{11,3},{4,12},{12,4},... | collective-permute-start | bytes 811016 | tf_op jit(solution)/shard_map/ppermute | solution.py:244
  67.6 7.4 %collective-permute-start.13 = (bf16[1,1056,128]{2,1,0:T(8,128)(2,1)S(1)}, bf16[1,1056,128]{2,1,0:T(8,128)(2,1)S(1)}, u32[]{:S(2)}, u32[]{:S(2)}) collective-permute-start(bf16[1,1056,128]{2,1,0:T(8,128)(2,1)S(1)} %get-tuple-element.26), channel_id=1, source_target_pairs={{0,8},{8,0},{1,9},{9,1},{2,10},{10,2},{3,11},{11,3},{4,12},{12,4},... | collective-permute-start | bytes 811016 | tf_op jit(solution)/shard_map/ppermute | solution.py:244
  69.5 14.9 %collective-permute-start.18 = (bf16[1056,128]{1,0:T(8,128)(2,1)S(1)}, bf16[1056,128]{1,0:T(8,128)(2,1)S(1)}, u32[]{:S(2)}, u32[]{:S(2)}) collective-permute-start(bf16[1056,128]{1,0:T(8,128)(2,1)S(1)} %pair.3), channel_id=1, source_target_pairs={{0,132},{128,0},{4,128},{132,4},{1,133},{129,1},{5,129},{133,5},{2... | collective-permute-start | bytes 811016 | tf_op jit(solution)/shard_map/ppermute | solution.py:240
  72.7 15.3 %collective-permute-start.15 = (bf16[1056,128]{1,0:T(8,128)(2,1)S(1)}, bf16[1056,128]{1,0:T(8,128)(2,1)S(1)}, u32[]{:S(2)}, u32[]{:S(2)}) collective-permute-start(bf16[1056,128]{1,0:T(8,128)(2,1)S(1)} %get-tuple-element.28), channel_id=1, source_target_pairs={{0,128},{128,4},{4,132},{132,0},{1,129},{129,5},{5,133},{133,1},{2... | collective-permute-start | bytes 811016 | tf_op jit(solution)/shard_map/ppermute | solution.py:240
  72.8 15.2 %collective-permute-start.16 = (bf16[1056,128]{1,0:T(8,128)(2,1)S(1)}, bf16[1056,128]{1,0:T(8,128)(2,1)S(1)}, u32[]{:S(2)}, u32[]{:S(2)}) collective-permute-start(bf16[1056,128]{1,0:T(8,128)(2,1)S(1)} %get-tuple-element.29), channel_id=1, source_target_pairs={{0,4},{128,132},{4,0},{132,128},{1,5},{129,133},{5,1},{133,129},{2... | collective-permute-start | bytes 811016 | tf_op jit(solution)/shard_map/ppermute | solution.py:240
